TPU v7x, 256 devices: a whole 4x4x8 slice. The times are simulated.
256 devices in a mesh: grp: 16 (over z, core), ing: 16 (over y, x).
Axes of the slice: x: 4, y: 4, z: 8, core: 2. Of those that a mesh axis runs over, the one named last changes fastest.
Arguments:
- image_embed: bfloat16 [32768, 1152], P(('grp', 'ing')), may hold values from -20 to 20
- text_embed: bfloat16 [32768, 1152], P(('grp', 'ing')), may hold values from -20 to 20
- scale_logarithm: float32 [1], replicated, may hold values from 1.8 to 2.6
- logit_bias: float32 [1], replicated, may hold values from -4 to -1
- loss_grad: float32 [1], replicated, may hold values from 2048 to 8192
Outputs:
- image_gradient: float32 [32768, 1152], P(('grp', 'ing'))
- text_gradient: float32 [32768, 1152], P(('grp', 'ing'))
All inputs are finite; a program needn't handle non-finite values.
Results may differ from a plain program's by a relative error of at most 0.0042.
Values may be sent and summed in bfloat16 or wider, within the bound.
No kernel may reach another device: no remote copies, remote signals or barrier semaphores. Data moves between devices by JAX's collectives and lax.ppermute only.
A program may use at most 128 MiB of HBM per device.

v0:
```python
import jax
import jax.numpy as jnp
from jax import lax
from jax.sharding import PartitionSpec as P

epsilon = 1e-06


def swapped(value, axis, stride):
    mask = 2**stride
    pairs = [(source, source ^ mask) for source in range(lax.axis_size(axis))]
    return lax.ppermute(value, axis, pairs)


def unit_rows(matrix):
    values = matrix.astype(jnp.float32)
    length = jnp.sqrt(jnp.sum(values * values, axis=1, keepdims=True) + epsilon)
    return (values / length, length)


def remove_projection(gradient, unit, length):
    return (gradient - unit * jnp.sum(unit * gradient, axis=1, keepdims=True)) / length


def loss_factors(
    left_side, right_side, left_begin, right_begin, softness_scale, offset_bias, scale_factor
):
    cosine_scores = lax.dot_general(
        left_side, right_side, (((1,), (1,)), ((), ())), preferred_element_type=jnp.float32
    )
    logit_matrix = softness_scale * cosine_scores + offset_bias
    row_ids = left_begin + jnp.arange(left_side.shape[0], dtype=jnp.int32)[:, None]
    col_ids = right_begin + jnp.arange(right_side.shape[0], dtype=jnp.int32)[None, :]
    labels = jnp.where(row_ids == col_ids, jnp.float32(1.0), jnp.float32(-1.0))
    return (-scale_factor * labels * jax.nn.sigmoid(-labels * logit_matrix)).astype(jnp.bfloat16)


def with_partials(
    image_halfway,
    local_text,
    foreign_text,
    row_begin,
    local_shift,
    foreign_shift,
    softness_scale,
    offset_bias,
    scale_factor,
):
    own_w = loss_factors(
        image_halfway, local_text, row_begin, local_shift, softness_scale, offset_bias, scale_factor
    )
    other_w = loss_factors(
        image_halfway,
        foreign_text,
        row_begin,
        foreign_shift,
        softness_scale,
        offset_bias,
        scale_factor,
    )
    image_running = jnp.dot(own_w, local_text, preferred_element_type=jnp.float32)
    image_running = image_running + jnp.dot(
        other_w, foreign_text, preferred_element_type=jnp.float32
    )
    contract = (((0,), (0,)), ((), ()))
    own_part = lax.dot_general(own_w, image_halfway, contract, preferred_element_type=jnp.float32)
    other_part = lax.dot_general(
        other_w, image_halfway, contract, preferred_element_type=jnp.float32
    )
    arrived = swapped(other_part, "grp", 0)
    text_running = lax.psum_scatter(own_part + arrived, "ing", scatter_dimension=0, tiled=True)
    return (image_running, text_running)


def body(image_embed, text_embed, scale_logarithm, logit_bias, loss_grad):
    image_unit_vector, image_length_norm = unit_rows(image_embed)
    text_unit_vector, text_length_norm = unit_rows(text_embed)
    image_halfway = image_unit_vector.astype(jnp.bfloat16)
    text_half = text_unit_vector.astype(jnp.bfloat16)
    row_count = image_embed.shape[0]
    block_len = row_count * lax.axis_size("ing")
    set_size = 2 * block_len
    parity = lax.axis_index("grp") % 2
    local_shift = parity * block_len
    foreign_shift = (1 - parity) * block_len
    row_begin = local_shift + lax.axis_index("ing") * row_count
    softness_scale = jnp.exp(scale_logarithm[0])
    offset_bias = logit_bias[0]
    scale_factor = loss_grad[0] / set_size
    local_text = lax.all_gather(text_half, "ing", axis=0, tiled=True)
    foreign_text = swapped(local_text, "grp", 0)
    image_running, text_running = with_partials(
        image_halfway,
        local_text,
        foreign_text,
        row_begin,
        local_shift,
        foreign_shift,
        softness_scale,
        offset_bias,
        scale_factor,
    )
    image_gradient = remove_projection(
        softness_scale * image_running, image_unit_vector, image_length_norm
    )
    text_gradient = remove_projection(
        softness_scale * text_running, text_unit_vector, text_length_norm
    )
    return (image_gradient, text_gradient)


def solution(mesh):
    placed = (P(("grp", "ing"), None), P(("grp", "ing"), None), P(), P(), P())
    return jax.shard_map(
        body,
        mesh=mesh,
        in_specs=placed,
        out_specs=(P(("grp", "ing"), None), P(("grp", "ing"), None)),
        check_vma=False,
    )
```

profile of v0, /device:TPU:1, one launch (start us, length us, event | category | flops | bytes accessed | tf_op | source)
XLA Modules:
  0.0 209.3 jit_solution(1762759449097614017)
XLA Ops:
  7.2 0.0 all-gather.2.cloned.1.call-start
  7.2 1.1 fusion.18
  8.3 1.8 fusion.20
  10.1 0.0 all-gather.2.cloned.1.call-update
  10.2 0.0 reduce-scatter.2.cloned.1.call-start
  10.2 63.7 %all-gather.2.cloned.1.call-done = bf16[2048,1152]{1,0:T(8,128)(2,1)} async-done(((bf16[128,1152]{1,0:T(8,128)(2,1)}), bf16[2048,1152]{1,0:T(8,128)(2,1)}) %all-gather.2.cloned.1.call-update) | async-done | bytes 4718608 | tf_op jit(solution)/shard_map/all_gather | solution.py:90
  73.9 0.7 collective-permute-start
  76.6 1.1 fusion.17
  77.7 4.8 %collective-permute-done = bf16[2048,1152]{1,0:T(8,128)(2,1)} collective-permute-done((bf16[2048,1152]{1,0:T(8,128)(2,1)}, bf16[2048,1152]{1,0:T(8,128)(2,1)}, u32[]{:S(2)}, u32[]{:S(2)}) %collective-permute-start) | collective-permute-done | bytes 4718624 | tf_op jit(solution)/shard_map/ppermute | solution.py:12
  82.4 4.3 %fusion.15 = bf16[128,2048]{1,0:T(8,128)(2,1)S(1)} fusion(bf16[2048,1152]{1,0:T(8,128)(2,1)} %collective-permute-done, s32[2048]{0:T(1024)S(1)} %iota_add_fusion, f32[]{:T(128)} %bitcast.12, f32[]{:T(128)} %bitcast, f32[]{:T(128)} %bitcast.1, s32[128]{0:T(128)S(1)} %iota_add_fusion.2, f32[128]{0:T(128)S(1)} %add_sqrt_fusion.1, bf16[128,1152]{1,0:T(8,128)(2,1)} %param.5), kind=kOutput, calls=%fused_computation.19 | convolution fusion | flops 607567872 | bytes 5547020 | tf_op jit(solution)/shard_map/dot_general | solution.py:28
  86.8 0.0 slice-start.1
  86.8 1.5 fusion.21
  88.2 0.5 collective-permute-start.1
  88.7 1.7 fusion.16
  90.5 12.5 %collective-permute-done.1 = f32[2048,1152]{1,0:T(8,128)S(1)} collective-permute-done((f32[2048,1152]{1,0:T(8,128)S(1)}, f32[2048,1152]{1,0:T(8,128)S(1)}, u32[]{:S(2)}, u32[]{:S(2)}) %collective-permute-start.1) | collective-permute-done | bytes 9437216 | tf_op jit(solution)/shard_map/ppermute | solution.py:12
  103.0 5.1 %convolution_add_fusion = f32[2048,1152]{1,0:T(8,128)} fusion(f32[2048,1152]{1,0:T(8,128)S(1)} %collective-permute-done.1, bf16[128,2048]{1,0:T(8,128)(2,1)S(1)} %fusion.16, f32[128]{0:T(128)S(1)} %add_sqrt_fusion.1, bf16[128,1152]{1,0:T(8,128)(2,1)S(1)} %copy-done.1), kind=kOutput, calls=%fused_computation | convolution fusion | flops 606781440 | bytes 19694080 | tf_op jit(solution)/shard_map/dot_general | solution.py:66
  108.1 0.0 reduce-scatter.2.cloned.1.call-update
  108.1 3.2 %fusion.26 = f32[128,1152]{1,0:T(8,128)S(1)} fusion(bf16[128,2048]{1,0:T(8,128)(2,1)S(1)} %fusion.16, bf16[2048,1152]{1,0:T(8,128)(2,1)} %all-gather.2.cloned.1.call-done), kind=kOutput, calls=%fused_computation.43 | convolution fusion | flops 603979776 | bytes 5832704 | tf_op jit(solution)/shard_map/dot_general | solution.py:61
  111.3 0.0 copy-start
  111.3 3.4 %multiply_reduce_fusion.1 = (f32[128]{0:T(128)S(1)}, f32[128,1152]{1,0:T(8,128)S(1)}) fusion(f32[128]{0:T(128)S(1)} %add_sqrt_fusion.1, bf16[128,1152]{1,0:T(8,128)(2,1)S(1)} %copy-done.1, f32[128,1152]{1,0:T(8,128)S(1)} %fusion.26, bf16[128,2048]{1,0:T(8,128)(2,1)S(1)} %fusion.15, bf16[2048,1152]{1,0:T(8,128)(2,1)} %collective-permute-done, f32[]{:T(128)} %bitcast), kind=kOutput, calls=%fused_computation.34 | convolution fusion | flops 604864384 | bytes 6718468 | tf_op jit(solution)/shard_map/dot_general | solution.py:62
  114.7 1.0 subtract_divide_fusion.1
  115.7 83.4 %reduce-scatter.2.cloned.1.call-done = f32[128,1152]{1,0:T(8,128)} async-done(((f32[2048,1152]{1,0:T(8,128)}), f32[128,1152]{1,0:T(8,128)}) %reduce-scatter.2.cloned.1.call-update) | async-done | bytes 589840 | tf_op jit(solution)/shard_map/reduce_scatter | solution.py:71
  199.1 1.3 multiply_reduce_fusion
  200.4 2.1 subtract_divide_fusion
  (12 shorter events, 0.0 us)
Async XLA Ops:
  7.2 66.7 %all-gather.2.cloned.1.call-start = ((), (), s32[]{:S(2)}) async-start(), calls=%async_computation.1 | async-start | bytes 5013504 | tf_op jit(solution)/shard_map/all_gather | solution.py:90
  10.2 189.0 %reduce-scatter.2.cloned.1.call-start = ((), (), s32[]{:S(2)}) async-start(), calls=%async_computation.2 | async-start | bytes 10027008 | tf_op jit(solution)/shard_map/reduce_scatter | solution.py:71
  73.9 8.6 %collective-permute-start = (bf16[2048,1152]{1,0:T(8,128)(2,1)}, bf16[2048,1152]{1,0:T(8,128)(2,1)}, u32[]{:S(2)}, u32[]{:S(2)}) collective-permute-start(bf16[2048,1152]{1,0:T(8,128)(2,1)} %all-gather.2.cloned.1.call-done), channel_id=1, source_target_pairs={{0,16},{16,0},{32,48},{48,32},{64,80},{80,64},{96,112},{112,96},{1... | collective-permute-start | bytes 14155784 | tf_op jit(solution)/shard_map/ppermute | solution.py:12
  82.4 4.3 %copy-start.1 = (bf16[128,1152]{1,0:T(8,128)(2,1)S(1)}, bf16[128,1152]{1,0:T(8,128)(2,1)}, u32[]{:S(2)}) copy-start(bf16[128,1152]{1,0:T(8,128)(2,1)} %param.5) | copy-start | bytes 884740
  82.4 6.3 %slice-start = ((s8[4718592]{0:T(1024)(128)(4,1)}), s8[4194304]{0:T(1024)(128)(4,1)S(1)}, s32[]{:S(2)}) async-start(s8[4718592]{0:T(1024)(128)(4,1)} %bitcast.13), calls=%async_computation.3 | async-start | bytes 8388608
  86.8 2.0 slice-start.1
  88.2 14.7 %collective-permute-start.1 = (f32[2048,1152]{1,0:T(8,128)S(1)}, f32[2048,1152]{1,0:T(8,128)S(1)}, u32[]{:S(2)}, u32[]{:S(2)}) collective-permute-start(f32[2048,1152]{1,0:T(8,128)S(1)} %fusion.21), channel_id=1, source_target_pairs={{0,16},{16,0},{32,48},{48,32},{64,80},{80,64},{96,112},{112,96},{1... | collective-permute-start | bytes 28311560 | tf_op jit(solution)/shard_map/ppermute | solution.py:12
  111.3 87.8 %copy-start = (bf16[128,1152]{1,0:T(8,128)(2,1)S(1)}, bf16[128,1152]{1,0:T(8,128)(2,1)}, u32[]{:S(2)}) copy-start(bf16[128,1152]{1,0:T(8,128)(2,1)} %param.6) | copy-start | bytes 884740
Sparse Core Ops, SparseCore 0:
  11.0 62.8 all-gather.1
  108.2 90.8 reduce-scatter.1
where the time goes:
time: 210 us; the launch traced here: 209 us
  waiting for transfers between devices  164 us (78%)
  matrix products  19.2 us (9%)
  between operations  16.1 us (8%)
  other arithmetic  8.43 us (4%)
    reduce_scatter x1, waiting for transfers between devices, with_partials(): lax.psum_scatter(own_part + arrived, 'ing', scatter_dimension=0, tiled=True)  83.4 us
    all_gather x1, waiting for transfers between devices, body(): local_text = lax.all_gather(text_half, 'ing', axis=0, tiled=True)  63.7 us
    ppermute x2, waiting for transfers between devices, swapped(): return lax.ppermute(value, axis, pairs)  17.3 us
    dot_general x2, matrix products, loss_factors(): lax.dot_general(left_side, right_side, (((1,), (1,)), ((), ())), preferre...  6.05 us
    dot_general x1, matrix products, with_partials(): lax.dot_general(own_w, image_halfway, contract, preferred_element_type=jn...  5.1 us
  transfers between devices with their start and end apart: 4, of which 4 were waited for; matrix products, arithmetic and copies ran while one was open for 5% of the time, Pallas kernels for 0%

commit v1 on v0

v1 whole, which is shorter than its diff:
```python
import jax
import jax.numpy as jnp
from jax import lax
from jax.sharding import PartitionSpec as P

epsilon = 1e-06
AXES = ("grp", "ing")
SIDE = 4


def ring_pairs(step):
    pairs = []
    for grp in range(lax.axis_size("grp")):
        for ing in range(SIDE * SIDE):
            y, x = divmod(ing, SIDE)
            if grp % 2:
                y = (y + step) % SIDE
            else:
                x = (x + step) % SIDE
            pairs.append((grp * SIDE * SIDE + ing, grp * SIDE * SIDE + y * SIDE + x))
    return pairs


def hop(value, step):
    return lax.ppermute(value, AXES, ring_pairs(step))


def swap(value):
    size = SIDE * SIDE
    pairs = [
        (grp * size + ing, (grp ^ 1) * size + ing)
        for grp in range(lax.axis_size("grp"))
        for ing in range(size)
    ]
    return lax.ppermute(value, AXES, pairs)


def unit_rows(matrix):
    values = matrix.astype(jnp.float32)
    length = jnp.sqrt(jnp.sum(values * values, axis=1, keepdims=True) + epsilon)
    return (values / length, length)


def remove_projection(gradient, unit, length):
    return (gradient - unit * jnp.sum(unit * gradient, axis=1, keepdims=True)) / length


def logits_of(left, right, scale, bias):
    cosine = lax.dot_general(
        left, right, (((1,), (1,)), ((), ())), preferred_element_type=jnp.float32
    )
    return scale * cosine + bias


def body(image_embed, text_embed, scale_logarithm, logit_bias, loss_grad):
    rows = image_embed.shape[0]
    core = lax.axis_index("grp") % 2
    scale = jnp.exp(scale_logarithm[0])
    bias = logit_bias[0]
    factor = loss_grad[0] / (2 * rows * SIDE * SIDE)
    image_unit, image_length = unit_rows(image_embed)
    text_unit, text_length = unit_rows(text_embed)
    image_half = image_unit.astype(jnp.bfloat16)
    text_half = text_unit.astype(jnp.bfloat16)
    first = jnp.where(core == 0, image_half, text_half)
    other = jnp.where(core == 0, text_half, image_half)
    second = swap(other)

    back_first = hop(first, 1)
    ahead_second = hop(second, -1)
    back_second = hop(second, 1)
    ahead_first = hop(first, -1)
    far_first = hop(back_first, 1)
    far_second = hop(ahead_second, -1)

    own = jnp.concatenate([first, second], 0)
    back = jnp.concatenate([back_first, back_second], 0)
    ahead = jnp.concatenate([ahead_first, ahead_second], 0)
    far = jnp.concatenate([far_first, far_second], 0)
    other_own = swap(own)
    other_back = swap(back)
    other_ahead = swap(ahead)
    other_far = swap(far)

    def negative(left, right):
        return (factor * jax.nn.sigmoid(logits_of(left, right, scale, bias))).astype(jnp.bfloat16)

    def with_pairs(left, right):
        ids = jnp.arange(2 * rows, dtype=jnp.int32)
        same = ids[:, None] == ((ids + rows) % (2 * rows))[None, :]
        labels = jnp.where(same, jnp.float32(1.0), jnp.float32(-1.0))
        values = logits_of(left, right, scale, bias)
        return (-factor * labels * jax.nn.sigmoid(-labels * values)).astype(jnp.bfloat16)

    others = jnp.concatenate([other_own, other_back, other_ahead, other_far], 0)

    def share(left):
        return jnp.dot(negative(left, others), others, preferred_element_type=jnp.float32)

    share_far = share(far).astype(jnp.bfloat16)
    share_back = share(back)
    share_ahead = share(ahead)
    rest = jnp.concatenate([other_back, other_ahead, other_far], 0)
    share_own = jnp.dot(
        with_pairs(own, other_own), other_own, preferred_element_type=jnp.float32
    ) + jnp.dot(negative(own, rest), rest, preferred_element_type=jnp.float32)

    relay_first = hop(share_far[:rows], -1)
    relay_second = hop(share_far[rows:], 1)
    from_ahead_second = hop(share_back[rows:].astype(jnp.bfloat16), -1)
    from_back_first = hop(share_ahead[:rows].astype(jnp.bfloat16), 1)
    from_ahead_first = hop((share_back[:rows] + relay_first).astype(jnp.bfloat16), -1)
    from_back_second = hop((share_ahead[rows:] + relay_second).astype(jnp.bfloat16), 1)
    own_first = share_own[:rows] + from_back_first + from_ahead_first
    own_second = share_own[rows:] + from_back_second + from_ahead_second
    other_first = swap(own_second)
    image_dir = jnp.where(core == 0, own_first, other_first)
    text_dir = jnp.where(core == 0, other_first, own_first)
    image_gradient = remove_projection(scale * image_dir, image_unit, image_length)
    text_gradient = remove_projection(scale * text_dir, text_unit, text_length)
    return (image_gradient, text_gradient)


def solution(mesh):
    placed = (P(AXES, None), P(AXES, None), P(), P(), P())
    return jax.shard_map(
        body,
        mesh=mesh,
        in_specs=placed,
        out_specs=(P(AXES, None), P(AXES, None)),
        check_vma=False,
    )
```

time: 210 us -> 79.3 us (0.38)
  waiting for transfers between devices: 164 us -> 17.7 us
  starting transfers between devices: 1.21 us -> 25.2 us
  between operations: 16.1 us -> 2.86 us
  local copies, waits for them, and re-layouts: 0.02 us -> 4.96 us
    reduce_scatter x1 -> x0, waiting for transfers between devices: 83.4 us -> none  [with_partials(): lax.psum_scatter(own_part + arrived, 'ing', scatter_dimension=0, tiled=True)]
    all_gather x1 -> x0, waiting for transfers between devices: 63.7 us -> none  [body(): local_text = lax.all_gather(text_half, 'ing', axis=0, tiled=True)]
    ppermute x2 -> x18, starting transfers between devices: 1.13 us -> 25.2 us  [the longest x6 12.7 us: swap(): return lax.ppermute(value, AXES, pairs)]
    slice x0 -> x3, local copies, waits for them, and re-layouts: none -> 2.38 us  [the longest x1 0.88 us: body(): relay_first = hop(share_far[:rows], -1)]
    unnamed x8 -> x18, local copies, waits for them, and re-layouts: 0.02 us -> 2.34 us
    ppermute x2 -> x18, waiting for transfers between devices: 17.3 us -> 17.7 us  [the longest x12 16.4 us: hop(): return lax.ppermute(value, AXES, ring_pairs(step))]
    dot_general x6 -> x5, matrix products: 19.2 us -> 19 us  [the longest x3 12.1 us: share(): jnp.dot(negative(left, others), others, preferred_element_type=jnp.float32)]
  transfers between devices with their start and end apart: 4 -> 18, of which waited for: 4 -> 5; matrix products, arithmetic and copies ran while one was open for 5% -> 27% of each run, Pallas kernels for 0% -> 0%
where the time goes in v1:
time: 79.3 us; the launch traced here: 78.9 us
  starting transfers between devices  25.2 us (32%)
  matrix products  19 us (24%)
  waiting for transfers between devices  17.7 us (22%)
  other arithmetic  9.19 us (12%)
  local copies, waits for them, and re-layouts  4.96 us (6%)
  between operations  2.86 us (4%)
    ppermute x12, waiting for transfers between devices, hop(): return lax.ppermute(value, AXES, ring_pairs(step))  16.4 us
    ppermute x6, starting transfers between devices, swap(): return lax.ppermute(value, AXES, pairs)  12.7 us
    ppermute x12, starting transfers between devices, hop(): return lax.ppermute(value, AXES, ring_pairs(step))  12.5 us
    dot_general x3, matrix products, share(): jnp.dot(negative(left, others), others, preferred_element_type=jnp.float32)  12.1 us
    dot_general x1, matrix products, body(): jnp.dot(negative(own, rest), rest, preferred_element_type=jnp.float32)  4.64 us
    unnamed x18, local copies, waits for them, and re-layouts  2.34 us
    dot_general x1, matrix products, body(): jnp.dot(with_pairs(own, other_own), other_own, preferred_element_type=jnp...  2.31 us
    reduce_sum x2, other arithmetic, unit_rows(): length = jnp.sqrt(jnp.sum(values * values, axis=1, keepdims=True) + epsilon)  2.21 us
  transfers between devices with their start and end apart: 18, of which 5 were waited for; matrix products, arithmetic and copies ran while one was open for 27% of the time, Pallas kernels for 0%

profile of v1, /device:TPU:1, one launch (start us, length us, event | category | flops | bytes accessed | tf_op | source)
XLA Modules:
  0.0 78.9 jit_solution(133787814961272006)
XLA Ops:
  2.9 1.3 %broadcast_select_fusion = (bf16[128,1152]{1,0:T(8,128)(2,1)S(1)}, bf16[128,1152]{1,0:T(8,128)(2,1)S(1)}) fusion(pred[]{:T(512)S(6)} %eq.29, f32[128]{0:T(128)S(1)} %get-tuple-element.18, bf16[128,1152]{1,0:T(8,128)(2,1)} %param.5, f32[128]{0:T(128)S(1)} %get-tuple-element.17, bf16[128,1152]{1,0:T(8,128)(2,1)} %param.6), kind=kLoop, calls=%fused_computation.87 | loop fusion | flops 1179648 | bytes 1180673 | tf_op jit(solution)/shard_map/jit(_where)/select_n | solution.py:66
  4.2 3.3 %collective-permute-start = (bf16[128,1152]{1,0:T(8,128)(2,1)S(1)}, bf16[128,1152]{1,0:T(8,128)(2,1)S(1)}, u32[]{:S(2)}, u32[]{:S(2)}) collective-permute-start(bf16[128,1152]{1,0:T(8,128)(2,1)S(1)} %get-tuple-element.7), channel_id=1, source_target_pairs={{0,16},{1,17},{2,18},{3,19},{4,20},{5,21},{6,22},{7,23},{8,24},{9,... | collective-permute-start | bytes 884744 | tf_op jit(solution)/shard_map/ppermute | solution.py:35
  7.5 2.7 %collective-permute-start.5 = (bf16[128,1152]{1,0:T(8,128)(2,1)S(1)}, bf16[128,1152]{1,0:T(8,128)(2,1)S(1)}, u32[]{:S(2)}, u32[]{:S(2)}) collective-permute-start(bf16[128,1152]{1,0:T(8,128)(2,1)S(1)} %get-tuple-element.8), channel_id=1, source_target_pairs={{0,3},{1,0},{2,1},{3,2},{4,7},{5,4},{6,5},{7,6},{8,11},{9,8},{10,9... | collective-permute-start | bytes 884744 | tf_op jit(solution)/shard_map/ppermute | solution.py:25
  13.0 2.7 %collective-permute-start.6 = (bf16[128,1152]{1,0:T(8,128)(2,1)S(1)}, bf16[128,1152]{1,0:T(8,128)(2,1)S(1)}, u32[]{:S(2)}, u32[]{:S(2)}) collective-permute-start(bf16[128,1152]{1,0:T(8,128)(2,1)S(1)} %collective-permute-done), channel_id=1, source_target_pairs={{0,3},{1,0},{2,1},{3,2},{4,7},{5,4},{6,5},{7,6},{8,11},{9,8},{10,9... | collective-permute-start | bytes 884744 | tf_op jit(solution)/shard_map/ppermute | solution.py:25
  15.8 4.2 %collective-permute-done.3 = bf16[128,1152]{1,0:T(8,128)(2,1)S(1)} collective-permute-done((bf16[128,1152]{1,0:T(8,128)(2,1)S(1)}, bf16[128,1152]{1,0:T(8,128)(2,1)S(1)}, u32[]{:S(2)}, u32[]{:S(2)}) %collective-permute-start.3) | collective-permute-done | bytes 294944 | tf_op jit(solution)/shard_map/ppermute | solution.py:25
  21.1 1.6 %collective-permute-start.9 = (bf16[128,1152]{1,0:T(8,128)(2,1)S(1)}, bf16[128,1152]{1,0:T(8,128)(2,1)S(1)}, u32[]{:S(2)}, u32[]{:S(2)}) collective-permute-start(bf16[128,1152]{1,0:T(8,128)(2,1)S(1)} %collective-permute-done.6), channel_id=1, source_target_pairs={{0,3},{1,0},{2,1},{3,2},{4,7},{5,4},{6,5},{7,6},{8,11},{9,8},{10,9... | collective-permute-start | bytes 884744 | tf_op jit(solution)/shard_map/ppermute | solution.py:25
  22.8 1.6 %collective-permute-start.7 = (bf16[256,1152]{1,0:T(8,128)(2,1)S(1)}, bf16[256,1152]{1,0:T(8,128)(2,1)S(1)}, u32[]{:S(2)}, u32[]{:S(2)}) collective-permute-start(bf16[256,1152]{1,0:T(8,128)(2,1)S(1)} %constant_dynamic-update-slice_fusion.2), channel_id=1, source_target_pairs={{0,16},{1,17},{2,18},{3,19},{4,20},{5,21},{6,22},{7,23},{8,24},{9,... | collective-permute-start | bytes 1769480 | tf_op jit(solution)/shard_map/ppermute | solution.py:35
  24.4 2.6 %collective-permute-done.9 = bf16[128,1152]{1,0:T(8,128)(2,1)S(1)} collective-permute-done((bf16[128,1152]{1,0:T(8,128)(2,1)S(1)}, bf16[128,1152]{1,0:T(8,128)(2,1)S(1)}, u32[]{:S(2)}, u32[]{:S(2)}) %collective-permute-start.9) | collective-permute-done | bytes 294944 | tf_op jit(solution)/shard_map/ppermute | solution.py:25
  27.0 1.6 %collective-permute-start.10 = (bf16[256,1152]{1,0:T(8,128)(2,1)S(1)}, bf16[256,1152]{1,0:T(8,128)(2,1)S(1)}, u32[]{:S(2)}, u32[]{:S(2)}) collective-permute-start(bf16[256,1152]{1,0:T(8,128)(2,1)S(1)} %constant_dynamic-update-slice_fusion.4), channel_id=1, source_target_pairs={{0,16},{1,17},{2,18},{3,19},{4,20},{5,21},{6,22},{7,23},{8,24},{9,... | collective-permute-start | bytes 1769480 | tf_op jit(solution)/shard_map/ppermute | solution.py:35
  29.0 1.3 %collective-permute-done.10 = bf16[256,1152]{1,0:T(8,128)(2,1)S(1)} collective-permute-done((bf16[256,1152]{1,0:T(8,128)(2,1)S(1)}, bf16[256,1152]{1,0:T(8,128)(2,1)S(1)}, u32[]{:S(2)}, u32[]{:S(2)}) %collective-permute-start.10) | collective-permute-done | bytes 589856 | tf_op jit(solution)/shard_map/ppermute | solution.py:35
  30.4 1.2 %copy-done.3 = bf16[768,1152]{1,0:T(8,128)(2,1)} copy-done((bf16[768,1152]{1,0:T(8,128)(2,1)}, bf16[768,1152]{1,0:T(8,128)(2,1)S(1)}, u32[]{:S(2)}) %copy-start.3) | copy-done | bytes 1769496
  32.3 4.0 %convolution_convert_fusion = bf16[256,1152]{1,0:T(8,128)(2,1)S(1)} fusion(bf16[1024,1152]{1,0:T(8,128)(2,1)} %copy-done.4, bf16[256,1152]{1,0:T(8,128)(2,1)S(1)} %constant_dynamic-update-slice_fusion.4, f32[]{:T(128)} %bitcast.19, f32[]{:T(128)} %bitcast, f32[]{:T(128)} %bitcast.1), kind=kOutput, calls=%fused_computation.1 | convolution fusion | flops 1210089472 | bytes 3538956 | tf_op jit(solution)/shard_map/dot_general | solution.py:98
  37.2 1.4 %collective-permute-start.12 = (bf16[128,1152]{1,0:T(8,128)(2,1)}, bf16[128,1152]{1,0:T(8,128)(2,1)}, u32[]{:S(2)}, u32[]{:S(2)}) collective-permute-start(bf16[128,1152]{1,0:T(8,128)(2,1)} %get-tuple-element.9), channel_id=1, source_target_pairs={{0,3},{1,0},{2,1},{3,2},{4,7},{5,4},{6,5},{7,6},{8,11},{9,8},{10,9... | collective-permute-start | bytes 884744 | tf_op jit(solution)/shard_map/ppermute | solution.py:25
  38.6 4.0 %fusion.37 = f32[256,1152]{1,0:T(8,128)S(1)} fusion(bf16[1024,1152]{1,0:T(8,128)(2,1)} %copy-done.4, bf16[256,1152]{1,0:T(8,128)(2,1)S(1)} %constant_dynamic-update-slice_fusion, f32[]{:T(128)} %bitcast.20, f32[]{:T(128)} %bitcast, f32[]{:T(128)} %bitcast.1), kind=kOutput, calls=%fused_computation.44 | convolution fusion | flops 1209794560 | bytes 4128780 | tf_op jit(solution)/shard_map/dot_general | solution.py:98
  42.9 4.1 %fusion.38 = f32[256,1152]{1,0:T(8,128)S(1)} fusion(bf16[1024,1152]{1,0:T(8,128)(2,1)} %copy-done.4, bf16[256,1152]{1,0:T(8,128)(2,1)} %copy-done.5, f32[]{:T(128)} %bitcast.18, f32[]{:T(128)} %bitcast, f32[]{:T(128)} %bitcast.1), kind=kOutput, calls=%fused_computation.45 | convolution fusion | flops 1209794560 | bytes 4128780 | tf_op jit(solution)/shard_map/dot_general | solution.py:98
  47.8 2.6 %collective-permute-start.16 = (bf16[128,1152]{1,0:T(8,128)(2,1)}, bf16[128,1152]{1,0:T(8,128)(2,1)}, u32[]{:S(2)}, u32[]{:S(2)}) collective-permute-start(bf16[128,1152]{1,0:T(8,128)(2,1)} %slice.56), channel_id=1, source_target_pairs={{0,3},{1,0},{2,1},{3,2},{4,7},{5,4},{6,5},{7,6},{8,11},{9,8},{10,9... | collective-permute-start | bytes 884744 | tf_op jit(solution)/shard_map/ppermute | solution.py:25
  51.1 4.6 %fusion.36 = f32[256,1152]{1,0:T(8,128)} fusion(bf16[768,1152]{1,0:T(8,128)(2,1)} %copy-done.3, f32[]{:T(128)} %bitcast.17, f32[]{:T(128)} %bitcast, f32[]{:T(128)} %bitcast.1, bf16[128,1152]{1,0:T(8,128)(2,1)} %copy-done.2, bf16[128,1152]{1,0:T(8,128)(2,1)S(1)} %get-tuple-element.8), kind=kOutput, calls=%fused_computation.43 | convolution fusion | flops 908525568 | bytes 3538956 | tf_op jit(solution)/shard_map/dot_general | solution.py:106
  55.8 1.7 %fusion.41 = bf16[128,1152]{1,0:T(8,128)(2,1)} fusion(f32[256,1152]{1,0:T(8,128)S(1)} %fusion.38, bf16[128,1152]{1,0:T(8,128)(2,1)} %collective-permute-done.14), kind=kLoop, calls=%fused_computation.54 | loop fusion | flops 442368 | bytes 1179648 | tf_op jit(solution)/shard_map/convert_element_type | solution.py:113
  57.5 2.3 %convolution_add_fusion = f32[256,1152]{1,0:T(8,128)S(1)} fusion(f32[256,1152]{1,0:T(8,128)} %fusion.36, bf16[256,1152]{1,0:T(8,128)(2,1)S(1)} %collective-permute-done.1, f32[]{:T(128)} %bitcast.16, f32[]{:T(128)} %bitcast, s32[256]{0:T(256)S(1)} %and_select_fusion, f32[]{:T(128)S(6)} %neg.21, bf16[128,1152]{1,0:T(8,128)(2,1)} %copy-done.2, ...), kind=kOutput, calls=%fused_computation | convolution fusion | flops 304250880 | bytes 3539980 | tf_op jit(solution)/shard_map/dot_general | solution.py:104
  59.9 4.7 %collective-permute-done.15 = bf16[128,1152]{1,0:T(8,128)(2,1)} collective-permute-done((bf16[128,1152]{1,0:T(8,128)(2,1)}, bf16[128,1152]{1,0:T(8,128)(2,1)}, u32[]{:S(2)}, u32[]{:S(2)}) %collective-permute-start.15) | collective-permute-done | bytes 294944 | tf_op jit(solution)/shard_map/ppermute | solution.py:25
  64.6 1.1 %fusion.42 = f32[128,1152]{1,0:T(8,128)S(1)} fusion(f32[256,1152]{1,0:T(8,128)S(1)} %convolution_add_fusion, bf16[128,1152]{1,0:T(8,128)(2,1)} %collective-permute-done.16, bf16[128,1152]{1,0:T(8,128)(2,1)} %collective-permute-done.15), kind=kLoop, calls=%fused_computation.56 | loop fusion | flops 589824 | bytes 1769472 | tf_op jit(solution)/shard_map/add | solution.py:115
  65.8 4.4 %collective-permute-start.17 = (f32[128,1152]{1,0:T(8,128)S(1)}, f32[128,1152]{1,0:T(8,128)S(1)}, u32[]{:S(2)}, u32[]{:S(2)}) collective-permute-start(f32[128,1152]{1,0:T(8,128)S(1)} %fusion.42), channel_id=1, source_target_pairs={{0,16},{1,17},{2,18},{3,19},{4,20},{5,21},{6,22},{7,23},{8,24},{9,... | collective-permute-start | bytes 1769480 | tf_op jit(solution)/shard_map/ppermute | solution.py:35
  72.3 4.9 %collective-permute-done.13 = bf16[128,1152]{1,0:T(8,128)(2,1)S(1)} collective-permute-done((bf16[128,1152]{1,0:T(8,128)(2,1)S(1)}, bf16[128,1152]{1,0:T(8,128)(2,1)S(1)}, u32[]{:S(2)}, u32[]{:S(2)}) %collective-permute-start.13) | collective-permute-done | bytes 294944 | tf_op jit(solution)/shard_map/ppermute | solution.py:25
  77.6 1.3 %subtract_divide_fusion = (f32[128,1152]{1,0:T(8,128)}, f32[128,1152]{1,0:T(8,128)}) fusion(f32[128]{0:T(128)S(1)} %get-tuple-element.2, f32[128]{0:T(128)S(1)} %get-tuple-element.17, f32[128,1152]{1,0:T(8,128)S(1)} %collective-permute-done.17, f32[128,1152]{1,0:T(8,128)S(1)} %get-tuple-element.4, pred[]{:T(512)S(6)} %eq.29, f32[]{:T(128)} %bitcast, ...), kind=kLoop, calls=%fused_computation.63 | loop fusion | flops 2064384 | bytes 2951173 | tf_op jit(solution)/shard_map/div | solution.py:45
  (53 shorter events, 10.7 us)
Async XLA Ops:
  4.2 8.0 %collective-permute-start = (bf16[128,1152]{1,0:T(8,128)(2,1)S(1)}, bf16[128,1152]{1,0:T(8,128)(2,1)S(1)}, u32[]{:S(2)}, u32[]{:S(2)}) collective-permute-start(bf16[128,1152]{1,0:T(8,128)(2,1)S(1)} %get-tuple-element.7), channel_id=1, source_target_pairs={{0,16},{1,17},{2,18},{3,19},{4,20},{5,21},{6,22},{7,23},{8,24},{9,... | collective-permute-start | bytes 884744 | tf_op jit(solution)/shard_map/ppermute | solution.py:35
  7.5 8.2 %collective-permute-start.2 = (bf16[128,1152]{1,0:T(8,128)(2,1)S(1)}, bf16[128,1152]{1,0:T(8,128)(2,1)S(1)}, u32[]{:S(2)}, u32[]{:S(2)}) collective-permute-start(bf16[128,1152]{1,0:T(8,128)(2,1)S(1)} %get-tuple-element.8), channel_id=1, source_target_pairs={{0,1},{1,2},{2,3},{3,0},{4,5},{5,6},{6,7},{7,4},{8,9},{9,10},{10,1... | collective-permute-start | bytes 884744 | tf_op jit(solution)/shard_map/ppermute | solution.py:25
  7.5 8.3 %collective-permute-start.5 = (bf16[128,1152]{1,0:T(8,128)(2,1)S(1)}, bf16[128,1152]{1,0:T(8,128)(2,1)S(1)}, u32[]{:S(2)}, u32[]{:S(2)}) collective-permute-start(bf16[128,1152]{1,0:T(8,128)(2,1)S(1)} %get-tuple-element.8), channel_id=1, source_target_pairs={{0,3},{1,0},{2,1},{3,2},{4,7},{5,4},{6,5},{7,6},{8,11},{9,8},{10,9... | collective-permute-start | bytes 884744 | tf_op jit(solution)/shard_map/ppermute | solution.py:25
  12.2 10.6 %copy-start.2 = (bf16[128,1152]{1,0:T(8,128)(2,1)}, bf16[128,1152]{1,0:T(8,128)(2,1)S(1)}, u32[]{:S(2)}) copy-start(bf16[128,1152]{1,0:T(8,128)(2,1)S(1)} %collective-permute-done) | copy-start | bytes 884740
  12.2 16.4 %collective-permute-start.1 = (bf16[256,1152]{1,0:T(8,128)(2,1)S(1)}, bf16[256,1152]{1,0:T(8,128)(2,1)S(1)}, u32[]{:S(2)}, u32[]{:S(2)}) collective-permute-start(bf16[256,1152]{1,0:T(8,128)(2,1)S(1)} %pad_maximum_fusion), channel_id=1, source_target_pairs={{0,16},{1,17},{2,18},{3,19},{4,20},{5,21},{6,22},{7,23},{8,24},{9,... | collective-permute-start | bytes 1769480 | tf_op jit(solution)/shard_map/ppermute | solution.py:35
  13.0 7.1 %collective-permute-start.3 = (bf16[128,1152]{1,0:T(8,128)(2,1)S(1)}, bf16[128,1152]{1,0:T(8,128)(2,1)S(1)}, u32[]{:S(2)}, u32[]{:S(2)}) collective-permute-start(bf16[128,1152]{1,0:T(8,128)(2,1)S(1)} %collective-permute-done), channel_id=1, source_target_pairs={{0,1},{1,2},{2,3},{3,0},{4,5},{5,6},{6,7},{7,4},{8,9},{9,10},{10,1... | collective-permute-start | bytes 884744 | tf_op jit(solution)/shard_map/ppermute | solution.py:25
  13.0 8.1 %collective-permute-start.6 = (bf16[128,1152]{1,0:T(8,128)(2,1)S(1)}, bf16[128,1152]{1,0:T(8,128)(2,1)S(1)}, u32[]{:S(2)}, u32[]{:S(2)}) collective-permute-start(bf16[128,1152]{1,0:T(8,128)(2,1)S(1)} %collective-permute-done), channel_id=1, source_target_pairs={{0,3},{1,0},{2,1},{3,2},{4,7},{5,4},{6,5},{7,6},{8,11},{9,8},{10,9... | collective-permute-start | bytes 884744 | tf_op jit(solution)/shard_map/ppermute | solution.py:25
  15.7 8.7 %collective-permute-start.8 = (bf16[128,1152]{1,0:T(8,128)(2,1)S(1)}, bf16[128,1152]{1,0:T(8,128)(2,1)S(1)}, u32[]{:S(2)}, u32[]{:S(2)}) collective-permute-start(bf16[128,1152]{1,0:T(8,128)(2,1)S(1)} %collective-permute-done.2), channel_id=1, source_target_pairs={{0,1},{1,2},{2,3},{3,0},{4,5},{5,6},{6,7},{7,4},{8,9},{9,10},{10,1... | collective-permute-start | bytes 884744 | tf_op jit(solution)/shard_map/ppermute | solution.py:25
  20.1 8.6 %collective-permute-start.4 = (bf16[256,1152]{1,0:T(8,128)(2,1)S(1)}, bf16[256,1152]{1,0:T(8,128)(2,1)S(1)}, u32[]{:S(2)}, u32[]{:S(2)}) collective-permute-start(bf16[256,1152]{1,0:T(8,128)(2,1)S(1)} %constant_dynamic-update-slice_fusion), channel_id=1, source_target_pairs={{0,16},{1,17},{2,18},{3,19},{4,20},{5,21},{6,22},{7,23},{8,24},{9,... | collective-permute-start | bytes 1769480 | tf_op jit(solution)/shard_map/ppermute | solution.py:35
  21.1 5.9 %collective-permute-start.9 = (bf16[128,1152]{1,0:T(8,128)(2,1)S(1)}, bf16[128,1152]{1,0:T(8,128)(2,1)S(1)}, u32[]{:S(2)}, u32[]{:S(2)}) collective-permute-start(bf16[128,1152]{1,0:T(8,128)(2,1)S(1)} %collective-permute-done.6), channel_id=1, source_target_pairs={{0,3},{1,0},{2,1},{3,2},{4,7},{5,4},{6,5},{7,6},{8,11},{9,8},{10,9... | collective-permute-start | bytes 884744 | tf_op jit(solution)/shard_map/ppermute | solution.py:25
  22.8 6.0 %copy-start.5 = (bf16[256,1152]{1,0:T(8,128)(2,1)}, bf16[256,1152]{1,0:T(8,128)(2,1)S(1)}, u32[]{:S(2)}) copy-start(bf16[256,1152]{1,0:T(8,128)(2,1)S(1)} %constant_dynamic-update-slice_fusion.2) | copy-start | bytes 1769476
  22.8 6.0 %collective-permute-start.7 = (bf16[256,1152]{1,0:T(8,128)(2,1)S(1)}, bf16[256,1152]{1,0:T(8,128)(2,1)S(1)}, u32[]{:S(2)}, u32[]{:S(2)}) collective-permute-start(bf16[256,1152]{1,0:T(8,128)(2,1)S(1)} %constant_dynamic-update-slice_fusion.2), channel_id=1, source_target_pairs={{0,16},{1,17},{2,18},{3,19},{4,20},{5,21},{6,22},{7,23},{8,24},{9,... | collective-permute-start | bytes 1769480 | tf_op jit(solution)/shard_map/ppermute | solution.py:35
  27.0 3.2 %collective-permute-start.10 = (bf16[256,1152]{1,0:T(8,128)(2,1)S(1)}, bf16[256,1152]{1,0:T(8,128)(2,1)S(1)}, u32[]{:S(2)}, u32[]{:S(2)}) collective-permute-start(bf16[256,1152]{1,0:T(8,128)(2,1)S(1)} %constant_dynamic-update-slice_fusion.4), channel_id=1, source_target_pairs={{0,16},{1,17},{2,18},{3,19},{4,20},{5,21},{6,22},{7,23},{8,24},{9,... | collective-permute-start | bytes 1769480 | tf_op jit(solution)/shard_map/ppermute | solution.py:35
  30.4 1.2 %copy-start.3 = (bf16[768,1152]{1,0:T(8,128)(2,1)}, bf16[768,1152]{1,0:T(8,128)(2,1)S(1)}, u32[]{:S(2)}) copy-start(bf16[768,1152]{1,0:T(8,128)(2,1)S(1)} %get-tuple-element.12) | copy-start | bytes 5308420
  30.4 1.9 %copy-start.4 = (bf16[1024,1152]{1,0:T(8,128)(2,1)}, bf16[1024,1152]{1,0:T(8,128)(2,1)S(1)}, u32[]{:S(2)}) copy-start(bf16[1024,1152]{1,0:T(8,128)(2,1)S(1)} %get-tuple-element.11) | copy-start | bytes 7077892
  37.2 33.0 %collective-permute-start.12 = (bf16[128,1152]{1,0:T(8,128)(2,1)}, bf16[128,1152]{1,0:T(8,128)(2,1)}, u32[]{:S(2)}, u32[]{:S(2)}) collective-permute-start(bf16[128,1152]{1,0:T(8,128)(2,1)} %get-tuple-element.9), channel_id=1, source_target_pairs={{0,3},{1,0},{2,1},{3,2},{4,7},{5,4},{6,5},{7,6},{8,11},{9,8},{10,9... | collective-permute-start | bytes 884744 | tf_op jit(solution)/shard_map/ppermute | solution.py:25
  42.6 13.2 %collective-permute-start.14 = (bf16[128,1152]{1,0:T(8,128)(2,1)}, bf16[128,1152]{1,0:T(8,128)(2,1)}, u32[]{:S(2)}, u32[]{:S(2)}) collective-permute-start(bf16[128,1152]{1,0:T(8,128)(2,1)} %get-tuple-element.10), channel_id=1, source_target_pairs={{0,1},{1,2},{2,3},{3,0},{4,5},{5,6},{6,7},{7,4},{8,9},{9,10},{10,1... | collective-permute-start | bytes 884744 | tf_op jit(solution)/shard_map/ppermute | solution.py:25
  47.8 12.1 %collective-permute-start.16 = (bf16[128,1152]{1,0:T(8,128)(2,1)}, bf16[128,1152]{1,0:T(8,128)(2,1)}, u32[]{:S(2)}, u32[]{:S(2)}) collective-permute-start(bf16[128,1152]{1,0:T(8,128)(2,1)} %slice.56), channel_id=1, source_target_pairs={{0,3},{1,0},{2,1},{3,2},{4,7},{5,4},{6,5},{7,6},{8,11},{9,8},{10,9... | collective-permute-start | bytes 884744 | tf_op jit(solution)/shard_map/ppermute | solution.py:25
  51.1 21.2 %collective-permute-start.11 = (bf16[128,1152]{1,0:T(8,128)(2,1)}, bf16[128,1152]{1,0:T(8,128)(2,1)S(1)}, u32[]{:S(2)}, u32[]{:S(2)}) collective-permute-start(bf16[128,1152]{1,0:T(8,128)(2,1)} %slice.57), channel_id=1, source_target_pairs={{0,1},{1,2},{2,3},{3,0},{4,5},{5,6},{6,7},{7,4},{8,9},{9,10},{10,1... | collective-permute-start | bytes 884744 | tf_op jit(solution)/shard_map/ppermute | solution.py:25
  57.5 7.1 %collective-permute-start.15 = (bf16[128,1152]{1,0:T(8,128)(2,1)}, bf16[128,1152]{1,0:T(8,128)(2,1)}, u32[]{:S(2)}, u32[]{:S(2)}) collective-permute-start(bf16[128,1152]{1,0:T(8,128)(2,1)} %fusion.41), channel_id=1, source_target_pairs={{0,1},{1,2},{2,3},{3,0},{4,5},{5,6},{6,7},{7,4},{8,9},{9,10},{10,1... | collective-permute-start | bytes 884744 | tf_op jit(solution)/shard_map/ppermute | solution.py:25
  59.8 17.3 %copy-start = (bf16[128,1152]{1,0:T(8,128)(2,1)S(1)}, bf16[128,1152]{1,0:T(8,128)(2,1)}, u32[]{:S(2)}) copy-start(bf16[128,1152]{1,0:T(8,128)(2,1)} %param.6) | copy-start | bytes 884740
  59.9 17.3 %copy-start.1 = (bf16[128,1152]{1,0:T(8,128)(2,1)S(1)}, bf16[128,1152]{1,0:T(8,128)(2,1)}, u32[]{:S(2)}) copy-start(bf16[128,1152]{1,0:T(8,128)(2,1)} %param.5) | copy-start | bytes 884740
  65.8 11.4 %collective-permute-start.17 = (f32[128,1152]{1,0:T(8,128)S(1)}, f32[128,1152]{1,0:T(8,128)S(1)}, u32[]{:S(2)}, u32[]{:S(2)}) collective-permute-start(f32[128,1152]{1,0:T(8,128)S(1)} %fusion.42), channel_id=1, source_target_pairs={{0,16},{1,17},{2,18},{3,19},{4,20},{5,21},{6,22},{7,23},{8,24},{9,... | collective-permute-start | bytes 1769480 | tf_op jit(solution)/shard_map/ppermute | solution.py:35
  71.2 5.9 %collective-permute-start.13 = (bf16[128,1152]{1,0:T(8,128)(2,1)S(1)}, bf16[128,1152]{1,0:T(8,128)(2,1)S(1)}, u32[]{:S(2)}, u32[]{:S(2)}) collective-permute-start(bf16[128,1152]{1,0:T(8,128)(2,1)S(1)} %fusion.43), channel_id=1, source_target_pairs={{0,3},{1,0},{2,1},{3,2},{4,7},{5,4},{6,5},{7,6},{8,11},{9,8},{10,9... | collective-permute-start | bytes 884744 | tf_op jit(solution)/shard_map/ppermute | solution.py:25

commit v2 on v1

v2 whole, which is shorter than its diff:
```python
import jax
import jax.numpy as jnp
from jax import lax
from jax.experimental import pallas as pl
from jax.experimental.pallas import tpu as pltpu
from jax.sharding import PartitionSpec as P

epsilon = 1e-06
AXES = ("grp", "ing")
SIDE = 4
VMEM_BYTES = 16 * 1024 * 1024
VMEM = pl.BlockSpec(memory_space=pltpu.VMEM)
SMEM = pl.BlockSpec(memory_space=pltpu.SMEM)


def moved(value, step, core_change=0, ring_change=0):
    size = SIDE * SIDE
    pairs = []
    for grp in range(lax.axis_size("grp")):
        target = grp ^ core_change
        for ing in range(size):
            y, x = divmod(ing, SIDE)
            if (grp ^ ring_change) % 2:
                y = (y + step) % SIDE
            else:
                x = (x + step) % SIDE
            pairs.append((grp * size + ing, target * size + y * SIDE + x))
    return lax.ppermute(value, AXES, pairs)


def hop(value, step):
    return moved(value, step)


def cross(value, step):
    return moved(value, step, 1, 1)


def cross_back(value, step):
    return moved(value, step, 1, 0)


def swap(value):
    return moved(value, 0, 1)


def dot_t(left, right):
    return lax.dot_general(left, right, (((1,), (1,)), ((), ())), preferred_element_type=jnp.float32)


def dot(left, right):
    return jnp.dot(left, right, preferred_element_type=jnp.float32)


def call(kernel, outs, specs, flops, name):
    run = pl.pallas_call(
        kernel,
        out_shape=[pltpu.VMEM(o.shape, o.dtype) for o in outs],
        in_specs=specs,
        out_specs=[VMEM] * len(outs),
        cost_estimate=pl.CostEstimate(flops=flops, bytes_accessed=flops // 4000, transcendentals=0),
        compiler_params=pltpu.CompilerParams(vmem_limit_bytes=VMEM_BYTES),
        name=name,
    )
    return lambda *args: run(
        *[pltpu.with_memory_space_constraint(a, pltpu.VMEM) if s is VMEM else a for a, s in zip(args, specs)]
    )


def unit_rows(matrix):
    values = matrix.astype(jnp.float32)
    length = jnp.sqrt(jnp.sum(values * values, axis=1, keepdims=True) + epsilon)
    return (values / length, length)


def norm_kernel(core, image, text, first, other):
    image_half = unit_rows(image[...])[0].astype(jnp.bfloat16)
    text_half = unit_rows(text[...])[0].astype(jnp.bfloat16)

    @pl.when(core[0] == 0)
    def _():
        first[...] = image_half
        other[...] = text_half

    @pl.when(core[0] != 0)
    def _():
        first[...] = text_half
        other[...] = image_half


def negative(cosine, consts):
    return (consts[2] / (1.0 + jnp.exp(-(consts[0] * cosine + consts[1])))).astype(jnp.bfloat16)


def positive(cosine, consts):
    return (-consts[2] / (1.0 + jnp.exp(consts[0] * cosine + consts[1]))).astype(jnp.bfloat16)


def near_kernel(consts, first, other, second, other_second, back_first, back_second, ahead_first,
                ahead_second, near_others, late_others, w_own, w_back, w_ahead):
    rows = first.shape[0]
    lefts = [(w_own, first, second), (w_back, back_first, back_second), (w_ahead, ahead_first, ahead_second)]
    rights = [(other, other_second), (near_others,), (late_others,)]
    for place, parts in enumerate(rights):
        right = jnp.concatenate([p[...] for p in parts], 0) if len(parts) > 1 else parts[0][...]
        cols = pl.ds(place * 2 * rows, 2 * rows)
        for out, up, down in lefts:
            cosine = dot_t(jnp.concatenate([up[...], down[...]], 0), right)
            weights = negative(cosine, consts)
            if place == 0 and out is w_own:
                i = lax.broadcasted_iota(jnp.int32, cosine.shape, 0)
                j = lax.broadcasted_iota(jnp.int32, cosine.shape, 1)
                weights = jnp.where(i == j, positive(cosine, consts), weights)
            out[:, cols] = weights


def far_w_kernel(consts, far_first, far_second, other, other_second, near_others, late_others, w_far):
    rows = far_first.shape[0]
    left = jnp.concatenate([far_first[...], far_second[...]], 0)
    rights = [(other, other_second), (near_others,), (late_others,)]
    for place, parts in enumerate(rights):
        right = jnp.concatenate([p[...] for p in parts], 0) if len(parts) > 1 else parts[0][...]
        w_far[:, pl.ds(place * 2 * rows, 2 * rows)] = negative(dot_t(left, right), consts)


def mixed(weights, far_weights, other, other_second, near_others, late_others, far_others):
    rows = other.shape[0]
    total = dot(weights[:, : rows], other[...])
    total += dot(weights[:, rows : 2 * rows], other_second[...])
    total += dot(weights[:, 2 * rows : 4 * rows], near_others[...])
    total += dot(weights[:, 4 * rows :], late_others[...])
    return total + dot(far_weights, far_others[...])


def far_kernel(consts, w_far, far_first, far_second, other, other_second, near_others, late_others,
               far_others, share_first, share_second):
    rows = far_first.shape[0]
    left = jnp.concatenate([far_first[...], far_second[...]], 0)
    weights = negative(dot_t(left, far_others[...]), consts)
    total = mixed(w_far[...], weights, other, other_second, near_others, late_others, far_others)
    share_first[...] = total[:rows].astype(jnp.bfloat16)
    share_second[...] = total[rows:].astype(jnp.bfloat16)


def share_kernel(consts, w_back, w_ahead, back_first, back_second, ahead_first, ahead_second, other,
                 other_second, near_others, late_others, far_others, out_back_first, out_back_second,
                 out_ahead_first, out_ahead_second):
    rows = other.shape[0]
    for weights, up, down, out_up, out_down in (
        (w_back, back_first, back_second, out_back_first, out_back_second),
        (w_ahead, ahead_first, ahead_second, out_ahead_first, out_ahead_second),
    ):
        left = jnp.concatenate([up[...], down[...]], 0)
        last = negative(dot_t(left, far_others[...]), consts)
        total = mixed(weights[...], last, other, other_second, near_others, late_others, far_others)
        out_up[...] = total[:rows].astype(out_up.dtype)
        out_down[...] = total[rows:].astype(out_down.dtype)


def own_kernel(consts, w_own, first, second, other, other_second, near_others, late_others,
               far_others, out_first, out_second):
    rows = other.shape[0]
    left = jnp.concatenate([first[...], second[...]], 0)
    last = negative(dot_t(left, far_others[...]), consts)
    total = mixed(w_own[...], last, other, other_second, near_others, late_others, far_others)
    out_first[...] = total[:rows]
    out_second[...] = total[rows:]


def relay_kernel(up, up_got, down, down_got, up_out, down_out):
    up_out[...] = (up[...] + up_got[...].astype(jnp.float32)).astype(jnp.bfloat16)
    down_out[...] = (down[...] + down_got[...].astype(jnp.float32)).astype(jnp.bfloat16)


def last_kernel(core, consts, image, text, own, own_one, own_two, their, their_one, their_two, image_out, text_out):
    own_dir = consts[0] * (own[...] + own_one[...].astype(jnp.float32) + own_two[...].astype(jnp.float32))
    their_dir = consts[0] * (their[...] + their_one[...].astype(jnp.float32) + their_two[...].astype(jnp.float32))
    is_image = core[0] == 0
    for embed, out, direction in (
        (image, image_out, jnp.where(is_image, own_dir, their_dir)),
        (text, text_out, jnp.where(is_image, their_dir, own_dir)),
    ):
        unit, length = unit_rows(embed[...])
        out[...] = (direction - unit * jnp.sum(unit * direction, axis=1, keepdims=True)) / length


def body(image_embed, text_embed, scale_logarithm, logit_bias, loss_grad):
    rows, width = image_embed.shape
    half = jax.ShapeDtypeStruct((rows, width), jnp.bfloat16)
    full = jax.ShapeDtypeStruct((rows, width), jnp.float32)
    core = (lax.axis_index("grp") % 2).astype(jnp.int32).reshape(1)
    consts = jnp.concatenate(
        [jnp.exp(scale_logarithm), logit_bias, loss_grad / (2 * rows * SIDE * SIDE)]
    )
    unit = 2 * rows * rows * width

    first, other = call(norm_kernel, [half, half], [SMEM, VMEM, VMEM], 10**8, "norms")(
        core, image_embed, text_embed
    )
    back_first = hop(first, 1)
    ahead_second = cross(other, -1)
    other_second = swap(first)
    second = swap(other)
    back_second = hop(second, 1)
    ahead_first = cross(other_second, -1)
    near_others = swap(jnp.concatenate([back_first, ahead_second], 0))
    far_first = hop(back_first, 1)
    far_second = hop(ahead_second, -1)
    late_others = swap(jnp.concatenate([back_second, ahead_first], 0))
    far_others = swap(jnp.concatenate([far_first, far_second], 0))

    weights_shape = jax.ShapeDtypeStruct((2 * rows, 6 * rows), jnp.bfloat16)
    w_own, w_back, w_ahead = call(
        near_kernel, [weights_shape] * 3, [SMEM] + [VMEM] * 10, 36 * unit, "near"
    )(consts, first, other, second, other_second, back_first, back_second, ahead_first, ahead_second,
      near_others, late_others)
    (w_far,) = call(far_w_kernel, [weights_shape], [SMEM] + [VMEM] * 6, 12 * unit, "far_weights")(
        consts, far_first, far_second, other, other_second, near_others, late_others
    )
    others = (other, other_second, near_others, late_others, far_others)
    share_first, share_second = call(
        far_kernel, [half, half], [SMEM] + [VMEM] * 8, 20 * unit, "far"
    )(consts, w_far, far_first, far_second, *others)
    relay_first = hop(share_first, -1)
    relay_second = hop(share_second, 1)
    keep_back_first, share_back_second, share_ahead_first, keep_ahead_second = call(
        share_kernel, [full, half, half, full], [SMEM] + [VMEM] * 11, 40 * unit, "shares"
    )(consts, w_back, w_ahead, back_first, back_second, ahead_first, ahead_second, *others)
    their_one = cross_back(share_back_second, -1)
    own_one = hop(share_ahead_first, 1)
    own_first, own_second = call(own_kernel, [full, full], [SMEM] + [VMEM] * 8, 20 * unit, "own")(
        consts, w_own, first, second, *others
    )
    their_second = swap(own_second)
    send_first, send_second = call(relay_kernel, [half, half], [VMEM] * 4, 10**7, "relay")(
        keep_back_first, relay_first, keep_ahead_second, relay_second
    )
    own_two = hop(send_first, -1)
    their_two = cross_back(send_second, 1)
    image_gradient, text_gradient = call(
        last_kernel, [full, full], [SMEM] * 2 + [VMEM] * 8, 10**8, "last"
    )(core, consts, image_embed, text_embed, own_first, own_one, own_two, their_second, their_one, their_two)
    return (image_gradient, text_gradient)


def solution(mesh):
    placed = (P(AXES, None), P(AXES, None), P(), P(), P())
    return jax.shard_map(
        body,
        mesh=mesh,
        in_specs=placed,
        out_specs=(P(AXES, None), P(AXES, None)),
        check_vma=False,
    )
```

time: 79.3 us -> 52.3 us (0.66)
  matrix products: 19 us -> 0 us
  Pallas kernels: 0 us -> 11.7 us
  other arithmetic: 9.19 us -> 0.22 us
  waiting for transfers between devices: 17.7 us -> 12.4 us
  starting transfers between devices: 25.2 us -> 21.5 us
  local copies, waits for them, and re-layouts: 4.96 us -> 3.56 us
    dot_general x5 -> x0, matrix products: 19 us -> none  [the longest x3 12.1 us: share(): jnp.dot(negative(left, others), others, preferred_element_type=jnp.float32)]
    pallas_call x0 -> x8, Pallas kernels: none -> 11.7 us  [call(): run(*[pltpu.with_memory_space_constraint(a, pltpu.VMEM) if s is VMEM else...]
    ppermute x18, waiting for transfers between devices: 17.7 us -> 12.4 us  [moved(): return lax.ppermute(value, AXES, pairs)]
    ppermute x18, starting transfers between devices: 25.2 us -> 21.5 us  [moved(): return lax.ppermute(value, AXES, pairs)]
    convert_element_type x2 -> x0, other arithmetic: 2.75 us -> none  [the longest x1 1.74 us: body(): (share_ahead[rows:] + relay_second).astype(jnp.bfloat16)]
    reduce_sum x3 -> x0, other arithmetic: 2.62 us -> none  [the longest x2 2.21 us: unit_rows(): length = jnp.sqrt(jnp.sum(values * values, axis=1, keepdims=True) + epsilon)]
    slice x3 -> x0, local copies, waits for them, and re-layouts: 2.38 us -> none  [the longest x1 0.88 us: body(): relay_first = hop(share_far[:rows], -1)]
    div x1 -> x0, other arithmetic: 1.33 us -> none  [remove_projection(): (gradient - unit * jnp.sum(unit * gradient, axis=1, keepdims=True)) / length]
  transfers between devices with their start and end apart: 18 -> 18, of which waited for: 5 -> 7; matrix products, arithmetic and copies ran while one was open for 27% -> 0% of each run, Pallas kernels for 0% -> 16%
where the time goes in v2:
time: 52.3 us; the launch traced here: 52.1 us
  starting transfers between devices  21.5 us (41%)
  waiting for transfers between devices  12.4 us (24%)
  Pallas kernels  11.7 us (22%)
  local copies, waits for them, and re-layouts  3.56 us (7%)
  between operations  2.75 us (5%)
    ppermute x18, starting transfers between devices, moved(): return lax.ppermute(value, AXES, pairs)  21.5 us
    ppermute x18, waiting for transfers between devices, moved(): return lax.ppermute(value, AXES, pairs)  12.4 us
    pallas_call x8, Pallas kernels, call(): run(*[pltpu.with_memory_space_constraint(a, pltpu.VMEM) if s is VMEM else...  11.7 us
    unnamed x10, local copies, waits for them, and re-layouts  3.56 us
  transfers between devices with their start and end apart: 18, of which 7 were waited for; matrix products, arithmetic and copies ran while one was open for 0% of the time, Pallas kernels for 16%

profile of v2, /device:TPU:1, one launch (start us, length us, event | category | flops | bytes accessed | tf_op | source)
XLA Modules:
  0.0 52.1 jit_solution(13700808116060715236)
XLA Ops:
  0.7 1.0 %copy-done = bf16[128,1152]{1,0:T(8,128)(2,1)S(1)} copy-done((bf16[128,1152]{1,0:T(8,128)(2,1)S(1)}, bf16[128,1152]{1,0:T(8,128)(2,1)}, u32[]{:S(2)}) %copy-start) | copy-done | bytes 294936
  1.6 1.0 %copy-done.2 = bf16[128,1152]{1,0:T(8,128)(2,1)S(1)} copy-done((bf16[128,1152]{1,0:T(8,128)(2,1)S(1)}, bf16[128,1152]{1,0:T(8,128)(2,1)}, u32[]{:S(2)}) %copy-start.2) | copy-done | bytes 294936
  2.9 3.3 %collective-permute-start = (bf16[128,1152]{1,0:T(8,128)(2,1)S(1)}, bf16[128,1152]{1,0:T(8,128)(2,1)S(1)}, u32[]{:S(2)}, u32[]{:S(2)}) collective-permute-start(bf16[128,1152]{1,0:T(8,128)(2,1)S(1)} %get-tuple-element.18.other), channel_id=1, source_target_pairs={{0,16},{1,17},{2,18},{3,19},{4,20},{5,21},{6,22},{7,23},{8,24},{9,... | collective-permute-start | bytes 884744 | tf_op jit(solution)/shard_map/ppermute | solution.py:28
  6.3 1.0 %collective-permute-start.5 = (bf16[128,1152]{1,0:T(8,128)(2,1)S(1)}, bf16[128,1152]{1,0:T(8,128)(2,1)S(1)}, u32[]{:S(2)}, u32[]{:S(2)}) collective-permute-start(bf16[128,1152]{1,0:T(8,128)(2,1)S(1)} %get-tuple-element.18.other), channel_id=1, source_target_pairs={{0,28},{1,29},{2,30},{3,31},{4,16},{5,17},{6,18},{7,19},{8,20},{9,... | collective-permute-start | bytes 884744 | tf_op jit(solution)/shard_map/ppermute | solution.py:28
  7.3 1.3 %collective-permute-start.2 = (bf16[128,1152]{1,0:T(8,128)(2,1)S(1)}, bf16[128,1152]{1,0:T(8,128)(2,1)S(1)}, u32[]{:S(2)}, u32[]{:S(2)}) collective-permute-start(bf16[128,1152]{1,0:T(8,128)(2,1)S(1)} %get-tuple-element.17.first), channel_id=1, source_target_pairs={{0,1},{1,2},{2,3},{3,0},{4,5},{5,6},{6,7},{7,4},{8,9},{9,10},{10,1... | collective-permute-start | bytes 884744 | tf_op jit(solution)/shard_map/ppermute | solution.py:28
  8.6 1.3 %collective-permute-start.3 = (bf16[128,1152]{1,0:T(8,128)(2,1)S(1)}, bf16[128,1152]{1,0:T(8,128)(2,1)S(1)}, u32[]{:S(2)}, u32[]{:S(2)}) collective-permute-start(bf16[128,1152]{1,0:T(8,128)(2,1)S(1)} %collective-permute-done.second), channel_id=1, source_target_pairs={{0,1},{1,2},{2,3},{3,0},{4,5},{5,6},{6,7},{7,4},{8,9},{9,10},{10,1... | collective-permute-start | bytes 884744 | tf_op jit(solution)/shard_map/ppermute | solution.py:28
  9.9 2.1 %collective-permute-start.4 = (bf16[128,1152]{1,0:T(8,128)(2,1)S(1)}, bf16[128,1152]{1,0:T(8,128)(2,1)S(1)}, u32[]{:S(2)}, u32[]{:S(2)}) collective-permute-start(bf16[128,1152]{1,0:T(8,128)(2,1)S(1)} %collective-permute-done.1.other_second), channel_id=1, source_target_pairs={{0,28},{1,29},{2,30},{3,31},{4,16},{5,17},{6,18},{7,19},{8,20},{9,... | collective-permute-start | bytes 884744 | tf_op jit(solution)/shard_map/ppermute | solution.py:28
  12.7 2.2 %collective-permute-start.9 = (bf16[128,1152]{1,0:T(8,128)(2,1)S(1)}, bf16[128,1152]{1,0:T(8,128)(2,1)S(1)}, u32[]{:S(2)}, u32[]{:S(2)}) collective-permute-start(bf16[128,1152]{1,0:T(8,128)(2,1)S(1)} %collective-permute-done.5.ahead_second), channel_id=1, source_target_pairs={{0,3},{1,0},{2,1},{3,2},{4,7},{5,4},{6,5},{7,6},{8,11},{9,8},{10,9... | collective-permute-start | bytes 884744 | tf_op jit(solution)/shard_map/ppermute | solution.py:28
  15.0 1.0 %collective-permute-start.6 = (bf16[256,1152]{1,0:T(8,128)(2,1)S(1)}, bf16[256,1152]{1,0:T(8,128)(2,1)S(1)}, u32[]{:S(2)}, u32[]{:S(2)}) collective-permute-start(bf16[256,1152]{1,0:T(8,128)(2,1)S(1)} %pad_maximum_fusion), channel_id=1, source_target_pairs={{0,16},{1,17},{2,18},{3,19},{4,20},{5,21},{6,22},{7,23},{8,24},{9,... | collective-permute-start | bytes 1769480 | tf_op jit(solution)/shard_map/ppermute | solution.py:28
  16.0 1.6 %collective-permute-done.3.back_second = bf16[128,1152]{1,0:T(8,128)(2,1)S(1)} collective-permute-done((bf16[128,1152]{1,0:T(8,128)(2,1)S(1)}, bf16[128,1152]{1,0:T(8,128)(2,1)S(1)}, u32[]{:S(2)}, u32[]{:S(2)}) %collective-permute-start.3) | collective-permute-done | bytes 294944 | tf_op jit(solution)/shard_map/ppermute | solution.py:28
  17.7 1.2 %collective-permute-start.7 = (bf16[256,1152]{1,0:T(8,128)(2,1)S(1)}, bf16[256,1152]{1,0:T(8,128)(2,1)S(1)}, u32[]{:S(2)}, u32[]{:S(2)}) collective-permute-start(bf16[256,1152]{1,0:T(8,128)(2,1)S(1)} %pad_maximum_fusion.1), channel_id=1, source_target_pairs={{0,16},{1,17},{2,18},{3,19},{4,20},{5,21},{6,22},{7,23},{8,24},{9,... | collective-permute-start | bytes 1769480 | tf_op jit(solution)/shard_map/ppermute | solution.py:28
  19.5 2.5 %collective-permute-done.8.far_first = bf16[128,1152]{1,0:T(8,128)(2,1)S(1)} collective-permute-done((bf16[128,1152]{1,0:T(8,128)(2,1)S(1)}, bf16[128,1152]{1,0:T(8,128)(2,1)S(1)}, u32[]{:S(2)}, u32[]{:S(2)}) %collective-permute-start.8) | collective-permute-done | bytes 294944 | tf_op jit(solution)/shard_map/ppermute | solution.py:28
  22.1 1.6 %collective-permute-start.10 = (bf16[256,1152]{1,0:T(8,128)(2,1)S(1)}, bf16[256,1152]{1,0:T(8,128)(2,1)S(1)}, u32[]{:S(2)}, u32[]{:S(2)}) collective-permute-start(bf16[256,1152]{1,0:T(8,128)(2,1)S(1)} %pad_maximum_fusion.2), channel_id=1, source_target_pairs={{0,16},{1,17},{2,18},{3,19},{4,20},{5,21},{6,22},{7,23},{8,24},{9,... | collective-permute-start | bytes 1769480 | tf_op jit(solution)/shard_map/ppermute | solution.py:28
  25.8 1.3 %far_weights.1.w_far = bf16[256,768]{1,0:T(8,128)(2,1)S(1)} custom-call(f32[3]{0:T(128)S(1)} %pad_maximum_fusion.3.consts, bf16[128,1152]{1,0:T(8,128)(2,1)S(1)} %collective-permute-done.8.far_first, bf16[128,1152]{1,0:T(8,128)(2,1)S(1)} %collective-permute-done.9.far_second, bf16[128,1152]{1,0:T(8,128)(2,1)S(1)} %get-tuple-element.18.other, ...), custom_call_target="tpu_custom_call" | custom-call | flops 452984832 | bytes 113246 | tf_op jit(solution)/shard_map/far_weights/pallas_call | solution.py:65
  27.1 1.7 %far.1 = (bf16[128,1152]{1,0:T(8,128)(2,1)S(1)}, bf16[128,1152]{1,0:T(8,128)(2,1)S(1)}) custom-call(f32[3]{0:T(128)S(1)} %pad_maximum_fusion.3.consts, bf16[256,768]{1,0:T(8,128)(2,1)S(1)} %far_weights.1.w_far, bf16[128,1152]{1,0:T(8,128)(2,1)S(1)} %collective-permute-done.8.far_first, bf16[128,1152]{1,0:T(8,128)(2,1)S(1)} %collective-permute-done.9.far_second, ...), custom_call_target="tpu_custom_call" | custom-call | flops 754974720 | bytes 188743 | tf_op jit(solution)/shard_map/far/pallas_call | solution.py:65
  28.8 2.3 %collective-permute-start.12 = (bf16[128,1152]{1,0:T(8,128)(2,1)S(1)}, bf16[128,1152]{1,0:T(8,128)(2,1)S(1)}, u32[]{:S(2)}, u32[]{:S(2)}) collective-permute-start(bf16[128,1152]{1,0:T(8,128)(2,1)S(1)} %get-tuple-element.25), channel_id=1, source_target_pairs={{0,3},{1,0},{2,1},{3,2},{4,7},{5,4},{6,5},{7,6},{8,11},{9,8},{10,9... | collective-permute-start | bytes 884744 | tf_op jit(solution)/shard_map/ppermute | solution.py:28
  31.1 2.4 %near.1 = (bf16[256,768]{1,0:T(8,128)(2,1)S(1)}, bf16[256,768]{1,0:T(8,128)(2,1)S(1)}, bf16[256,768]{1,0:T(8,128)(2,1)S(1)}) custom-call(f32[3]{0:T(128)S(1)} %pad_maximum_fusion.3.consts, bf16[128,1152]{1,0:T(8,128)(2,1)S(1)} %get-tuple-element.17.first, bf16[128,1152]{1,0:T(8,128)(2,1)S(1)} %get-tuple-element.18.other, ...), custom_call_target="tpu_custom_call" | custom-call | flops 1358954496 | bytes 339738 | tf_op jit(solution)/shard_map/near/pallas_call | solution.py:65
  33.5 1.7 %own.1 = (f32[128,1152]{1,0:T(8,128)S(1)}, f32[128,1152]{1,0:T(8,128)S(1)}) custom-call(f32[3]{0:T(128)S(1)} %pad_maximum_fusion.3.consts, bf16[256,768]{1,0:T(8,128)(2,1)S(1)} %get-tuple-element.19.w_own, bf16[128,1152]{1,0:T(8,128)(2,1)S(1)} %get-tuple-element.17.first, bf16[128,1152]{1,0:T(8,128)(2,1)S(1)} %collective-permute-done.second, ...), custom_call_target="tpu_custom_call" | custom-call | flops 754974720 | bytes 188743 | tf_op jit(solution)/shard_map/own/pallas_call | solution.py:65
  35.3 3.0 %shares.1 = (f32[128,1152]{1,0:T(8,128)S(1)}, bf16[128,1152]{1,0:T(8,128)(2,1)S(1)}, bf16[128,1152]{1,0:T(8,128)(2,1)S(1)}, f32[128,1152]{1,0:T(8,128)S(1)}) custom-call(f32[3]{0:T(128)S(1)} %pad_maximum_fusion.3.consts, bf16[256,768]{1,0:T(8,128)(2,1)S(1)} %get-tuple-element.21.w_back, bf16[256,768]{1,0:T(8,128)(2,1)S(1)} %get-tuple-element.22.w_ahead, ...), custom_call_target="tpu_custom_call" | custom-call | flops 1509949440 | bytes 377487 | tf_op jit(solution)/shard_map/shares/pallas_call | solution.py:65
  38.9 2.6 %collective-permute-start.16 = (bf16[128,1152]{1,0:T(8,128)(2,1)S(1)}, bf16[128,1152]{1,0:T(8,128)(2,1)S(1)}, u32[]{:S(2)}, u32[]{:S(2)}) collective-permute-start(bf16[128,1152]{1,0:T(8,128)(2,1)S(1)} %get-tuple-element.30), channel_id=1, source_target_pairs={{0,19},{1,16},{2,17},{3,18},{4,23},{5,20},{6,21},{7,22},{8,27},{9,... | collective-permute-start | bytes 884744 | tf_op jit(solution)/shard_map/ppermute | solution.py:28
  42.3 3.1 %collective-permute-done.11.own_one = bf16[128,1152]{1,0:T(8,128)(2,1)S(1)} collective-permute-done((bf16[128,1152]{1,0:T(8,128)(2,1)S(1)}, bf16[128,1152]{1,0:T(8,128)(2,1)S(1)}, u32[]{:S(2)}, u32[]{:S(2)}) %collective-permute-start.11) | collective-permute-done | bytes 294944 | tf_op jit(solution)/shard_map/ppermute | solution.py:28
  45.4 2.9 %collective-permute-done.14.own_two = bf16[128,1152]{1,0:T(8,128)(2,1)S(1)} collective-permute-done((bf16[128,1152]{1,0:T(8,128)(2,1)S(1)}, bf16[128,1152]{1,0:T(8,128)(2,1)S(1)}, u32[]{:S(2)}, u32[]{:S(2)}) %collective-permute-start.14) | collective-permute-done | bytes 294944 | tf_op jit(solution)/shard_map/ppermute | solution.py:28
  48.3 1.0 %collective-permute-done.17.their_two = bf16[128,1152]{1,0:T(8,128)(2,1)S(1)} collective-permute-done((bf16[128,1152]{1,0:T(8,128)(2,1)S(1)}, bf16[128,1152]{1,0:T(8,128)(2,1)S(1)}, u32[]{:S(2)}, u32[]{:S(2)}) %collective-permute-start.17) | collective-permute-done | bytes 294944 | tf_op jit(solution)/shard_map/ppermute | solution.py:28
  49.3 1.2 %last.1 = (f32[128,1152]{1,0:T(8,128)S(1)}, f32[128,1152]{1,0:T(8,128)S(1)}) custom-call(s32[1]{0:T(128)} %bitcast.core, f32[3]{0:T(128)S(1)} %pad_maximum_fusion.3.consts, bf16[128,1152]{1,0:T(8,128)(2,1)S(1)} %copy-done.1, bf16[128,1152]{1,0:T(8,128)(2,1)S(1)} %copy-done.3, f32[128,1152]{1,0:T(8,128)S(1)} %get-tuple-element.20.own, ...), custom_call_target="tpu_custom_call" | custom-call | flops 100000000 | bytes 25000 | tf_op jit(solution)/shard_map/last/pallas_call | solution.py:65
  (34 shorter events, 5.2 us)
Async XLA Ops:
  0.6 1.0 %copy-start = (bf16[128,1152]{1,0:T(8,128)(2,1)S(1)}, bf16[128,1152]{1,0:T(8,128)(2,1)}, u32[]{:S(2)}) copy-start(bf16[128,1152]{1,0:T(8,128)(2,1)} %image.3) | copy-start | bytes 884740
  1.6 1.0 %copy-start.2 = (bf16[128,1152]{1,0:T(8,128)(2,1)S(1)}, bf16[128,1152]{1,0:T(8,128)(2,1)}, u32[]{:S(2)}) copy-start(bf16[128,1152]{1,0:T(8,128)(2,1)} %text.3) | copy-start | bytes 884740
  2.9 5.8 %collective-permute-start = (bf16[128,1152]{1,0:T(8,128)(2,1)S(1)}, bf16[128,1152]{1,0:T(8,128)(2,1)S(1)}, u32[]{:S(2)}, u32[]{:S(2)}) collective-permute-start(bf16[128,1152]{1,0:T(8,128)(2,1)S(1)} %get-tuple-element.18.other), channel_id=1, source_target_pairs={{0,16},{1,17},{2,18},{3,19},{4,20},{5,21},{6,22},{7,23},{8,24},{9,... | collective-permute-start | bytes 884744 | tf_op jit(solution)/shard_map/ppermute | solution.py:28
  6.2 3.7 %collective-permute-start.1 = (bf16[128,1152]{1,0:T(8,128)(2,1)S(1)}, bf16[128,1152]{1,0:T(8,128)(2,1)S(1)}, u32[]{:S(2)}, u32[]{:S(2)}) collective-permute-start(bf16[128,1152]{1,0:T(8,128)(2,1)S(1)} %get-tuple-element.17.first), channel_id=1, source_target_pairs={{0,16},{1,17},{2,18},{3,19},{4,20},{5,21},{6,22},{7,23},{8,24},{9,... | collective-permute-start | bytes 884744 | tf_op jit(solution)/shard_map/ppermute | solution.py:28
  6.3 6.4 %collective-permute-start.5 = (bf16[128,1152]{1,0:T(8,128)(2,1)S(1)}, bf16[128,1152]{1,0:T(8,128)(2,1)S(1)}, u32[]{:S(2)}, u32[]{:S(2)}) collective-permute-start(bf16[128,1152]{1,0:T(8,128)(2,1)S(1)} %get-tuple-element.18.other), channel_id=1, source_target_pairs={{0,28},{1,29},{2,30},{3,31},{4,16},{5,17},{6,18},{7,19},{8,20},{9,... | collective-permute-start | bytes 884744 | tf_op jit(solution)/shard_map/ppermute | solution.py:28
  7.3 7.6 %collective-permute-start.2 = (bf16[128,1152]{1,0:T(8,128)(2,1)S(1)}, bf16[128,1152]{1,0:T(8,128)(2,1)S(1)}, u32[]{:S(2)}, u32[]{:S(2)}) collective-permute-start(bf16[128,1152]{1,0:T(8,128)(2,1)S(1)} %get-tuple-element.17.first), channel_id=1, source_target_pairs={{0,1},{1,2},{2,3},{3,0},{4,5},{5,6},{6,7},{7,4},{8,9},{9,10},{10,1... | collective-permute-start | bytes 884744 | tf_op jit(solution)/shard_map/ppermute | solution.py:28
  8.6 9.0 %collective-permute-start.3 = (bf16[128,1152]{1,0:T(8,128)(2,1)S(1)}, bf16[128,1152]{1,0:T(8,128)(2,1)S(1)}, u32[]{:S(2)}, u32[]{:S(2)}) collective-permute-start(bf16[128,1152]{1,0:T(8,128)(2,1)S(1)} %collective-permute-done.second), channel_id=1, source_target_pairs={{0,1},{1,2},{2,3},{3,0},{4,5},{5,6},{6,7},{7,4},{8,9},{9,10},{10,1... | collective-permute-start | bytes 884744 | tf_op jit(solution)/shard_map/ppermute | solution.py:28
  9.9 7.7 %collective-permute-start.4 = (bf16[128,1152]{1,0:T(8,128)(2,1)S(1)}, bf16[128,1152]{1,0:T(8,128)(2,1)S(1)}, u32[]{:S(2)}, u32[]{:S(2)}) collective-permute-start(bf16[128,1152]{1,0:T(8,128)(2,1)S(1)} %collective-permute-done.1.other_second), channel_id=1, source_target_pairs={{0,28},{1,29},{2,30},{3,31},{4,16},{5,17},{6,18},{7,19},{8,20},{9,... | collective-permute-start | bytes 884744 | tf_op jit(solution)/shard_map/ppermute | solution.py:28
  12.7 6.8 %collective-permute-start.9 = (bf16[128,1152]{1,0:T(8,128)(2,1)S(1)}, bf16[128,1152]{1,0:T(8,128)(2,1)S(1)}, u32[]{:S(2)}, u32[]{:S(2)}) collective-permute-start(bf16[128,1152]{1,0:T(8,128)(2,1)S(1)} %collective-permute-done.5.ahead_second), channel_id=1, source_target_pairs={{0,3},{1,0},{2,1},{3,2},{4,7},{5,4},{6,5},{7,6},{8,11},{9,8},{10,9... | collective-permute-start | bytes 884744 | tf_op jit(solution)/shard_map/ppermute | solution.py:28
  15.0 7.1 %collective-permute-start.8 = (bf16[128,1152]{1,0:T(8,128)(2,1)S(1)}, bf16[128,1152]{1,0:T(8,128)(2,1)S(1)}, u32[]{:S(2)}, u32[]{:S(2)}) collective-permute-start(bf16[128,1152]{1,0:T(8,128)(2,1)S(1)} %collective-permute-done.2.back_first), channel_id=1, source_target_pairs={{0,1},{1,2},{2,3},{3,0},{4,5},{5,6},{6,7},{7,4},{8,9},{9,10},{10,1... | collective-permute-start | bytes 884744 | tf_op jit(solution)/shard_map/ppermute | solution.py:28
  15.0 10.8 %collective-permute-start.6 = (bf16[256,1152]{1,0:T(8,128)(2,1)S(1)}, bf16[256,1152]{1,0:T(8,128)(2,1)S(1)}, u32[]{:S(2)}, u32[]{:S(2)}) collective-permute-start(bf16[256,1152]{1,0:T(8,128)(2,1)S(1)} %pad_maximum_fusion), channel_id=1, source_target_pairs={{0,16},{1,17},{2,18},{3,19},{4,20},{5,21},{6,22},{7,23},{8,24},{9,... | collective-permute-start | bytes 1769480 | tf_op jit(solution)/shard_map/ppermute | solution.py:28
  17.7 8.1 %collective-permute-start.7 = (bf16[256,1152]{1,0:T(8,128)(2,1)S(1)}, bf16[256,1152]{1,0:T(8,128)(2,1)S(1)}, u32[]{:S(2)}, u32[]{:S(2)}) collective-permute-start(bf16[256,1152]{1,0:T(8,128)(2,1)S(1)} %pad_maximum_fusion.1), channel_id=1, source_target_pairs={{0,16},{1,17},{2,18},{3,19},{4,20},{5,21},{6,22},{7,23},{8,24},{9,... | collective-permute-start | bytes 1769480 | tf_op jit(solution)/shard_map/ppermute | solution.py:28
  22.1 5.0 %collective-permute-start.10 = (bf16[256,1152]{1,0:T(8,128)(2,1)S(1)}, bf16[256,1152]{1,0:T(8,128)(2,1)S(1)}, u32[]{:S(2)}, u32[]{:S(2)}) collective-permute-start(bf16[256,1152]{1,0:T(8,128)(2,1)S(1)} %pad_maximum_fusion.2), channel_id=1, source_target_pairs={{0,16},{1,17},{2,18},{3,19},{4,20},{5,21},{6,22},{7,23},{8,24},{9,... | collective-permute-start | bytes 1769480 | tf_op jit(solution)/shard_map/ppermute | solution.py:28
  28.8 12.6 %collective-permute-start.12 = (bf16[128,1152]{1,0:T(8,128)(2,1)S(1)}, bf16[128,1152]{1,0:T(8,128)(2,1)S(1)}, u32[]{:S(2)}, u32[]{:S(2)}) collective-permute-start(bf16[128,1152]{1,0:T(8,128)(2,1)S(1)} %get-tuple-element.25), channel_id=1, source_target_pairs={{0,3},{1,0},{2,1},{3,2},{4,7},{5,4},{6,5},{7,6},{8,11},{9,8},{10,9... | collective-permute-start | bytes 884744 | tf_op jit(solution)/shard_map/ppermute | solution.py:28
  31.1 10.4 %collective-permute-start.13 = (bf16[128,1152]{1,0:T(8,128)(2,1)S(1)}, bf16[128,1152]{1,0:T(8,128)(2,1)S(1)}, u32[]{:S(2)}, u32[]{:S(2)}) collective-permute-start(bf16[128,1152]{1,0:T(8,128)(2,1)S(1)} %get-tuple-element.27), channel_id=1, source_target_pairs={{0,1},{1,2},{2,3},{3,0},{4,5},{5,6},{6,7},{7,4},{8,9},{9,10},{10,1... | collective-permute-start | bytes 884744 | tf_op jit(solution)/shard_map/ppermute | solution.py:28
  35.2 14.1 %collective-permute-start.15 = (f32[128,1152]{1,0:T(8,128)S(1)}, f32[128,1152]{1,0:T(8,128)S(1)}, u32[]{:S(2)}, u32[]{:S(2)}) collective-permute-start(f32[128,1152]{1,0:T(8,128)S(1)} %get-tuple-element.29), channel_id=1, source_target_pairs={{0,16},{1,17},{2,18},{3,19},{4,20},{5,21},{6,22},{7,23},{8,24},{9,... | collective-permute-start | bytes 1769480 | tf_op jit(solution)/shard_map/ppermute | solution.py:28
  38.2 7.2 %collective-permute-start.11 = (bf16[128,1152]{1,0:T(8,128)(2,1)S(1)}, bf16[128,1152]{1,0:T(8,128)(2,1)S(1)}, u32[]{:S(2)}, u32[]{:S(2)}) collective-permute-start(bf16[128,1152]{1,0:T(8,128)(2,1)S(1)} %get-tuple-element.23), channel_id=1, source_target_pairs={{0,1},{1,2},{2,3},{3,0},{4,5},{5,6},{6,7},{7,4},{8,9},{9,10},{10,1... | collective-permute-start | bytes 884744 | tf_op jit(solution)/shard_map/ppermute | solution.py:28
  38.9 6.5 %collective-permute-start.16 = (bf16[128,1152]{1,0:T(8,128)(2,1)S(1)}, bf16[128,1152]{1,0:T(8,128)(2,1)S(1)}, u32[]{:S(2)}, u32[]{:S(2)}) collective-permute-start(bf16[128,1152]{1,0:T(8,128)(2,1)S(1)} %get-tuple-element.30), channel_id=1, source_target_pairs={{0,19},{1,16},{2,17},{3,18},{4,23},{5,20},{6,21},{7,22},{8,27},{9,... | collective-permute-start | bytes 884744 | tf_op jit(solution)/shard_map/ppermute | solution.py:28
  41.5 7.8 %copy-start.1 = (bf16[128,1152]{1,0:T(8,128)(2,1)S(1)}, bf16[128,1152]{1,0:T(8,128)(2,1)}, u32[]{:S(2)}) copy-start(bf16[128,1152]{1,0:T(8,128)(2,1)} %image.3) | copy-start | bytes 884740
  41.5 7.8 %copy-start.3 = (bf16[128,1152]{1,0:T(8,128)(2,1)S(1)}, bf16[128,1152]{1,0:T(8,128)(2,1)}, u32[]{:S(2)}) copy-start(bf16[128,1152]{1,0:T(8,128)(2,1)} %text.3) | copy-start | bytes 884740
  41.6 6.7 %collective-permute-start.14 = (bf16[128,1152]{1,0:T(8,128)(2,1)S(1)}, bf16[128,1152]{1,0:T(8,128)(2,1)S(1)}, u32[]{:S(2)}, u32[]{:S(2)}) collective-permute-start(bf16[128,1152]{1,0:T(8,128)(2,1)S(1)} %get-tuple-element.28), channel_id=1, source_target_pairs={{0,3},{1,0},{2,1},{3,2},{4,7},{5,4},{6,5},{7,6},{8,11},{9,8},{10,9... | collective-permute-start | bytes 884744 | tf_op jit(solution)/shard_map/ppermute | solution.py:28
  41.7 7.5 %collective-permute-start.17 = (bf16[128,1152]{1,0:T(8,128)(2,1)S(1)}, bf16[128,1152]{1,0:T(8,128)(2,1)S(1)}, u32[]{:S(2)}, u32[]{:S(2)}) collective-permute-start(bf16[128,1152]{1,0:T(8,128)(2,1)S(1)} %get-tuple-element.31), channel_id=1, source_target_pairs={{0,17},{1,18},{2,19},{3,16},{4,21},{5,22},{6,23},{7,20},{8,25},{9,... | collective-permute-start | bytes 884744 | tf_op jit(solution)/shard_map/ppermute | solution.py:28

commit v3 on v2

v3 whole, which is shorter than its diff:
```python
import math

import jax
import jax.numpy as jnp
from jax import lax
from jax.experimental import pallas as pl
from jax.experimental.pallas import tpu as pltpu
from jax.sharding import PartitionSpec as P

epsilon = 1e-06
AXES = ("grp", "ing")
SIDE = 4
VMEM_BYTES = 16 * 1024 * 1024
VMEM = pl.BlockSpec(memory_space=pltpu.VMEM)
SMEM = pl.BlockSpec(memory_space=pltpu.SMEM)
HBM = pl.BlockSpec(memory_space=pl.ANY)


def moved(value, step, core_change=0, ring_change=0):
    size = SIDE * SIDE
    pairs = []
    for grp in range(lax.axis_size("grp")):
        target = grp ^ core_change
        for ing in range(size):
            y, x = divmod(ing, SIDE)
            if (grp ^ ring_change) % 2:
                y = (y + step) % SIDE
            else:
                x = (x + step) % SIDE
            pairs.append((grp * size + ing, target * size + y * SIDE + x))
    return lax.ppermute(value, AXES, pairs)


def hop(value, step):
    return moved(value, step)


def cross(value, step):
    return moved(value, step, 1, 1)


def cross_back(value, step):
    return moved(value, step, 1, 0)


def swap(value):
    return moved(value, 0, 1)


def dot_t(left, right):
    return lax.dot_general(left, right, (((1,), (1,)), ((), ())), preferred_element_type=jnp.float32)


def dot(left, right):
    return jnp.dot(left, right, preferred_element_type=jnp.float32)


def call(kernel, outs, specs, flops, name, out_specs=None, scratch=()):
    out_specs = out_specs or [VMEM] * len(outs)
    run = pl.pallas_call(
        kernel,
        out_shape=[pltpu.VMEM(o.shape, o.dtype) if s is VMEM else o for o, s in zip(outs, out_specs)],
        in_specs=specs,
        out_specs=out_specs,
        scratch_shapes=scratch,
        cost_estimate=pl.CostEstimate(flops=flops, bytes_accessed=1, transcendentals=0),
        compiler_params=pltpu.CompilerParams(vmem_limit_bytes=VMEM_BYTES),
        name=name,
    )
    return lambda *args: run(
        *[
            pltpu.with_memory_space_constraint(a, pltpu.VMEM if s is VMEM else pltpu.HBM) if s is not SMEM else a
            for a, s in zip(args, specs)
        ]
    )


def unit_rows(matrix):
    values = matrix.astype(jnp.float32)
    length = jnp.sqrt(jnp.sum(values * values, axis=1, keepdims=True) + epsilon)
    return (values / length, length)


def rows_kernel(core, image, text, first, other, raw_first, raw_other, sems):

    @pl.when(core[0] == 0)
    def _():
        pltpu.make_async_copy(image, raw_first, sems.at[0]).start()
        pltpu.make_async_copy(text, raw_other, sems.at[1]).start()

    @pl.when(core[0] != 0)
    def _():
        pltpu.make_async_copy(text, raw_first, sems.at[0]).start()
        pltpu.make_async_copy(image, raw_other, sems.at[1]).start()

    pltpu.make_async_copy(image, raw_first, sems.at[0]).wait()
    first[...] = unit_rows(raw_first[...])[0].astype(jnp.bfloat16)
    pltpu.make_async_copy(text, raw_other, sems.at[1]).wait()
    other[...] = unit_rows(raw_other[...])[0].astype(jnp.bfloat16)


def consts_kernel(numbers, after, consts):
    scale = jnp.exp(numbers[0:8])
    consts[0:8] = scale
    consts[8:16] = scale * (-math.log2(math.e))
    consts[16:24] = numbers[8:16] * (-math.log2(math.e))
    consts[24:32] = numbers[16:24] / (2 * after.shape[0] * SIDE * SIDE)


def negative(cosine, consts):
    power = cosine * consts[8:9, 0:1] + consts[16:17, 0:1]
    return (consts[24:25, 0:1] / (1.0 + jnp.exp2(power))).astype(jnp.bfloat16)


def positive(cosine, consts):
    power = cosine * consts[8:9, 0:1] + consts[16:17, 0:1]
    return (-consts[24:25, 0:1] / (1.0 + jnp.exp2(-power))).astype(jnp.bfloat16)


def joined(up, down):
    return jnp.concatenate([up[...], down[...]], 0)


def near_kernel(consts, first, second, back_first, ahead_second, other, other_second, near_others, part_own,
                part_back_first, part_ahead_second):
    rows = first.shape[0]
    left = jnp.concatenate([first[...], second[...], back_first[...], ahead_second[...]], 0)
    right = joined(other, other_second)
    cosine = dot_t(left, right)
    weights = negative(cosine, consts)
    pairs = cosine[: 2 * rows]
    i = lax.broadcasted_iota(jnp.int32, pairs.shape, 0)
    j = lax.broadcasted_iota(jnp.int32, pairs.shape, 1)
    own = jnp.where(i == j, positive(pairs, consts), weights[: 2 * rows])
    total = dot(jnp.concatenate([own, weights[2 * rows :]], 0), right)
    total += dot(negative(dot_t(left, near_others[...]), consts), near_others[...])
    part_own[...] = total[: 2 * rows]
    part_back_first[...] = total[2 * rows : 3 * rows]
    part_ahead_second[...] = total[3 * rows :]


def second_kernel(consts, back_second, ahead_first, other, other_second, near_others, part_back_second,
                  part_ahead_first):
    rows = back_second.shape[0]
    left = joined(back_second, ahead_first)
    right = joined(other, other_second)
    total = dot(negative(dot_t(left, right), consts), right)
    total += dot(negative(dot_t(left, near_others[...]), consts), near_others[...])
    part_back_second[...] = total[:rows]
    part_ahead_first[...] = total[rows:]


def far_near_kernel(consts, far_first, far_second, other, other_second, near_others, late_others, part):
    left = joined(far_first, far_second)
    right = joined(other, other_second)
    total = dot(negative(dot_t(left, right), consts), right)
    for others in (near_others, late_others):
        total += dot(negative(dot_t(left, others[...]), consts), others[...])
    part[...] = total


def far_kernel(consts, part, far_first, far_second, far_others_first, far_others_second, share_first, share_second):
    rows = far_first.shape[0]
    others = joined(far_others_first, far_others_second)
    weights = negative(dot_t(joined(far_first, far_second), others), consts)
    total = part[...] + dot(weights, others)
    share_first[...] = total[:rows].astype(jnp.bfloat16)
    share_second[...] = total[rows:].astype(jnp.bfloat16)


def rest_kernel(consts, part_own, part_back_first, part_back_second, part_ahead_first, part_ahead_second, first, second,
                back_first, back_second, ahead_first, ahead_second, late_others, far_others_first, far_others_second,
                after, own_first, own_second, out_back_first, out_back_second, out_ahead_first, out_ahead_second):
    rows = first.shape[0]
    late = late_others[...]
    far_others = joined(far_others_first, far_others_second)
    for up, down, part, out_up, out_down in (
        (back_first, back_second, (part_back_first, part_back_second), out_back_first, out_back_second),
        (ahead_first, ahead_second, (part_ahead_first, part_ahead_second), out_ahead_first, out_ahead_second),
        (first, second, (part_own,), own_first, own_second),
    ):
        left = joined(up, down)
        total = dot(negative(dot_t(left, late), consts), late)
        total += dot(negative(dot_t(left, far_others), consts), far_others)
        total += joined(*part) if len(part) > 1 else part[0][...]
        out_up[...] = total[:rows].astype(out_up.dtype)
        out_down[...] = total[rows:].astype(out_down.dtype)


def relay_kernel(up, up_got, down, down_got, up_out, down_out):
    up_out[...] = (up[...] + up_got[...].astype(jnp.float32)).astype(jnp.bfloat16)
    down_out[...] = (down[...] + down_got[...].astype(jnp.float32)).astype(jnp.bfloat16)


def last_kernel(core, consts, raw_first, raw_other, own, own_one, own_two, their, their_one, their_two,
                image_out, text_out, own_grad, their_grad, sems):
    rows = own.shape[0]
    parts = sems.shape[1]
    block = rows // parts
    scale = consts[0:1, 0:1]
    for part in range(parts):
        at = pl.ds(part * block, block)
        for kind, (raw, mine, one, two, grad) in enumerate((
            (raw_first, own, own_one, own_two, own_grad),
            (raw_other, their, their_one, their_two, their_grad),
        )):
            direction = scale * (mine[at] + one[at].astype(jnp.float32) + two[at].astype(jnp.float32))
            unit, length = unit_rows(raw[at])
            grad[at] = (direction - unit * jnp.sum(unit * direction, axis=1, keepdims=True)) / length
            sem = sems.at[kind, part]
            for value, out in ((0, (image_out, text_out)[kind]), (1, (text_out, image_out)[kind])):

                @pl.when(core[0] == value)
                def _(grad=grad, out=out, at=at, sem=sem):
                    pltpu.make_async_copy(grad.at[at], out.at[at], sem).start()

    for part in range(parts):
        at = pl.ds(part * block, block)
        pltpu.make_async_copy(own_grad.at[at], image_out.at[at], sems.at[0, part]).wait()
        pltpu.make_async_copy(their_grad.at[at], text_out.at[at], sems.at[1, part]).wait()


def gate_kernel(value, after, out):
    pass


def gate(value, after):
    return pl.pallas_call(
        gate_kernel,
        out_shape=pltpu.VMEM(value.shape, value.dtype),
        in_specs=[VMEM, VMEM],
        out_specs=VMEM,
        input_output_aliases={0: 0},
        cost_estimate=pl.CostEstimate(flops=1, bytes_accessed=1, transcendentals=0),
        compiler_params=pltpu.CompilerParams(vmem_limit_bytes=VMEM_BYTES),
        name="gate",
    )(pltpu.with_memory_space_constraint(value, pltpu.VMEM), pltpu.with_memory_space_constraint(after, pltpu.VMEM))


def pair_kernel(up, down, after, out):
    rows = up.shape[0]
    out[:rows] = up[...]
    out[rows:] = down[...]


def body(image_embed, text_embed, scale_logarithm, logit_bias, loss_grad):
    rows, width = image_embed.shape
    half = jax.ShapeDtypeStruct((rows, width), jnp.bfloat16)
    full = jax.ShapeDtypeStruct((rows, width), jnp.float32)
    double = jax.ShapeDtypeStruct((2 * rows, width), jnp.float32)
    core = (lax.axis_index("grp") % 2).astype(jnp.int32).reshape(1)
    numbers = jnp.concatenate(
        [jnp.broadcast_to(value, (8, 128)) for value in (scale_logarithm, logit_bias, loss_grad)], 0
    )
    unit = 2 * rows * rows * width

    first, other, raw_first, raw_other = call(
        rows_kernel,
        [half, half, half, half],
        [SMEM, HBM, HBM],
        10**8,
        "rows",
        scratch=[pltpu.SemaphoreType.DMA((2,))],
    )(core, image_embed, text_embed)

    back_first = hop(first, 1)
    ahead_second = cross(other, -1)
    other_second = swap(first)
    second = swap(other)
    (consts,) = call(consts_kernel, [jax.ShapeDtypeStruct((32, 128), jnp.float32)], [VMEM] * 2, 1, "consts")(
        numbers, second
    )
    back_second = hop(second, 1)
    ahead_first = cross(other_second, -1)
    far_first = hop(back_first, 1)
    far_second = hop(ahead_second, -1)
    (near,) = call(pair_kernel, [jax.ShapeDtypeStruct((2 * rows, width), jnp.bfloat16)], [VMEM] * 3, 1, "pair")(
        back_first, ahead_second, consts
    )
    near_others = swap(near)
    late_others = swap(jnp.concatenate([back_second, ahead_first], 0))
    part_own, part_back_first, part_ahead_second = call(near_kernel, [double, full, full], [VMEM] * 8, 1, "near")(
        consts, first, second, back_first, ahead_second, other, other_second, near_others
    )
    part_back_second, part_ahead_first = call(second_kernel, [full] * 2, [VMEM] * 6, 1, "second")(
        consts, back_second, ahead_first, other, other_second, near_others
    )
    far_first = gate(far_first, part_back_second)
    far_second = gate(far_second, part_own)
    far_others_first = swap(far_first)
    far_others_second = swap(far_second)
    (part_far,) = call(far_near_kernel, [double], [VMEM] * 7, 1, "far_near")(
        consts, far_first, far_second, other, other_second, near_others, late_others
    )
    share_first, share_second = call(far_kernel, [half, half], [VMEM] * 6, 8 * unit, "far")(
        consts, part_far, far_first, far_second, far_others_first, far_others_second
    )

    relay_first = hop(share_first, -1)
    relay_second = hop(share_second, 1)
    own_first, own_second, keep_back_first, share_back_second, share_ahead_first, keep_ahead_second = call(
        rest_kernel, [full, full, full, half, half, full], [VMEM] * 16, 40 * unit, "rest"
    )(
        consts, part_own, part_back_first, part_back_second, part_ahead_first, part_ahead_second, first, second,
        back_first, back_second, ahead_first, ahead_second, late_others, far_others_first, far_others_second, share_first,
    )
    their_one = cross_back(share_back_second, -1)
    own_one = hop(share_ahead_first, 1)
    their_second = swap(own_second)
    send_first, send_second = call(relay_kernel, [half, half], [VMEM] * 4, 10**7, "relay")(
        keep_back_first, relay_first, keep_ahead_second, relay_second
    )
    own_two = hop(send_first, -1)
    their_two = cross_back(send_second, 1)
    image_gradient, text_gradient = call(
        last_kernel,
        [full, full],
        [SMEM] + [VMEM] * 9,
        10**8,
        "last",
        out_specs=[HBM] * 2,
        scratch=[
            pltpu.VMEM((rows, width), jnp.float32),
            pltpu.VMEM((rows, width), jnp.float32),
            pltpu.SemaphoreType.DMA((2, 4)),
        ],
    )(core, consts, raw_first, raw_other, own_first, own_one, own_two, their_second, their_one, their_two)
    return (image_gradient, text_gradient)


def solution(mesh):
    placed = (P(AXES, None), P(AXES, None), P(), P(), P())
    return jax.shard_map(
        body,
        mesh=mesh,
        in_specs=placed,
        out_specs=(P(AXES, None), P(AXES, None)),
        check_vma=False,
    )
```

time: 52.3 us -> 46.3 us (0.89)
  local copies, waits for them, and re-layouts: 3.56 us -> 0.08 us
  waiting for transfers between devices: 12.4 us -> 9.12 us
  starting transfers between devices: 21.5 us -> 22.6 us
    unnamed x10 -> x0, local copies, waits for them, and re-layouts: 3.56 us -> none
    ppermute x18 -> x19, waiting for transfers between devices: 12.4 us -> 9.12 us  [moved(): return lax.ppermute(value, AXES, pairs)]
    ppermute x18 -> x19, starting transfers between devices: 21.5 us -> 22.6 us  [moved(): return lax.ppermute(value, AXES, pairs)]
    pallas_call x8 -> x12, Pallas kernels: 11.7 us -> 11.3 us  [the longest x10 11.3 us: call(): run(*[pltpu.with_memory_space_constraint(a, pltpu.VMEM if s is VMEM else...]
  transfers between devices with their start and end apart: 18 -> 19, of which waited for: 7 -> 5; matrix products, arithmetic and copies ran while one was open for 0% -> 0% of each run, Pallas kernels for 16% -> 16%
where the time goes in v3:
time: 46.3 us; the launch traced here: 46.2 us
  starting transfers between devices  22.6 us (49%)
  Pallas kernels  11.3 us (24%)
  waiting for transfers between devices  9.12 us (20%)
  between operations  2.9 us (6%)
    ppermute x19, starting transfers between devices, moved(): return lax.ppermute(value, AXES, pairs)  22.6 us
    pallas_call x10, Pallas kernels, call(): run(*[pltpu.with_memory_space_constraint(a, pltpu.VMEM if s is VMEM else...  11.3 us
    ppermute x19, waiting for transfers between devices, moved(): return lax.ppermute(value, AXES, pairs)  9.12 us
  transfers between devices with their start and end apart: 19, of which 5 were waited for; matrix products, arithmetic and copies ran while one was open for 0% of the time, Pallas kernels for 16%

profile of v3, /device:TPU:1, one launch (start us, length us, event | category | flops | bytes accessed | tf_op | source)
XLA Modules:
  0.0 46.2 jit_solution(18018874667244036618)
XLA Ops:
  0.6 1.3 %rows.1 = (bf16[128,1152]{1,0:T(8,128)(2,1)S(1)}, bf16[128,1152]{1,0:T(8,128)(2,1)S(1)}, bf16[128,1152]{1,0:T(8,128)(2,1)S(1)}, bf16[128,1152]{1,0:T(8,128)(2,1)S(1)}) custom-call(s32[1]{0:T(128)} %bitcast.core, bf16[128,1152]{1,0:T(8,128)(2,1)} %image.1, bf16[128,1152]{1,0:T(8,128)(2,1)} %text.1), custom_call_target="tpu_custom_call" | custom-call | flops 100000000 | bytes 1 | tf_op jit(solution)/shard_map/rows/pallas_call | solution.py:70
  1.9 3.3 %collective-permute-start.3 = (bf16[128,1152]{1,0:T(8,128)(2,1)S(1)}, bf16[128,1152]{1,0:T(8,128)(2,1)S(1)}, u32[]{:S(2)}, u32[]{:S(2)}) collective-permute-start(bf16[128,1152]{1,0:T(8,128)(2,1)S(1)} %get-tuple-element.24.first), channel_id=1, source_target_pairs={{0,16},{1,17},{2,18},{3,19},{4,20},{5,21},{6,22},{7,23},{8,24},{9,... | collective-permute-start | bytes 884744 | tf_op jit(solution)/shard_map/ppermute | solution.py:31
  5.4 3.2 %collective-permute-start.2 = (bf16[128,1152]{1,0:T(8,128)(2,1)S(1)}, bf16[128,1152]{1,0:T(8,128)(2,1)S(1)}, u32[]{:S(2)}, u32[]{:S(2)}) collective-permute-start(bf16[128,1152]{1,0:T(8,128)(2,1)S(1)} %get-tuple-element.21.other), channel_id=1, source_target_pairs={{0,28},{1,29},{2,30},{3,31},{4,16},{5,17},{6,18},{7,19},{8,20},{9,... | collective-permute-start | bytes 884744 | tf_op jit(solution)/shard_map/ppermute | solution.py:31
  8.6 0.5 %collective-permute-start.6 = (bf16[128,1152]{1,0:T(8,128)(2,1)S(1)}, bf16[128,1152]{1,0:T(8,128)(2,1)S(1)}, u32[]{:S(2)}, u32[]{:S(2)}) collective-permute-start(bf16[128,1152]{1,0:T(8,128)(2,1)S(1)} %collective-permute-done.3.other_second), channel_id=1, source_target_pairs={{0,28},{1,29},{2,30},{3,31},{4,16},{5,17},{6,18},{7,19},{8,20},{9,... | collective-permute-start | bytes 884744 | tf_op jit(solution)/shard_map/ppermute | solution.py:31
  11.3 1.1 %collective-permute-done.1.up.back_first = bf16[128,1152]{1,0:T(8,128)(2,1)S(1)} collective-permute-done((bf16[128,1152]{1,0:T(8,128)(2,1)S(1)}, bf16[128,1152]{1,0:T(8,128)(2,1)S(1)}, u32[]{:S(2)}, u32[]{:S(2)}) %collective-permute-start.1) | collective-permute-done | bytes 294944 | tf_op jit(solution)/shard_map/ppermute | solution.py:31
  12.5 1.4 %collective-permute-start.4 = (bf16[256,1152]{1,0:T(8,128)(2,1)S(1)}, bf16[256,1152]{1,0:T(8,128)(2,1)S(1)}, u32[]{:S(2)}, u32[]{:S(2)}) collective-permute-start(bf16[256,1152]{1,0:T(8,128)(2,1)S(1)} %pair.1), channel_id=1, source_target_pairs={{0,16},{1,17},{2,18},{3,19},{4,20},{5,21},{6,22},{7,23},{8,24},{9,... | collective-permute-start | bytes 1769480 | tf_op jit(solution)/shard_map/ppermute | solution.py:31
  13.9 2.7 %collective-permute-start.10 = (bf16[128,1152]{1,0:T(8,128)(2,1)S(1)}, bf16[128,1152]{1,0:T(8,128)(2,1)S(1)}, u32[]{:S(2)}, u32[]{:S(2)}) collective-permute-start(bf16[128,1152]{1,0:T(8,128)(2,1)S(1)} %collective-permute-done.2.down.ahead_second), channel_id=1, source_target_pairs={{0,3},{1,0},{2,1},{3,2},{4,7},{5,4},{6,5},{7,6},{8,11},{9,8},{10,9... | collective-permute-start | bytes 884744 | tf_op jit(solution)/shard_map/ppermute | solution.py:31
  16.6 1.5 %collective-permute-start.7 = (bf16[256,1152]{1,0:T(8,128)(2,1)S(1)}, bf16[256,1152]{1,0:T(8,128)(2,1)S(1)}, u32[]{:S(2)}, u32[]{:S(2)}) collective-permute-start(bf16[256,1152]{1,0:T(8,128)(2,1)S(1)} %pad_maximum_fusion), channel_id=1, source_target_pairs={{0,16},{1,17},{2,18},{3,19},{4,20},{5,21},{6,22},{7,23},{8,24},{9,... | collective-permute-start | bytes 1769480 | tf_op jit(solution)/shard_map/ppermute | solution.py:31
  18.1 1.0 %second.1 = (f32[128,1152]{1,0:T(8,128)S(1)}, f32[128,1152]{1,0:T(8,128)S(1)}) custom-call(f32[32,128]{1,0:T(8,128)S(1)} %consts.1.after, bf16[128,1152]{1,0:T(8,128)(2,1)S(1)} %collective-permute-done.5.back_second, bf16[128,1152]{1,0:T(8,128)(2,1)S(1)} %collective-permute-done.6.ahead_first, bf16[128,1152]{1,0:T(8,128)(2,1)S(1)} %get-tuple-element.21.other, ...), custom_call_target="tpu_custom_call" | custom-call | flops 1 | bytes 1 | tf_op jit(solution)/shard_map/second/pallas_call | solution.py:70
  19.1 1.8 %collective-permute-done.8.value = bf16[128,1152]{1,0:T(8,128)(2,1)S(1)} collective-permute-done((bf16[128,1152]{1,0:T(8,128)(2,1)S(1)}, bf16[128,1152]{1,0:T(8,128)(2,1)S(1)}, u32[]{:S(2)}, u32[]{:S(2)}) %collective-permute-start.8) | collective-permute-done | bytes 294944 | tf_op jit(solution)/shard_map/ppermute | solution.py:31
  20.9 0.9 %collective-permute-start.9 = (bf16[128,1152]{1,0:T(8,128)(2,1)S(1)}, bf16[128,1152]{1,0:T(8,128)(2,1)S(1)}, u32[]{:S(2)}, u32[]{:S(2)}) collective-permute-start(bf16[128,1152]{1,0:T(8,128)(2,1)S(1)} %gate.2.far_first), channel_id=1, source_target_pairs={{0,16},{1,17},{2,18},{3,19},{4,20},{5,21},{6,22},{7,23},{8,24},{9,... | collective-permute-start | bytes 884744 | tf_op jit(solution)/shard_map/ppermute | solution.py:31
  21.9 1.8 %near.1 = (f32[256,1152]{1,0:T(8,128)S(1)}, f32[128,1152]{1,0:T(8,128)S(1)}, f32[128,1152]{1,0:T(8,128)S(1)}) custom-call(f32[32,128]{1,0:T(8,128)S(1)} %consts.1.after, bf16[128,1152]{1,0:T(8,128)(2,1)S(1)} %get-tuple-element.24.first, bf16[128,1152]{1,0:T(8,128)(2,1)S(1)} %collective-permute-done.after.second, ...), custom_call_target="tpu_custom_call" | custom-call | flops 1 | bytes 1 | tf_op jit(solution)/shard_map/near/pallas_call | solution.py:70
  24.0 1.8 %far_near.1.part = f32[256,1152]{1,0:T(8,128)S(1)} custom-call(f32[32,128]{1,0:T(8,128)S(1)} %consts.1.after, bf16[128,1152]{1,0:T(8,128)(2,1)S(1)} %gate.2.far_first, bf16[128,1152]{1,0:T(8,128)(2,1)S(1)} %gate.3.far_second, bf16[128,1152]{1,0:T(8,128)(2,1)S(1)} %get-tuple-element.21.other, bf16[128,1152]{1,0:T(8,128)(2,1)S(1)} %collective-permute-done.3.other_second, ...), custom_call_target="tpu_custom_call" | custom-call | flops 1 | bytes 1 | tf_op jit(solution)/shard_map/far_near/pallas_call | solution.py:70
  25.8 0.9 %far.1 = (bf16[128,1152]{1,0:T(8,128)(2,1)S(1)}, bf16[128,1152]{1,0:T(8,128)(2,1)S(1)}) custom-call(f32[32,128]{1,0:T(8,128)S(1)} %consts.1.after, f32[256,1152]{1,0:T(8,128)S(1)} %far_near.1.part, bf16[128,1152]{1,0:T(8,128)(2,1)S(1)} %gate.2.far_first, bf16[128,1152]{1,0:T(8,128)(2,1)S(1)} %gate.3.far_second, ...), custom_call_target="tpu_custom_call" | custom-call | flops 301989888 | bytes 1 | tf_op jit(solution)/shard_map/far/pallas_call | solution.py:70
  26.9 2.7 %collective-permute-start.13 = (bf16[128,1152]{1,0:T(8,128)(2,1)S(1)}, bf16[128,1152]{1,0:T(8,128)(2,1)S(1)}, u32[]{:S(2)}, u32[]{:S(2)}) collective-permute-start(bf16[128,1152]{1,0:T(8,128)(2,1)S(1)} %get-tuple-element.30.after), channel_id=1, source_target_pairs={{0,3},{1,0},{2,1},{3,2},{4,7},{5,4},{6,5},{7,6},{8,11},{9,8},{10,9... | collective-permute-start | bytes 884744 | tf_op jit(solution)/shard_map/ppermute | solution.py:31
  29.5 2.7 %rest.1 = (f32[128,1152]{1,0:T(8,128)S(1)}, f32[128,1152]{1,0:T(8,128)S(1)}, f32[128,1152]{1,0:T(8,128)S(1)}, bf16[128,1152]{1,0:T(8,128)(2,1)S(1)}, bf16[128,11...) custom-call(f32[32,128]{1,0:T(8,128)S(1)} %consts.1.after, f32[256,1152]{1,0:T(8,128)S(1)} %get-tuple-element.25.after.part_own, ...), custom_call_target="tpu_custom_call" | custom-call | flops 1509949440 | bytes 1 | tf_op jit(solution)/shard_map/rest/pallas_call | solution.py:70
  32.3 1.1 %collective-permute-start.16 = (f32[128,1152]{1,0:T(8,128)S(1)}, f32[128,1152]{1,0:T(8,128)S(1)}, u32[]{:S(2)}, u32[]{:S(2)}) collective-permute-start(f32[128,1152]{1,0:T(8,128)S(1)} %get-tuple-element.37), channel_id=1, source_target_pairs={{0,16},{1,17},{2,18},{3,19},{4,20},{5,21},{6,22},{7,23},{8,24},{9,... | collective-permute-start | bytes 1769480 | tf_op jit(solution)/shard_map/ppermute | solution.py:31
  33.4 2.5 %collective-permute-start.17 = (bf16[128,1152]{1,0:T(8,128)(2,1)S(1)}, bf16[128,1152]{1,0:T(8,128)(2,1)S(1)}, u32[]{:S(2)}, u32[]{:S(2)}) collective-permute-start(bf16[128,1152]{1,0:T(8,128)(2,1)S(1)} %get-tuple-element.38), channel_id=1, source_target_pairs={{0,19},{1,16},{2,17},{3,18},{4,23},{5,20},{6,21},{7,22},{8,27},{9,... | collective-permute-start | bytes 884744 | tf_op jit(solution)/shard_map/ppermute | solution.py:31
  36.0 0.8 %collective-permute-start.15 = (bf16[128,1152]{1,0:T(8,128)(2,1)S(1)}, bf16[128,1152]{1,0:T(8,128)(2,1)S(1)}, u32[]{:S(2)}, u32[]{:S(2)}) collective-permute-start(bf16[128,1152]{1,0:T(8,128)(2,1)S(1)} %get-tuple-element.36), channel_id=1, source_target_pairs={{0,3},{1,0},{2,1},{3,2},{4,7},{5,4},{6,5},{7,6},{8,11},{9,8},{10,9... | collective-permute-start | bytes 884744 | tf_op jit(solution)/shard_map/ppermute | solution.py:31
  36.8 1.5 %collective-permute-start.18 = (bf16[128,1152]{1,0:T(8,128)(2,1)S(1)}, bf16[128,1152]{1,0:T(8,128)(2,1)S(1)}, u32[]{:S(2)}, u32[]{:S(2)}) collective-permute-start(bf16[128,1152]{1,0:T(8,128)(2,1)S(1)} %get-tuple-element.39), channel_id=1, source_target_pairs={{0,17},{1,18},{2,19},{3,16},{4,21},{5,22},{6,23},{7,20},{8,25},{9,... | collective-permute-start | bytes 884744 | tf_op jit(solution)/shard_map/ppermute | solution.py:31
  38.3 2.2 %collective-permute-done.12.own_one = bf16[128,1152]{1,0:T(8,128)(2,1)S(1)} collective-permute-done((bf16[128,1152]{1,0:T(8,128)(2,1)S(1)}, bf16[128,1152]{1,0:T(8,128)(2,1)S(1)}, u32[]{:S(2)}, u32[]{:S(2)}) %collective-permute-start.12) | collective-permute-done | bytes 294944 | tf_op jit(solution)/shard_map/ppermute | solution.py:31
  40.5 2.2 %collective-permute-done.15.own_two = bf16[128,1152]{1,0:T(8,128)(2,1)S(1)} collective-permute-done((bf16[128,1152]{1,0:T(8,128)(2,1)S(1)}, bf16[128,1152]{1,0:T(8,128)(2,1)S(1)}, u32[]{:S(2)}, u32[]{:S(2)}) %collective-permute-start.15) | collective-permute-done | bytes 294944 | tf_op jit(solution)/shard_map/ppermute | solution.py:31
  42.7 1.8 %collective-permute-done.18.their_two = bf16[128,1152]{1,0:T(8,128)(2,1)S(1)} collective-permute-done((bf16[128,1152]{1,0:T(8,128)(2,1)S(1)}, bf16[128,1152]{1,0:T(8,128)(2,1)S(1)}, u32[]{:S(2)}, u32[]{:S(2)}) %collective-permute-start.18) | collective-permute-done | bytes 294944 | tf_op jit(solution)/shard_map/ppermute | solution.py:31
  44.5 1.6 %last.1 = (f32[128,1152]{1,0:T(8,128)}, f32[128,1152]{1,0:T(8,128)}) custom-call(s32[1]{0:T(128)} %bitcast.core, f32[32,128]{1,0:T(8,128)S(1)} %consts.1.after, bf16[128,1152]{1,0:T(8,128)(2,1)S(1)} %get-tuple-element.22.raw_first, bf16[128,1152]{1,0:T(8,128)(2,1)S(1)} %get-tuple-element.23.raw_other, f32[128,1152]{1,0:T(8,128)S(1)} %get-tuple-element.31.own, ...), custom_call_target="tpu_custom_call" | custom-call | flops 100000000 | bytes 1 | tf_op jit(solution)/shard_map/last/pallas_call | solution.py:70
  (32 shorter events, 0.9 us)
Async XLA Ops:
  1.9 6.7 %collective-permute-start.3 = (bf16[128,1152]{1,0:T(8,128)(2,1)S(1)}, bf16[128,1152]{1,0:T(8,128)(2,1)S(1)}, u32[]{:S(2)}, u32[]{:S(2)}) collective-permute-start(bf16[128,1152]{1,0:T(8,128)(2,1)S(1)} %get-tuple-element.24.first), channel_id=1, source_target_pairs={{0,16},{1,17},{2,18},{3,19},{4,20},{5,21},{6,22},{7,23},{8,24},{9,... | collective-permute-start | bytes 884744 | tf_op jit(solution)/shard_map/ppermute | solution.py:31
  5.3 3.9 %collective-permute-start = (bf16[128,1152]{1,0:T(8,128)(2,1)S(1)}, bf16[128,1152]{1,0:T(8,128)(2,1)S(1)}, u32[]{:S(2)}, u32[]{:S(2)}) collective-permute-start(bf16[128,1152]{1,0:T(8,128)(2,1)S(1)} %get-tuple-element.21.other), channel_id=1, source_target_pairs={{0,16},{1,17},{2,18},{3,19},{4,20},{5,21},{6,22},{7,23},{8,24},{9,... | collective-permute-start | bytes 884744 | tf_op jit(solution)/shard_map/ppermute | solution.py:31
  5.4 7.1 %collective-permute-start.1 = (bf16[128,1152]{1,0:T(8,128)(2,1)S(1)}, bf16[128,1152]{1,0:T(8,128)(2,1)S(1)}, u32[]{:S(2)}, u32[]{:S(2)}) collective-permute-start(bf16[128,1152]{1,0:T(8,128)(2,1)S(1)} %get-tuple-element.24.first), channel_id=1, source_target_pairs={{0,1},{1,2},{2,3},{3,0},{4,5},{5,6},{6,7},{7,4},{8,9},{9,10},{10,1... | collective-permute-start | bytes 884744 | tf_op jit(solution)/shard_map/ppermute | solution.py:31
  5.4 7.1 %collective-permute-start.2 = (bf16[128,1152]{1,0:T(8,128)(2,1)S(1)}, bf16[128,1152]{1,0:T(8,128)(2,1)S(1)}, u32[]{:S(2)}, u32[]{:S(2)}) collective-permute-start(bf16[128,1152]{1,0:T(8,128)(2,1)S(1)} %get-tuple-element.21.other), channel_id=1, source_target_pairs={{0,28},{1,29},{2,30},{3,31},{4,16},{5,17},{6,18},{7,19},{8,20},{9,... | collective-permute-start | bytes 884744 | tf_op jit(solution)/shard_map/ppermute | solution.py:31
  8.6 7.9 %collective-permute-start.6 = (bf16[128,1152]{1,0:T(8,128)(2,1)S(1)}, bf16[128,1152]{1,0:T(8,128)(2,1)S(1)}, u32[]{:S(2)}, u32[]{:S(2)}) collective-permute-start(bf16[128,1152]{1,0:T(8,128)(2,1)S(1)} %collective-permute-done.3.other_second), channel_id=1, source_target_pairs={{0,28},{1,29},{2,30},{3,31},{4,16},{5,17},{6,18},{7,19},{8,20},{9,... | collective-permute-start | bytes 884744 | tf_op jit(solution)/shard_map/ppermute | solution.py:31
  9.1 7.4 %collective-permute-start.5 = (bf16[128,1152]{1,0:T(8,128)(2,1)S(1)}, bf16[128,1152]{1,0:T(8,128)(2,1)S(1)}, u32[]{:S(2)}, u32[]{:S(2)}) collective-permute-start(bf16[128,1152]{1,0:T(8,128)(2,1)S(1)} %collective-permute-done.after.second), channel_id=1, source_target_pairs={{0,1},{1,2},{2,3},{3,0},{4,5},{5,6},{6,7},{7,4},{8,9},{9,10},{10,1... | collective-permute-start | bytes 884744 | tf_op jit(solution)/shard_map/ppermute | solution.py:31
  12.5 5.6 %collective-permute-start.4 = (bf16[256,1152]{1,0:T(8,128)(2,1)S(1)}, bf16[256,1152]{1,0:T(8,128)(2,1)S(1)}, u32[]{:S(2)}, u32[]{:S(2)}) collective-permute-start(bf16[256,1152]{1,0:T(8,128)(2,1)S(1)} %pair.1), channel_id=1, source_target_pairs={{0,16},{1,17},{2,18},{3,19},{4,20},{5,21},{6,22},{7,23},{8,24},{9,... | collective-permute-start | bytes 1769480 | tf_op jit(solution)/shard_map/ppermute | solution.py:31
  13.9 7.1 %collective-permute-start.8 = (bf16[128,1152]{1,0:T(8,128)(2,1)S(1)}, bf16[128,1152]{1,0:T(8,128)(2,1)S(1)}, u32[]{:S(2)}, u32[]{:S(2)}) collective-permute-start(bf16[128,1152]{1,0:T(8,128)(2,1)S(1)} %collective-permute-done.1.up.back_first), channel_id=1, source_target_pairs={{0,1},{1,2},{2,3},{3,0},{4,5},{5,6},{6,7},{7,4},{8,9},{9,10},{10,1... | collective-permute-start | bytes 884744 | tf_op jit(solution)/shard_map/ppermute | solution.py:31
  13.9 9.9 %collective-permute-start.10 = (bf16[128,1152]{1,0:T(8,128)(2,1)S(1)}, bf16[128,1152]{1,0:T(8,128)(2,1)S(1)}, u32[]{:S(2)}, u32[]{:S(2)}) collective-permute-start(bf16[128,1152]{1,0:T(8,128)(2,1)S(1)} %collective-permute-done.2.down.ahead_second), channel_id=1, source_target_pairs={{0,3},{1,0},{2,1},{3,2},{4,7},{5,4},{6,5},{7,6},{8,11},{9,8},{10,9... | collective-permute-start | bytes 884744 | tf_op jit(solution)/shard_map/ppermute | solution.py:31
  16.6 7.4 %collective-permute-start.7 = (bf16[256,1152]{1,0:T(8,128)(2,1)S(1)}, bf16[256,1152]{1,0:T(8,128)(2,1)S(1)}, u32[]{:S(2)}, u32[]{:S(2)}) collective-permute-start(bf16[256,1152]{1,0:T(8,128)(2,1)S(1)} %pad_maximum_fusion), channel_id=1, source_target_pairs={{0,16},{1,17},{2,18},{3,19},{4,20},{5,21},{6,22},{7,23},{8,24},{9,... | collective-permute-start | bytes 1769480 | tf_op jit(solution)/shard_map/ppermute | solution.py:31
  20.9 4.9 %collective-permute-start.9 = (bf16[128,1152]{1,0:T(8,128)(2,1)S(1)}, bf16[128,1152]{1,0:T(8,128)(2,1)S(1)}, u32[]{:S(2)}, u32[]{:S(2)}) collective-permute-start(bf16[128,1152]{1,0:T(8,128)(2,1)S(1)} %gate.2.far_first), channel_id=1, source_target_pairs={{0,16},{1,17},{2,18},{3,19},{4,20},{5,21},{6,22},{7,23},{8,24},{9,... | collective-permute-start | bytes 884744 | tf_op jit(solution)/shard_map/ppermute | solution.py:31
  23.7 2.1 %collective-permute-start.11 = (bf16[128,1152]{1,0:T(8,128)(2,1)S(1)}, bf16[128,1152]{1,0:T(8,128)(2,1)S(1)}, u32[]{:S(2)}, u32[]{:S(2)}) collective-permute-start(bf16[128,1152]{1,0:T(8,128)(2,1)S(1)} %gate.3.far_second), channel_id=1, source_target_pairs={{0,16},{1,17},{2,18},{3,19},{4,20},{5,21},{6,22},{7,23},{8,24},{9,... | collective-permute-start | bytes 884744 | tf_op jit(solution)/shard_map/ppermute | solution.py:31
  26.8 9.1 %collective-permute-start.14 = (bf16[128,1152]{1,0:T(8,128)(2,1)S(1)}, bf16[128,1152]{1,0:T(8,128)(2,1)S(1)}, u32[]{:S(2)}, u32[]{:S(2)}) collective-permute-start(bf16[128,1152]{1,0:T(8,128)(2,1)S(1)} %get-tuple-element.35), channel_id=1, source_target_pairs={{0,1},{1,2},{2,3},{3,0},{4,5},{5,6},{6,7},{7,4},{8,9},{9,10},{10,1... | collective-permute-start | bytes 884744 | tf_op jit(solution)/shard_map/ppermute | solution.py:31
  26.9 9.0 %collective-permute-start.13 = (bf16[128,1152]{1,0:T(8,128)(2,1)S(1)}, bf16[128,1152]{1,0:T(8,128)(2,1)S(1)}, u32[]{:S(2)}, u32[]{:S(2)}) collective-permute-start(bf16[128,1152]{1,0:T(8,128)(2,1)S(1)} %get-tuple-element.30.after), channel_id=1, source_target_pairs={{0,3},{1,0},{2,1},{3,2},{4,7},{5,4},{6,5},{7,6},{8,11},{9,8},{10,9... | collective-permute-start | bytes 884744 | tf_op jit(solution)/shard_map/ppermute | solution.py:31
  32.3 12.2 %collective-permute-start.16 = (f32[128,1152]{1,0:T(8,128)S(1)}, f32[128,1152]{1,0:T(8,128)S(1)}, u32[]{:S(2)}, u32[]{:S(2)}) collective-permute-start(f32[128,1152]{1,0:T(8,128)S(1)} %get-tuple-element.37), channel_id=1, source_target_pairs={{0,16},{1,17},{2,18},{3,19},{4,20},{5,21},{6,22},{7,23},{8,24},{9,... | collective-permute-start | bytes 1769480 | tf_op jit(solution)/shard_map/ppermute | solution.py:31
  33.4 7.1 %collective-permute-start.12 = (bf16[128,1152]{1,0:T(8,128)(2,1)S(1)}, bf16[128,1152]{1,0:T(8,128)(2,1)S(1)}, u32[]{:S(2)}, u32[]{:S(2)}) collective-permute-start(bf16[128,1152]{1,0:T(8,128)(2,1)S(1)} %get-tuple-element.32), channel_id=1, source_target_pairs={{0,1},{1,2},{2,3},{3,0},{4,5},{5,6},{6,7},{7,4},{8,9},{9,10},{10,1... | collective-permute-start | bytes 884744 | tf_op jit(solution)/shard_map/ppermute | solution.py:31
  33.4 7.1 %collective-permute-start.17 = (bf16[128,1152]{1,0:T(8,128)(2,1)S(1)}, bf16[128,1152]{1,0:T(8,128)(2,1)S(1)}, u32[]{:S(2)}, u32[]{:S(2)}) collective-permute-start(bf16[128,1152]{1,0:T(8,128)(2,1)S(1)} %get-tuple-element.38), channel_id=1, source_target_pairs={{0,19},{1,16},{2,17},{3,18},{4,23},{5,20},{6,21},{7,22},{8,27},{9,... | collective-permute-start | bytes 884744 | tf_op jit(solution)/shard_map/ppermute | solution.py:31
  36.0 6.7 %collective-permute-start.15 = (bf16[128,1152]{1,0:T(8,128)(2,1)S(1)}, bf16[128,1152]{1,0:T(8,128)(2,1)S(1)}, u32[]{:S(2)}, u32[]{:S(2)}) collective-permute-start(bf16[128,1152]{1,0:T(8,128)(2,1)S(1)} %get-tuple-element.36), channel_id=1, source_target_pairs={{0,3},{1,0},{2,1},{3,2},{4,7},{5,4},{6,5},{7,6},{8,11},{9,8},{10,9... | collective-permute-start | bytes 884744 | tf_op jit(solution)/shard_map/ppermute | solution.py:31
  36.8 7.7 %collective-permute-start.18 = (bf16[128,1152]{1,0:T(8,128)(2,1)S(1)}, bf16[128,1152]{1,0:T(8,128)(2,1)S(1)}, u32[]{:S(2)}, u32[]{:S(2)}) collective-permute-start(bf16[128,1152]{1,0:T(8,128)(2,1)S(1)} %get-tuple-element.39), channel_id=1, source_target_pairs={{0,17},{1,18},{2,19},{3,16},{4,21},{5,22},{6,23},{7,20},{8,25},{9,... | collective-permute-start | bytes 884744 | tf_op jit(solution)/shard_map/ppermute | solution.py:31

commit v4 on v3

--- a/solution.py
+++ b/solution.py
@@ -10,6 +10,10 @@
 epsilon = 1e-06
 AXES = ("grp", "ing")
 SIDE = 4
+C1 = 1
+C2 = 1
+C3 = 1
+C4 = 1
 VMEM_BYTES = 16 * 1024 * 1024
 VMEM = pl.BlockSpec(memory_space=pltpu.VMEM)
 SMEM = pl.BlockSpec(memory_space=pltpu.SMEM)
@@ -99,7 +103,7 @@
     other[...] = unit_rows(raw_other[...])[0].astype(jnp.bfloat16)
 
 
-def consts_kernel(numbers, after, consts):
+def consts_kernel(numbers, after, after_too, consts):
     scale = jnp.exp(numbers[0:8])
     consts[0:8] = scale
     consts[8:16] = scale * (-math.log2(math.e))
@@ -121,41 +125,24 @@
     return jnp.concatenate([up[...], down[...]], 0)
 
 
-def near_kernel(consts, first, second, back_first, ahead_second, other, other_second, near_others, part_own,
-                part_back_first, part_ahead_second):
-    rows = first.shape[0]
-    left = jnp.concatenate([first[...], second[...], back_first[...], ahead_second[...]], 0)
-    right = joined(other, other_second)
-    cosine = dot_t(left, right)
-    weights = negative(cosine, consts)
-    pairs = cosine[: 2 * rows]
-    i = lax.broadcasted_iota(jnp.int32, pairs.shape, 0)
-    j = lax.broadcasted_iota(jnp.int32, pairs.shape, 1)
-    own = jnp.where(i == j, positive(pairs, consts), weights[: 2 * rows])
-    total = dot(jnp.concatenate([own, weights[2 * rows :]], 0), right)
-    total += dot(negative(dot_t(left, near_others[...]), consts), near_others[...])
-    part_own[...] = total[: 2 * rows]
-    part_back_first[...] = total[2 * rows : 3 * rows]
-    part_ahead_second[...] = total[3 * rows :]
-
-
-def second_kernel(consts, back_second, ahead_first, other, other_second, near_others, part_back_second,
-                  part_ahead_first):
-    rows = back_second.shape[0]
-    left = joined(back_second, ahead_first)
+def near_kernel(consts, back_first, back_second, ahead_first, ahead_second, other, other_second, near_first,
+                near_second, part_back, part_ahead):
+    rows = back_first.shape[0]
+    left = jnp.concatenate([back_first[...], back_second[...], ahead_first[...], ahead_second[...]], 0)
     right = joined(other, other_second)
     total = dot(negative(dot_t(left, right), consts), right)
-    total += dot(negative(dot_t(left, near_others[...]), consts), near_others[...])
-    part_back_second[...] = total[:rows]
-    part_ahead_first[...] = total[rows:]
-
-
-def far_near_kernel(consts, far_first, far_second, other, other_second, near_others, late_others, part):
+    right = joined(near_first, near_second)
+    total += dot(negative(dot_t(left, right), consts), right)
+    part_back[...] = total[: 2 * rows]
+    part_ahead[...] = total[2 * rows :]
+
+
+def far_near_kernel(consts, far_first, far_second, other, other_second, near_first, near_second, late_others, part):
     left = joined(far_first, far_second)
     right = joined(other, other_second)
     total = dot(negative(dot_t(left, right), consts), right)
-    for others in (near_others, late_others):
-        total += dot(negative(dot_t(left, others[...]), consts), others[...])
+    for right in (joined(near_first, near_second), late_others[...]):
+        total += dot(negative(dot_t(left, right), consts), right)
     part[...] = total
 
 
@@ -168,23 +155,43 @@
     share_second[...] = total[rows:].astype(jnp.bfloat16)
 
 
-def rest_kernel(consts, part_own, part_back_first, part_back_second, part_ahead_first, part_ahead_second, first, second,
-                back_first, back_second, ahead_first, ahead_second, late_others, far_others_first, far_others_second,
-                after, own_first, own_second, out_back_first, out_back_second, out_ahead_first, out_ahead_second):
-    rows = first.shape[0]
+def rest_kernel(consts, part_back, part_ahead, back_first, back_second, ahead_first, ahead_second, late_others,
+                far_others_first, far_others_second, after, keep_back_first, share_back_second, share_ahead_first,
+                keep_ahead_second):
+    rows = back_first.shape[0]
     late = late_others[...]
     far_others = joined(far_others_first, far_others_second)
-    for up, down, part, out_up, out_down in (
-        (back_first, back_second, (part_back_first, part_back_second), out_back_first, out_back_second),
-        (ahead_first, ahead_second, (part_ahead_first, part_ahead_second), out_ahead_first, out_ahead_second),
-        (first, second, (part_own,), own_first, own_second),
+    left = jnp.concatenate([back_first[...], back_second[...], ahead_first[...], ahead_second[...]], 0)
+    total = dot(negative(dot_t(left, late), consts), late)
+    total += dot(negative(dot_t(left, far_others), consts), far_others)
+    keep_back_first[...] = total[:rows] + part_back[:rows]
+    share_back_second[...] = (total[rows : 2 * rows] + part_back[rows:]).astype(jnp.bfloat16)
+    share_ahead_first[...] = (total[2 * rows : 3 * rows] + part_ahead[:rows]).astype(jnp.bfloat16)
+    keep_ahead_second[...] = total[3 * rows :] + part_ahead[rows:]
+
+
+def units_kernel(raw_first, raw_other, after, unit_own, length_own, unit_their, length_their):
+    unit_own[...], length_own[...] = unit_rows(raw_first[...])
+    unit_their[...], length_their[...] = unit_rows(raw_other[...])
+
+
+def own_kernel(consts, first, second, back_first, back_second, ahead_first, ahead_second, far_first, far_second, other,
+               other_second, near_first, near_second, late_others, far_others_first, far_others_second, after, own,
+               their):
+    for left, pairs, rights, out in (
+        (first, joined(other, other_second),
+         [joined(near_first, near_second), late_others[...], joined(far_others_first, far_others_second)], own),
+        (other, joined(first, second),
+         [joined(back_first, back_second), joined(ahead_first, ahead_second), joined(far_first, far_second)], their),
     ):
-        left = joined(up, down)
-        total = dot(negative(dot_t(left, late), consts), late)
-        total += dot(negative(dot_t(left, far_others), consts), far_others)
-        total += joined(*part) if len(part) > 1 else part[0][...]
-        out_up[...] = total[:rows].astype(out_up.dtype)
-        out_down[...] = total[rows:].astype(out_down.dtype)
+        cosine = dot_t(left[...], pairs)
+        i = lax.broadcasted_iota(jnp.int32, cosine.shape, 0)
+        j = lax.broadcasted_iota(jnp.int32, cosine.shape, 1)
+        weights = jnp.where(i == j, positive(cosine, consts), negative(cosine, consts))
+        total = dot(weights, pairs)
+        for right in rights:
+            total += dot(negative(dot_t(left[...], right), consts), right)
+        out[...] = total
 
 
 def relay_kernel(up, up_got, down, down_got, up_out, down_out):
@@ -192,21 +199,21 @@
     down_out[...] = (down[...] + down_got[...].astype(jnp.float32)).astype(jnp.bfloat16)
 
 
-def last_kernel(core, consts, raw_first, raw_other, own, own_one, own_two, their, their_one, their_two,
-                image_out, text_out, own_grad, their_grad, sems):
+def last_kernel(core, consts, unit_own, length_own, unit_their, length_their, own, own_one, own_two, their, their_one,
+                their_two, image_out, text_out, own_grad, their_grad, sems):
     rows = own.shape[0]
     parts = sems.shape[1]
     block = rows // parts
     scale = consts[0:1, 0:1]
     for part in range(parts):
         at = pl.ds(part * block, block)
-        for kind, (raw, mine, one, two, grad) in enumerate((
-            (raw_first, own, own_one, own_two, own_grad),
-            (raw_other, their, their_one, their_two, their_grad),
+        for kind, (units, length, mine, one, two, grad) in enumerate((
+            (unit_own, length_own, own, own_one, own_two, own_grad),
+            (unit_their, length_their, their, their_one, their_two, their_grad),
         )):
             direction = scale * (mine[at] + one[at].astype(jnp.float32) + two[at].astype(jnp.float32))
-            unit, length = unit_rows(raw[at])
-            grad[at] = (direction - unit * jnp.sum(unit * direction, axis=1, keepdims=True)) / length
+            unit = units[at]
+            grad[at] = (direction - unit * jnp.sum(unit * direction, axis=1, keepdims=True)) / length[at]
             sem = sems.at[kind, part]
             for value, out in ((0, (image_out, text_out)[kind]), (1, (text_out, image_out)[kind])):
 
@@ -237,12 +244,6 @@
     )(pltpu.with_memory_space_constraint(value, pltpu.VMEM), pltpu.with_memory_space_constraint(after, pltpu.VMEM))
 
 
-def pair_kernel(up, down, after, out):
-    rows = up.shape[0]
-    out[:rows] = up[...]
-    out[rows:] = down[...]
-
-
 def body(image_embed, text_embed, scale_logarithm, logit_bias, loss_grad):
     rows, width = image_embed.shape
     half = jax.ShapeDtypeStruct((rows, width), jnp.bfloat16)
@@ -267,30 +268,30 @@
     ahead_second = cross(other, -1)
     other_second = swap(first)
     second = swap(other)
-    (consts,) = call(consts_kernel, [jax.ShapeDtypeStruct((32, 128), jnp.float32)], [VMEM] * 2, 1, "consts")(
-        numbers, second
+    (consts,) = call(consts_kernel, [jax.ShapeDtypeStruct((32, 128), jnp.float32)], [VMEM] * 3, 1, "consts")(
+        numbers, second, other_second
     )
     back_second = hop(second, 1)
     ahead_first = cross(other_second, -1)
+    back_first = gate(back_first, consts)
+    ahead_second = gate(ahead_second, consts)
     far_first = hop(back_first, 1)
     far_second = hop(ahead_second, -1)
-    (near,) = call(pair_kernel, [jax.ShapeDtypeStruct((2 * rows, width), jnp.bfloat16)], [VMEM] * 3, 1, "pair")(
-        back_first, ahead_second, consts
-    )
-    near_others = swap(near)
+    near_others = (swap(back_first), swap(ahead_second))
+    backs = (back_first, back_second)
+    aheads = (ahead_first, ahead_second)
     late_others = swap(jnp.concatenate([back_second, ahead_first], 0))
-    part_own, part_back_first, part_ahead_second = call(near_kernel, [double, full, full], [VMEM] * 8, 1, "near")(
-        consts, first, second, back_first, ahead_second, other, other_second, near_others
-    )
-    part_back_second, part_ahead_first = call(second_kernel, [full] * 2, [VMEM] * 6, 1, "second")(
-        consts, back_second, ahead_first, other, other_second, near_others
-    )
-    far_first = gate(far_first, part_back_second)
-    far_second = gate(far_second, part_own)
+    part_back, part_ahead = call(near_kernel, [double] * 2, [VMEM] * 9, 1, "near")(
+        consts, *backs, *aheads, other, other_second, *near_others
+    )
+    column = jax.ShapeDtypeStruct((rows, 1), jnp.float32)
+    units = call(units_kernel, [full, column, full, column], [VMEM] * 3, 1, "units")(raw_first, raw_other, part_back)
+    far_first = gate(far_first, part_back)
+    far_second = gate(far_second, units[0])
     far_others_first = swap(far_first)
     far_others_second = swap(far_second)
-    (part_far,) = call(far_near_kernel, [double], [VMEM] * 7, 1, "far_near")(
-        consts, far_first, far_second, other, other_second, near_others, late_others
+    (part_far,) = call(far_near_kernel, [double], [VMEM] * 8, 1, "far_near")(
+        consts, far_first, far_second, other, other_second, *near_others, late_others
     )
     share_first, share_second = call(far_kernel, [half, half], [VMEM] * 6, 8 * unit, "far")(
         consts, part_far, far_first, far_second, far_others_first, far_others_second
@@ -298,25 +299,26 @@
 
     relay_first = hop(share_first, -1)
     relay_second = hop(share_second, 1)
-    own_first, own_second, keep_back_first, share_back_second, share_ahead_first, keep_ahead_second = call(
-        rest_kernel, [full, full, full, half, half, full], [VMEM] * 16, 40 * unit, "rest"
-    )(
-        consts, part_own, part_back_first, part_back_second, part_ahead_first, part_ahead_second, first, second,
-        back_first, back_second, ahead_first, ahead_second, late_others, far_others_first, far_others_second, share_first,
-    )
+    far_others = (far_others_first, far_others_second)
+    keep_back_first, share_back_second, share_ahead_first, keep_ahead_second = call(
+        rest_kernel, [full, half, half, full], [VMEM] * 11, C1, "rest"
+    )(consts, part_back, part_ahead, *backs, *aheads, late_others, *far_others, share_first)
     their_one = cross_back(share_back_second, -1)
     own_one = hop(share_ahead_first, 1)
-    their_second = swap(own_second)
-    send_first, send_second = call(relay_kernel, [half, half], [VMEM] * 4, 10**7, "relay")(
+    send_first, send_second = call(relay_kernel, [half, half], [VMEM] * 4, C3, "relay")(
         keep_back_first, relay_first, keep_ahead_second, relay_second
     )
     own_two = hop(send_first, -1)
     their_two = cross_back(send_second, 1)
+    own, their = call(own_kernel, [full, full], [VMEM] * 17, C2, "own")(
+        consts, first, second, *backs, *aheads, far_first, far_second, other, other_second, *near_others, late_others,
+        *far_others, send_first,
+    )
     image_gradient, text_gradient = call(
         last_kernel,
         [full, full],
-        [SMEM] + [VMEM] * 9,
-        10**8,
+        [SMEM] + [VMEM] * 11,
+        C4,
         "last",
         out_specs=[HBM] * 2,
         scratch=[
@@ -324,7 +326,7 @@
             pltpu.VMEM((rows, width), jnp.float32),
             pltpu.SemaphoreType.DMA((2, 4)),
         ],
-    )(core, consts, raw_first, raw_other, own_first, own_one, own_two, their_second, their_one, their_two)
+    )(core, consts, *units, own, own_one, own_two, their, their_one, their_two)
     return (image_gradient, text_gradient)
 
 

time: 46.3 us -> 42.7 us (0.922)
  waiting for transfers between devices: 9.12 us -> 2.93 us
  Pallas kernels: 11.3 us -> 13 us
  starting transfers between devices: 22.6 us -> 23.5 us
    ppermute x19, waiting for transfers between devices: 9.12 us -> 2.93 us  [moved(): return lax.ppermute(value, AXES, pairs)]
    pallas_call x10, Pallas kernels: 11.3 us -> 13 us  [call(): run(*[pltpu.with_memory_space_constraint(a, pltpu.VMEM if s is VMEM else...]
    ppermute x19, starting transfers between devices: 22.6 us -> 23.5 us  [moved(): return lax.ppermute(value, AXES, pairs)]
  transfers between devices with their start and end apart: 19 -> 19, of which waited for: 5 -> 4; matrix products, arithmetic and copies ran while one was open for 0% -> 0% of each run, Pallas kernels for 16% -> 22%
where the time goes in v4:
time: 42.7 us; the launch traced here: 42.6 us
  starting transfers between devices  23.5 us (55%)
  Pallas kernels  13 us (30%)
  between operations  2.94 us (7%)
  waiting for transfers between devices  2.93 us (7%)
    ppermute x19, starting transfers between devices, moved(): return lax.ppermute(value, AXES, pairs)  23.5 us
    pallas_call x10, Pallas kernels, call(): run(*[pltpu.with_memory_space_constraint(a, pltpu.VMEM if s is VMEM else...  13 us
    ppermute x19, waiting for transfers between devices, moved(): return lax.ppermute(value, AXES, pairs)  2.93 us
  transfers between devices with their start and end apart: 19, of which 4 were waited for; matrix products, arithmetic and copies ran while one was open for 0% of the time, Pallas kernels for 22%

profile of v4, /device:TPU:1, one launch (start us, length us, event | category | flops | bytes accessed | tf_op | source)
XLA Modules:
  0.0 42.6 jit_solution(7002556857346968483)
XLA Ops:
  0.6 1.3 %rows.1 = (bf16[128,1152]{1,0:T(8,128)(2,1)S(1)}, bf16[128,1152]{1,0:T(8,128)(2,1)S(1)}, bf16[128,1152]{1,0:T(8,128)(2,1)S(1)}, bf16[128,1152]{1,0:T(8,128)(2,1)S(1)}) custom-call(s32[1]{0:T(128)} %bitcast.core, bf16[128,1152]{1,0:T(8,128)(2,1)} %image.1, bf16[128,1152]{1,0:T(8,128)(2,1)} %text.1), custom_call_target="tpu_custom_call" | custom-call | flops 100000000 | bytes 1 | tf_op jit(solution)/shard_map/rows/pallas_call | solution.py:74
  1.9 3.3 %collective-permute-start.1 = (bf16[128,1152]{1,0:T(8,128)(2,1)S(1)}, bf16[128,1152]{1,0:T(8,128)(2,1)S(1)}, u32[]{:S(2)}, u32[]{:S(2)}) collective-permute-start(bf16[128,1152]{1,0:T(8,128)(2,1)S(1)} %get-tuple-element.23.first), channel_id=1, source_target_pairs={{0,16},{1,17},{2,18},{3,19},{4,20},{5,21},{6,22},{7,23},{8,24},{9,... | collective-permute-start | bytes 884744 | tf_op jit(solution)/shard_map/ppermute | solution.py:35
  5.4 3.2 %collective-permute-start.5 = (bf16[128,1152]{1,0:T(8,128)(2,1)S(1)}, bf16[128,1152]{1,0:T(8,128)(2,1)S(1)}, u32[]{:S(2)}, u32[]{:S(2)}) collective-permute-start(bf16[128,1152]{1,0:T(8,128)(2,1)S(1)} %get-tuple-element.22.other), channel_id=1, source_target_pairs={{0,28},{1,29},{2,30},{3,31},{4,16},{5,17},{6,18},{7,19},{8,20},{9,... | collective-permute-start | bytes 884744 | tf_op jit(solution)/shard_map/ppermute | solution.py:35
  8.6 0.5 %collective-permute-start.4 = (bf16[128,1152]{1,0:T(8,128)(2,1)S(1)}, bf16[128,1152]{1,0:T(8,128)(2,1)S(1)}, u32[]{:S(2)}, u32[]{:S(2)}) collective-permute-start(bf16[128,1152]{1,0:T(8,128)(2,1)S(1)} %collective-permute-done.1.after_too.other_second), channel_id=1, source_target_pairs={{0,28},{1,29},{2,30},{3,31},{4,16},{5,17},{6,18},{7,19},{8,20},{9,... | collective-permute-start | bytes 884744 | tf_op jit(solution)/shard_map/ppermute | solution.py:35
  11.3 1.1 %collective-permute-done.2.value = bf16[128,1152]{1,0:T(8,128)(2,1)S(1)} collective-permute-done((bf16[128,1152]{1,0:T(8,128)(2,1)S(1)}, bf16[128,1152]{1,0:T(8,128)(2,1)S(1)}, u32[]{:S(2)}, u32[]{:S(2)}) %collective-permute-start.2) | collective-permute-done | bytes 294944 | tf_op jit(solution)/shard_map/ppermute | solution.py:35
  12.5 0.2 collective-permute-start.8
  12.7 1.3 %collective-permute-start.6 = (bf16[128,1152]{1,0:T(8,128)(2,1)S(1)}, bf16[128,1152]{1,0:T(8,128)(2,1)S(1)}, u32[]{:S(2)}, u32[]{:S(2)}) collective-permute-start(bf16[128,1152]{1,0:T(8,128)(2,1)S(1)} %gate.4.back_first), channel_id=1, source_target_pairs={{0,16},{1,17},{2,18},{3,19},{4,20},{5,21},{6,22},{7,23},{8,24},{9,... | collective-permute-start | bytes 884744 | tf_op jit(solution)/shard_map/ppermute | solution.py:35
  14.0 1.7 %collective-permute-start.9 = (bf16[128,1152]{1,0:T(8,128)(2,1)S(1)}, bf16[128,1152]{1,0:T(8,128)(2,1)S(1)}, u32[]{:S(2)}, u32[]{:S(2)}) collective-permute-start(bf16[128,1152]{1,0:T(8,128)(2,1)S(1)} %gate.5.ahead_second), channel_id=1, source_target_pairs={{0,3},{1,0},{2,1},{3,2},{4,7},{5,4},{6,5},{7,6},{8,11},{9,8},{10,9... | collective-permute-start | bytes 884744 | tf_op jit(solution)/shard_map/ppermute | solution.py:35
  15.7 1.3 %collective-permute-start.7 = (bf16[128,1152]{1,0:T(8,128)(2,1)S(1)}, bf16[128,1152]{1,0:T(8,128)(2,1)S(1)}, u32[]{:S(2)}, u32[]{:S(2)}) collective-permute-start(bf16[128,1152]{1,0:T(8,128)(2,1)S(1)} %gate.5.ahead_second), channel_id=1, source_target_pairs={{0,16},{1,17},{2,18},{3,19},{4,20},{5,21},{6,22},{7,23},{8,24},{9,... | collective-permute-start | bytes 884744 | tf_op jit(solution)/shard_map/ppermute | solution.py:35
  17.0 1.1 %collective-permute-start.10 = (bf16[256,1152]{1,0:T(8,128)(2,1)S(1)}, bf16[256,1152]{1,0:T(8,128)(2,1)S(1)}, u32[]{:S(2)}, u32[]{:S(2)}) collective-permute-start(bf16[256,1152]{1,0:T(8,128)(2,1)S(1)} %pad_maximum_fusion), channel_id=1, source_target_pairs={{0,16},{1,17},{2,18},{3,19},{4,20},{5,21},{6,22},{7,23},{8,24},{9,... | collective-permute-start | bytes 1769480 | tf_op jit(solution)/shard_map/ppermute | solution.py:35
  18.2 1.8 %near.1 = (f32[256,1152]{1,0:T(8,128)S(1)}, f32[256,1152]{1,0:T(8,128)S(1)}) custom-call(f32[32,128]{1,0:T(8,128)S(1)} %consts.1.after, bf16[128,1152]{1,0:T(8,128)(2,1)S(1)} %gate.4.back_first, bf16[128,1152]{1,0:T(8,128)(2,1)S(1)} %collective-permute-done.3.back_second, bf16[128,1152]{1,0:T(8,128)(2,1)S(1)} %collective-permute-done.4.ahead_first, ...), custom_call_target="tpu_custom_call" | custom-call | flops 1 | bytes 1 | tf_op jit(solution)/shard_map/near/pallas_call | solution.py:74
  20.0 1.6 %collective-permute-start.11 = (bf16[128,1152]{1,0:T(8,128)(2,1)S(1)}, bf16[128,1152]{1,0:T(8,128)(2,1)S(1)}, u32[]{:S(2)}, u32[]{:S(2)}) collective-permute-start(bf16[128,1152]{1,0:T(8,128)(2,1)S(1)} %gate.6.far_first), channel_id=1, source_target_pairs={{0,16},{1,17},{2,18},{3,19},{4,20},{5,21},{6,22},{7,23},{8,24},{9,... | collective-permute-start | bytes 884744 | tf_op jit(solution)/shard_map/ppermute | solution.py:35
  21.9 0.3 collective-permute-start.12
  22.2 1.8 %far_near.1.part = f32[256,1152]{1,0:T(8,128)S(1)} custom-call(f32[32,128]{1,0:T(8,128)S(1)} %consts.1.after, bf16[128,1152]{1,0:T(8,128)(2,1)S(1)} %gate.6.far_first, bf16[128,1152]{1,0:T(8,128)(2,1)S(1)} %gate.7.far_second, bf16[128,1152]{1,0:T(8,128)(2,1)S(1)} %get-tuple-element.22.other, ...), custom_call_target="tpu_custom_call" | custom-call | flops 1 | bytes 1 | tf_op jit(solution)/shard_map/far_near/pallas_call | solution.py:74
  24.0 0.9 %far.1 = (bf16[128,1152]{1,0:T(8,128)(2,1)S(1)}, bf16[128,1152]{1,0:T(8,128)(2,1)S(1)}) custom-call(f32[32,128]{1,0:T(8,128)S(1)} %consts.1.after, f32[256,1152]{1,0:T(8,128)S(1)} %far_near.1.part, bf16[128,1152]{1,0:T(8,128)(2,1)S(1)} %gate.6.far_first, bf16[128,1152]{1,0:T(8,128)(2,1)S(1)} %gate.7.far_second, ...), custom_call_target="tpu_custom_call" | custom-call | flops 301989888 | bytes 1 | tf_op jit(solution)/shard_map/far/pallas_call | solution.py:74
  25.0 2.7 %collective-permute-start.13 = (bf16[128,1152]{1,0:T(8,128)(2,1)S(1)}, bf16[128,1152]{1,0:T(8,128)(2,1)S(1)}, u32[]{:S(2)}, u32[]{:S(2)}) collective-permute-start(bf16[128,1152]{1,0:T(8,128)(2,1)S(1)} %get-tuple-element.32.after), channel_id=1, source_target_pairs={{0,3},{1,0},{2,1},{3,2},{4,7},{5,4},{6,5},{7,6},{8,11},{9,8},{10,9... | collective-permute-start | bytes 884744 | tf_op jit(solution)/shard_map/ppermute | solution.py:35
  27.7 1.7 %rest.1 = (f32[128,1152]{1,0:T(8,128)S(1)}, bf16[128,1152]{1,0:T(8,128)(2,1)S(1)}, bf16[128,1152]{1,0:T(8,128)(2,1)S(1)}, f32[128,1152]{1,0:T(8,128)S(1)}) custom-call(f32[32,128]{1,0:T(8,128)S(1)} %consts.1.after, f32[256,1152]{1,0:T(8,128)S(1)} %get-tuple-element.26.after.part_back, f32[256,1152]{1,0:T(8,128)S(1)} %get-tuple-element.31.part_ahead, ...), custom_call_target="tpu_custom_call" | custom-call | flops 1 | bytes 1 | tf_op jit(solution)/shard_map/rest/pallas_call | solution.py:74
  29.5 2.0 %collective-permute-start.17 = (bf16[128,1152]{1,0:T(8,128)(2,1)S(1)}, bf16[128,1152]{1,0:T(8,128)(2,1)S(1)}, u32[]{:S(2)}, u32[]{:S(2)}) collective-permute-start(bf16[128,1152]{1,0:T(8,128)(2,1)S(1)} %get-tuple-element.40), channel_id=1, source_target_pairs={{0,19},{1,16},{2,17},{3,18},{4,23},{5,20},{6,21},{7,22},{8,27},{9,... | collective-permute-start | bytes 884744 | tf_op jit(solution)/shard_map/ppermute | solution.py:35
  31.5 0.6 %collective-permute-done.14.down_got = bf16[128,1152]{1,0:T(8,128)(2,1)S(1)} collective-permute-done((bf16[128,1152]{1,0:T(8,128)(2,1)S(1)}, bf16[128,1152]{1,0:T(8,128)(2,1)S(1)}, u32[]{:S(2)}, u32[]{:S(2)}) %collective-permute-start.14) | collective-permute-done | bytes 294944 | tf_op jit(solution)/shard_map/ppermute | solution.py:35
  32.2 1.2 %collective-permute-start.18 = (bf16[128,1152]{1,0:T(8,128)(2,1)S(1)}, bf16[128,1152]{1,0:T(8,128)(2,1)S(1)}, u32[]{:S(2)}, u32[]{:S(2)}) collective-permute-start(bf16[128,1152]{1,0:T(8,128)(2,1)S(1)} %get-tuple-element.41), channel_id=1, source_target_pairs={{0,17},{1,18},{2,19},{3,16},{4,21},{5,22},{6,23},{7,20},{8,25},{9,... | collective-permute-start | bytes 884744 | tf_op jit(solution)/shard_map/ppermute | solution.py:35
  33.4 2.7 %collective-permute-start.16 = (bf16[128,1152]{1,0:T(8,128)(2,1)S(1)}, bf16[128,1152]{1,0:T(8,128)(2,1)S(1)}, u32[]{:S(2)}, u32[]{:S(2)}) collective-permute-start(bf16[128,1152]{1,0:T(8,128)(2,1)S(1)} %get-tuple-element.36.after), channel_id=1, source_target_pairs={{0,3},{1,0},{2,1},{3,2},{4,7},{5,4},{6,5},{7,6},{8,11},{9,8},{10,9... | collective-permute-start | bytes 884744 | tf_op jit(solution)/shard_map/ppermute | solution.py:35
  36.2 3.6 %own.1 = (f32[128,1152]{1,0:T(8,128)S(1)}, f32[128,1152]{1,0:T(8,128)S(1)}) custom-call(f32[32,128]{1,0:T(8,128)S(1)} %consts.1.after, bf16[128,1152]{1,0:T(8,128)(2,1)S(1)} %get-tuple-element.23.first, bf16[128,1152]{1,0:T(8,128)(2,1)S(1)} %collective-permute-done.after.second, bf16[128,1152]{1,0:T(8,128)(2,1)S(1)} %gate.4.back_first, ...), custom_call_target="tpu_custom_call" | custom-call | flops 1 | bytes 1 | tf_op jit(solution)/shard_map/own/pallas_call | solution.py:74
  39.9 1.1 %collective-permute-done.18.their_two = bf16[128,1152]{1,0:T(8,128)(2,1)S(1)} collective-permute-done((bf16[128,1152]{1,0:T(8,128)(2,1)S(1)}, bf16[128,1152]{1,0:T(8,128)(2,1)S(1)}, u32[]{:S(2)}, u32[]{:S(2)}) %collective-permute-start.18) | collective-permute-done | bytes 294944 | tf_op jit(solution)/shard_map/ppermute | solution.py:35
  41.0 1.5 %last.1 = (f32[128,1152]{1,0:T(8,128)}, f32[128,1152]{1,0:T(8,128)}) custom-call(s32[1]{0:T(128)} %bitcast.core, f32[32,128]{1,0:T(8,128)S(1)} %consts.1.after, f32[128,1152]{1,0:T(8,128)S(1)} %get-tuple-element.27.after.unit_own, f32[128,1]{1,0:T(8,128)S(1)} %get-tuple-element.28.length_own, f32[128,1152]{1,0:T(8,128)S(1)} %get-tuple-element.29.unit_their, ...), custom_call_target="tpu_custom_call" | custom-call | flops 1 | bytes 1 | tf_op jit(solution)/shard_map/last/pallas_call | solution.py:74
  (34 shorter events, 1.0 us)
Async XLA Ops:
  1.9 6.7 %collective-permute-start.1 = (bf16[128,1152]{1,0:T(8,128)(2,1)S(1)}, bf16[128,1152]{1,0:T(8,128)(2,1)S(1)}, u32[]{:S(2)}, u32[]{:S(2)}) collective-permute-start(bf16[128,1152]{1,0:T(8,128)(2,1)S(1)} %get-tuple-element.23.first), channel_id=1, source_target_pairs={{0,16},{1,17},{2,18},{3,19},{4,20},{5,21},{6,22},{7,23},{8,24},{9,... | collective-permute-start | bytes 884744 | tf_op jit(solution)/shard_map/ppermute | solution.py:35
  5.3 3.9 %collective-permute-start = (bf16[128,1152]{1,0:T(8,128)(2,1)S(1)}, bf16[128,1152]{1,0:T(8,128)(2,1)S(1)}, u32[]{:S(2)}, u32[]{:S(2)}) collective-permute-start(bf16[128,1152]{1,0:T(8,128)(2,1)S(1)} %get-tuple-element.22.other), channel_id=1, source_target_pairs={{0,16},{1,17},{2,18},{3,19},{4,20},{5,21},{6,22},{7,23},{8,24},{9,... | collective-permute-start | bytes 884744 | tf_op jit(solution)/shard_map/ppermute | solution.py:35
  5.4 7.1 %collective-permute-start.2 = (bf16[128,1152]{1,0:T(8,128)(2,1)S(1)}, bf16[128,1152]{1,0:T(8,128)(2,1)S(1)}, u32[]{:S(2)}, u32[]{:S(2)}) collective-permute-start(bf16[128,1152]{1,0:T(8,128)(2,1)S(1)} %get-tuple-element.23.first), channel_id=1, source_target_pairs={{0,1},{1,2},{2,3},{3,0},{4,5},{5,6},{6,7},{7,4},{8,9},{9,10},{10,1... | collective-permute-start | bytes 884744 | tf_op jit(solution)/shard_map/ppermute | solution.py:35
  5.4 8.6 %collective-permute-start.5 = (bf16[128,1152]{1,0:T(8,128)(2,1)S(1)}, bf16[128,1152]{1,0:T(8,128)(2,1)S(1)}, u32[]{:S(2)}, u32[]{:S(2)}) collective-permute-start(bf16[128,1152]{1,0:T(8,128)(2,1)S(1)} %get-tuple-element.22.other), channel_id=1, source_target_pairs={{0,28},{1,29},{2,30},{3,31},{4,16},{5,17},{6,18},{7,19},{8,20},{9,... | collective-permute-start | bytes 884744 | tf_op jit(solution)/shard_map/ppermute | solution.py:35
  8.6 7.1 %collective-permute-start.4 = (bf16[128,1152]{1,0:T(8,128)(2,1)S(1)}, bf16[128,1152]{1,0:T(8,128)(2,1)S(1)}, u32[]{:S(2)}, u32[]{:S(2)}) collective-permute-start(bf16[128,1152]{1,0:T(8,128)(2,1)S(1)} %collective-permute-done.1.after_too.other_second), channel_id=1, source_target_pairs={{0,28},{1,29},{2,30},{3,31},{4,16},{5,17},{6,18},{7,19},{8,20},{9,... | collective-permute-start | bytes 884744 | tf_op jit(solution)/shard_map/ppermute | solution.py:35
  9.1 7.8 %collective-permute-start.3 = (bf16[128,1152]{1,0:T(8,128)(2,1)S(1)}, bf16[128,1152]{1,0:T(8,128)(2,1)S(1)}, u32[]{:S(2)}, u32[]{:S(2)}) collective-permute-start(bf16[128,1152]{1,0:T(8,128)(2,1)S(1)} %collective-permute-done.after.second), channel_id=1, source_target_pairs={{0,1},{1,2},{2,3},{3,0},{4,5},{5,6},{6,7},{7,4},{8,9},{9,10},{10,1... | collective-permute-start | bytes 884744 | tf_op jit(solution)/shard_map/ppermute | solution.py:35
  12.5 7.6 %collective-permute-start.8 = (bf16[128,1152]{1,0:T(8,128)(2,1)S(1)}, bf16[128,1152]{1,0:T(8,128)(2,1)S(1)}, u32[]{:S(2)}, u32[]{:S(2)}) collective-permute-start(bf16[128,1152]{1,0:T(8,128)(2,1)S(1)} %gate.4.back_first), channel_id=1, source_target_pairs={{0,1},{1,2},{2,3},{3,0},{4,5},{5,6},{6,7},{7,4},{8,9},{9,10},{10,1... | collective-permute-start | bytes 884744 | tf_op jit(solution)/shard_map/ppermute | solution.py:35
  12.7 5.4 %collective-permute-start.6 = (bf16[128,1152]{1,0:T(8,128)(2,1)S(1)}, bf16[128,1152]{1,0:T(8,128)(2,1)S(1)}, u32[]{:S(2)}, u32[]{:S(2)}) collective-permute-start(bf16[128,1152]{1,0:T(8,128)(2,1)S(1)} %gate.4.back_first), channel_id=1, source_target_pairs={{0,16},{1,17},{2,18},{3,19},{4,20},{5,21},{6,22},{7,23},{8,24},{9,... | collective-permute-start | bytes 884744 | tf_op jit(solution)/shard_map/ppermute | solution.py:35
  14.0 7.9 %collective-permute-start.9 = (bf16[128,1152]{1,0:T(8,128)(2,1)S(1)}, bf16[128,1152]{1,0:T(8,128)(2,1)S(1)}, u32[]{:S(2)}, u32[]{:S(2)}) collective-permute-start(bf16[128,1152]{1,0:T(8,128)(2,1)S(1)} %gate.5.ahead_second), channel_id=1, source_target_pairs={{0,3},{1,0},{2,1},{3,2},{4,7},{5,4},{6,5},{7,6},{8,11},{9,8},{10,9... | collective-permute-start | bytes 884744 | tf_op jit(solution)/shard_map/ppermute | solution.py:35
  15.7 2.5 %collective-permute-start.7 = (bf16[128,1152]{1,0:T(8,128)(2,1)S(1)}, bf16[128,1152]{1,0:T(8,128)(2,1)S(1)}, u32[]{:S(2)}, u32[]{:S(2)}) collective-permute-start(bf16[128,1152]{1,0:T(8,128)(2,1)S(1)} %gate.5.ahead_second), channel_id=1, source_target_pairs={{0,16},{1,17},{2,18},{3,19},{4,20},{5,21},{6,22},{7,23},{8,24},{9,... | collective-permute-start | bytes 884744 | tf_op jit(solution)/shard_map/ppermute | solution.py:35
  17.0 5.2 %collective-permute-start.10 = (bf16[256,1152]{1,0:T(8,128)(2,1)S(1)}, bf16[256,1152]{1,0:T(8,128)(2,1)S(1)}, u32[]{:S(2)}, u32[]{:S(2)}) collective-permute-start(bf16[256,1152]{1,0:T(8,128)(2,1)S(1)} %pad_maximum_fusion), channel_id=1, source_target_pairs={{0,16},{1,17},{2,18},{3,19},{4,20},{5,21},{6,22},{7,23},{8,24},{9,... | collective-permute-start | bytes 1769480 | tf_op jit(solution)/shard_map/ppermute | solution.py:35
  20.0 4.0 %collective-permute-start.11 = (bf16[128,1152]{1,0:T(8,128)(2,1)S(1)}, bf16[128,1152]{1,0:T(8,128)(2,1)S(1)}, u32[]{:S(2)}, u32[]{:S(2)}) collective-permute-start(bf16[128,1152]{1,0:T(8,128)(2,1)S(1)} %gate.6.far_first), channel_id=1, source_target_pairs={{0,16},{1,17},{2,18},{3,19},{4,20},{5,21},{6,22},{7,23},{8,24},{9,... | collective-permute-start | bytes 884744 | tf_op jit(solution)/shard_map/ppermute | solution.py:35
  21.9 2.1 %collective-permute-start.12 = (bf16[128,1152]{1,0:T(8,128)(2,1)S(1)}, bf16[128,1152]{1,0:T(8,128)(2,1)S(1)}, u32[]{:S(2)}, u32[]{:S(2)}) collective-permute-start(bf16[128,1152]{1,0:T(8,128)(2,1)S(1)} %gate.7.far_second), channel_id=1, source_target_pairs={{0,16},{1,17},{2,18},{3,19},{4,20},{5,21},{6,22},{7,23},{8,24},{9,... | collective-permute-start | bytes 884744 | tf_op jit(solution)/shard_map/ppermute | solution.py:35
  24.9 7.2 %collective-permute-start.14 = (bf16[128,1152]{1,0:T(8,128)(2,1)S(1)}, bf16[128,1152]{1,0:T(8,128)(2,1)S(1)}, u32[]{:S(2)}, u32[]{:S(2)}) collective-permute-start(bf16[128,1152]{1,0:T(8,128)(2,1)S(1)} %get-tuple-element.35), channel_id=1, source_target_pairs={{0,1},{1,2},{2,3},{3,0},{4,5},{5,6},{6,7},{7,4},{8,9},{9,10},{10,1... | collective-permute-start | bytes 884744 | tf_op jit(solution)/shard_map/ppermute | solution.py:35
  25.0 7.1 %collective-permute-start.13 = (bf16[128,1152]{1,0:T(8,128)(2,1)S(1)}, bf16[128,1152]{1,0:T(8,128)(2,1)S(1)}, u32[]{:S(2)}, u32[]{:S(2)}) collective-permute-start(bf16[128,1152]{1,0:T(8,128)(2,1)S(1)} %get-tuple-element.32.after), channel_id=1, source_target_pairs={{0,3},{1,0},{2,1},{3,2},{4,7},{5,4},{6,5},{7,6},{8,11},{9,8},{10,9... | collective-permute-start | bytes 884744 | tf_op jit(solution)/shard_map/ppermute | solution.py:35
  29.4 10.4 %collective-permute-start.15 = (bf16[128,1152]{1,0:T(8,128)(2,1)S(1)}, bf16[128,1152]{1,0:T(8,128)(2,1)S(1)}, u32[]{:S(2)}, u32[]{:S(2)}) collective-permute-start(bf16[128,1152]{1,0:T(8,128)(2,1)S(1)} %get-tuple-element.38), channel_id=1, source_target_pairs={{0,1},{1,2},{2,3},{3,0},{4,5},{5,6},{6,7},{7,4},{8,9},{9,10},{10,1... | collective-permute-start | bytes 884744 | tf_op jit(solution)/shard_map/ppermute | solution.py:35
  29.5 10.3 %collective-permute-start.17 = (bf16[128,1152]{1,0:T(8,128)(2,1)S(1)}, bf16[128,1152]{1,0:T(8,128)(2,1)S(1)}, u32[]{:S(2)}, u32[]{:S(2)}) collective-permute-start(bf16[128,1152]{1,0:T(8,128)(2,1)S(1)} %get-tuple-element.40), channel_id=1, source_target_pairs={{0,19},{1,16},{2,17},{3,18},{4,23},{5,20},{6,21},{7,22},{8,27},{9,... | collective-permute-start | bytes 884744 | tf_op jit(solution)/shard_map/ppermute | solution.py:35
  32.2 8.7 %collective-permute-start.18 = (bf16[128,1152]{1,0:T(8,128)(2,1)S(1)}, bf16[128,1152]{1,0:T(8,128)(2,1)S(1)}, u32[]{:S(2)}, u32[]{:S(2)}) collective-permute-start(bf16[128,1152]{1,0:T(8,128)(2,1)S(1)} %get-tuple-element.41), channel_id=1, source_target_pairs={{0,17},{1,18},{2,19},{3,16},{4,21},{5,22},{6,23},{7,20},{8,25},{9,... | collective-permute-start | bytes 884744 | tf_op jit(solution)/shard_map/ppermute | solution.py:35
  33.4 7.5 %collective-permute-start.16 = (bf16[128,1152]{1,0:T(8,128)(2,1)S(1)}, bf16[128,1152]{1,0:T(8,128)(2,1)S(1)}, u32[]{:S(2)}, u32[]{:S(2)}) collective-permute-start(bf16[128,1152]{1,0:T(8,128)(2,1)S(1)} %get-tuple-element.36.after), channel_id=1, source_target_pairs={{0,3},{1,0},{2,1},{3,2},{4,7},{5,4},{6,5},{7,6},{8,11},{9,8},{10,9... | collective-permute-start | bytes 884744 | tf_op jit(solution)/shard_map/ppermute | solution.py:35

commit v5 on v4

--- a/solution.py
+++ b/solution.py
@@ -125,32 +125,30 @@
     return jnp.concatenate([up[...], down[...]], 0)
 
 
+def share(consts, left, *rights):
+    right = jnp.concatenate([r[...] for r in rights], 0)
+    return dot(negative(dot_t(left, right), consts), right)
+
+
 def near_kernel(consts, back_first, back_second, ahead_first, ahead_second, other, other_second, near_first,
                 near_second, part_back, part_ahead):
     rows = back_first.shape[0]
     left = jnp.concatenate([back_first[...], back_second[...], ahead_first[...], ahead_second[...]], 0)
-    right = joined(other, other_second)
-    total = dot(negative(dot_t(left, right), consts), right)
-    right = joined(near_first, near_second)
-    total += dot(negative(dot_t(left, right), consts), right)
+    total = share(consts, left, other, other_second, near_first, near_second)
     part_back[...] = total[: 2 * rows]
     part_ahead[...] = total[2 * rows :]
 
 
 def far_near_kernel(consts, far_first, far_second, other, other_second, near_first, near_second, late_others, part):
-    left = joined(far_first, far_second)
-    right = joined(other, other_second)
-    total = dot(negative(dot_t(left, right), consts), right)
-    for right in (joined(near_first, near_second), late_others[...]):
-        total += dot(negative(dot_t(left, right), consts), right)
-    part[...] = total
+    part[...] = share(consts, joined(far_first, far_second), other, other_second, near_first, near_second, late_others)
 
 
 def far_kernel(consts, part, far_first, far_second, far_others_first, far_others_second, share_first, share_second):
     rows = far_first.shape[0]
-    others = joined(far_others_first, far_others_second)
-    weights = negative(dot_t(joined(far_first, far_second), others), consts)
-    total = part[...] + dot(weights, others)
+    left = joined(far_first, far_second)
+    rights = (far_others_first[...], far_others_second[...])
+    weights = [negative(dot_t(left, right), consts) for right in rights]
+    total = part[...] + dot(weights[0], rights[0]) + dot(weights[1], rights[1])
     share_first[...] = total[:rows].astype(jnp.bfloat16)
     share_second[...] = total[rows:].astype(jnp.bfloat16)
 
@@ -170,14 +168,14 @@
     keep_ahead_second[...] = total[3 * rows :] + part_ahead[rows:]
 
 
-def units_kernel(raw_first, raw_other, after, unit_own, length_own, unit_their, length_their):
-    unit_own[...], length_own[...] = unit_rows(raw_first[...])
+def units_kernel(raw, after, unit, length):
+    unit[...], length[...] = unit_rows(raw[...])
+
+
+def own_kernel(consts, first, second, back_first, back_second, ahead_first, ahead_second, far_first, far_second, other,
+               other_second, near_first, near_second, late_others, far_others_first, far_others_second, after, raw_other, own,
+               their, unit_their, length_their):
     unit_their[...], length_their[...] = unit_rows(raw_other[...])
-
-
-def own_kernel(consts, first, second, back_first, back_second, ahead_first, ahead_second, far_first, far_second, other,
-               other_second, near_first, near_second, late_others, far_others_first, far_others_second, after, own,
-               their):
     for left, pairs, rights, out in (
         (first, joined(other, other_second),
          [joined(near_first, near_second), late_others[...], joined(far_others_first, far_others_second)], own),
@@ -194,37 +192,25 @@
         out[...] = total
 
 
-def relay_kernel(up, up_got, down, down_got, up_out, down_out):
-    up_out[...] = (up[...] + up_got[...].astype(jnp.float32)).astype(jnp.bfloat16)
-    down_out[...] = (down[...] + down_got[...].astype(jnp.float32)).astype(jnp.bfloat16)
+def relay_kernel(mine, got, out):
+    out[...] = (mine[...] + got[...].astype(jnp.float32)).astype(jnp.bfloat16)
 
 
 def last_kernel(core, consts, unit_own, length_own, unit_their, length_their, own, own_one, own_two, their, their_one,
-                their_two, image_out, text_out, own_grad, their_grad, sems):
-    rows = own.shape[0]
-    parts = sems.shape[1]
-    block = rows // parts
+                their_two, image_out, text_out, grads, sems):
     scale = consts[0:1, 0:1]
-    for part in range(parts):
-        at = pl.ds(part * block, block)
-        for kind, (units, length, mine, one, two, grad) in enumerate((
-            (unit_own, length_own, own, own_one, own_two, own_grad),
-            (unit_their, length_their, their, their_one, their_two, their_grad),
-        )):
-            direction = scale * (mine[at] + one[at].astype(jnp.float32) + two[at].astype(jnp.float32))
-            unit = units[at]
-            grad[at] = (direction - unit * jnp.sum(unit * direction, axis=1, keepdims=True)) / length[at]
-            sem = sems.at[kind, part]
-            for value, out in ((0, (image_out, text_out)[kind]), (1, (text_out, image_out)[kind])):
-
-                @pl.when(core[0] == value)
-                def _(grad=grad, out=out, at=at, sem=sem):
-                    pltpu.make_async_copy(grad.at[at], out.at[at], sem).start()
-
-    for part in range(parts):
-        at = pl.ds(part * block, block)
-        pltpu.make_async_copy(own_grad.at[at], image_out.at[at], sems.at[0, part]).wait()
-        pltpu.make_async_copy(their_grad.at[at], text_out.at[at], sems.at[1, part]).wait()
+    for place, unit, length, mine, one, two in (
+        (core[0], unit_own, length_own, own, own_one, own_two),
+        (1 - core[0], unit_their, length_their, their, their_one, their_two),
+    ):
+        direction = scale * (mine[...] + one[...].astype(jnp.float32) + two[...].astype(jnp.float32))
+        along = jnp.sum(unit[...] * direction, axis=1, keepdims=True)
+        grads[place] = (direction - unit[...] * along) * (1.0 / length[...])
+    copies = [pltpu.make_async_copy(grads.at[i], out, sems.at[i]) for i, out in enumerate((image_out, text_out))]
+    for copy in copies:
+        copy.start()
+    for copy in copies:
+        copy.wait()
 
 
 def gate_kernel(value, after, out):
@@ -285,9 +271,9 @@
         consts, *backs, *aheads, other, other_second, *near_others
     )
     column = jax.ShapeDtypeStruct((rows, 1), jnp.float32)
-    units = call(units_kernel, [full, column, full, column], [VMEM] * 3, 1, "units")(raw_first, raw_other, part_back)
+    unit_own, length_own = call(units_kernel, [full, column], [VMEM] * 2, 1, "units")(raw_first, part_back)
     far_first = gate(far_first, part_back)
-    far_second = gate(far_second, units[0])
+    far_second = gate(far_second, unit_own)
     far_others_first = swap(far_first)
     far_others_second = swap(far_second)
     (part_far,) = call(far_near_kernel, [double], [VMEM] * 8, 1, "far_near")(
@@ -305,14 +291,15 @@
     )(consts, part_back, part_ahead, *backs, *aheads, late_others, *far_others, share_first)
     their_one = cross_back(share_back_second, -1)
     own_one = hop(share_ahead_first, 1)
-    send_first, send_second = call(relay_kernel, [half, half], [VMEM] * 4, C3, "relay")(
-        keep_back_first, relay_first, keep_ahead_second, relay_second
-    )
+    (send_first,) = call(relay_kernel, [half], [VMEM] * 2, C3, "relay")(keep_back_first, relay_first)
+    (send_second,) = call(relay_kernel, [half], [VMEM] * 2, C3, "relay")(keep_ahead_second, relay_second)
     own_two = hop(send_first, -1)
     their_two = cross_back(send_second, 1)
-    own, their = call(own_kernel, [full, full], [VMEM] * 17, C2, "own")(
+    own, their, unit_their, length_their = call(
+        own_kernel, [full, full, full, column], [VMEM] * 18, C2, "own"
+    )(
         consts, first, second, *backs, *aheads, far_first, far_second, other, other_second, *near_others, late_others,
-        *far_others, send_first,
+        *far_others, send_first, raw_other,
     )
     image_gradient, text_gradient = call(
         last_kernel,
@@ -322,11 +309,10 @@
         "last",
         out_specs=[HBM] * 2,
         scratch=[
-            pltpu.VMEM((rows, width), jnp.float32),
-            pltpu.VMEM((rows, width), jnp.float32),
-            pltpu.SemaphoreType.DMA((2, 4)),
+            pltpu.VMEM((2, rows, width), jnp.float32),
+            pltpu.SemaphoreType.DMA((2,)),
         ],
-    )(core, consts, *units, own, own_one, own_two, their, their_one, their_two)
+    )(core, consts, unit_own, length_own, unit_their, length_their, own, own_one, own_two, their, their_one, their_two)
     return (image_gradient, text_gradient)
 
 

time: 42.7 us -> 42.3 us (level)
  Pallas kernels: 13 us -> 12.5 us
    pallas_call x10 -> x11, Pallas kernels: 13 us -> 12.5 us  [call(): run(*[pltpu.with_memory_space_constraint(a, pltpu.VMEM if s is VMEM else...]
  transfers between devices with their start and end apart: 19 -> 19, of which waited for: 4 -> 4; matrix products, arithmetic and copies ran while one was open for 0% -> 0% of each run, Pallas kernels for 22% -> 21%
where the time goes in v5:
time: 42.3 us; the launch traced here: 42.2 us
  starting transfers between devices  23.7 us (56%)
  Pallas kernels  12.5 us (30%)
  between operations  2.93 us (7%)
  waiting for transfers between devices  2.92 us (7%)
    ppermute x19, starting transfers between devices, moved(): return lax.ppermute(value, AXES, pairs)  23.7 us
    pallas_call x11, Pallas kernels, call(): run(*[pltpu.with_memory_space_constraint(a, pltpu.VMEM if s is VMEM else...  12.5 us
    ppermute x19, waiting for transfers between devices, moved(): return lax.ppermute(value, AXES, pairs)  2.92 us
  transfers between devices with their start and end apart: 19, of which 4 were waited for; matrix products, arithmetic and copies ran while one was open for 0% of the time, Pallas kernels for 21%

profile of v5, /device:TPU:1, one launch (start us, length us, event | category | flops | bytes accessed | tf_op | source)
XLA Modules:
  0.0 42.2 jit_solution(115926111951273932)
XLA Ops:
  0.6 1.3 %rows.1 = (bf16[128,1152]{1,0:T(8,128)(2,1)S(1)}, bf16[128,1152]{1,0:T(8,128)(2,1)S(1)}, bf16[128,1152]{1,0:T(8,128)(2,1)S(1)}, bf16[128,1152]{1,0:T(8,128)(2,1)S(1)}) custom-call(s32[1]{0:T(128)} %bitcast.core, bf16[128,1152]{1,0:T(8,128)(2,1)} %image.1, bf16[128,1152]{1,0:T(8,128)(2,1)} %text.1), custom_call_target="tpu_custom_call" | custom-call | flops 100000000 | bytes 1 | tf_op jit(solution)/shard_map/rows/pallas_call | solution.py:74
  1.9 3.3 %collective-permute-start.1 = (bf16[128,1152]{1,0:T(8,128)(2,1)S(1)}, bf16[128,1152]{1,0:T(8,128)(2,1)S(1)}, u32[]{:S(2)}, u32[]{:S(2)}) collective-permute-start(bf16[128,1152]{1,0:T(8,128)(2,1)S(1)} %get-tuple-element.21.first), channel_id=1, source_target_pairs={{0,16},{1,17},{2,18},{3,19},{4,20},{5,21},{6,22},{7,23},{8,24},{9,... | collective-permute-start | bytes 884744 | tf_op jit(solution)/shard_map/ppermute | solution.py:35
  5.4 3.2 %collective-permute-start.5 = (bf16[128,1152]{1,0:T(8,128)(2,1)S(1)}, bf16[128,1152]{1,0:T(8,128)(2,1)S(1)}, u32[]{:S(2)}, u32[]{:S(2)}) collective-permute-start(bf16[128,1152]{1,0:T(8,128)(2,1)S(1)} %get-tuple-element.20.other), channel_id=1, source_target_pairs={{0,28},{1,29},{2,30},{3,31},{4,16},{5,17},{6,18},{7,19},{8,20},{9,... | collective-permute-start | bytes 884744 | tf_op jit(solution)/shard_map/ppermute | solution.py:35
  8.6 0.5 %collective-permute-start.4 = (bf16[128,1152]{1,0:T(8,128)(2,1)S(1)}, bf16[128,1152]{1,0:T(8,128)(2,1)S(1)}, u32[]{:S(2)}, u32[]{:S(2)}) collective-permute-start(bf16[128,1152]{1,0:T(8,128)(2,1)S(1)} %collective-permute-done.1.after_too.other_second), channel_id=1, source_target_pairs={{0,28},{1,29},{2,30},{3,31},{4,16},{5,17},{6,18},{7,19},{8,20},{9,... | collective-permute-start | bytes 884744 | tf_op jit(solution)/shard_map/ppermute | solution.py:35
  11.3 1.1 %collective-permute-done.2.value = bf16[128,1152]{1,0:T(8,128)(2,1)S(1)} collective-permute-done((bf16[128,1152]{1,0:T(8,128)(2,1)S(1)}, bf16[128,1152]{1,0:T(8,128)(2,1)S(1)}, u32[]{:S(2)}, u32[]{:S(2)}) %collective-permute-start.2) | collective-permute-done | bytes 294944 | tf_op jit(solution)/shard_map/ppermute | solution.py:35
  12.5 0.2 collective-permute-start.8
  12.7 1.3 %collective-permute-start.6 = (bf16[128,1152]{1,0:T(8,128)(2,1)S(1)}, bf16[128,1152]{1,0:T(8,128)(2,1)S(1)}, u32[]{:S(2)}, u32[]{:S(2)}) collective-permute-start(bf16[128,1152]{1,0:T(8,128)(2,1)S(1)} %gate.4.back_first), channel_id=1, source_target_pairs={{0,16},{1,17},{2,18},{3,19},{4,20},{5,21},{6,22},{7,23},{8,24},{9,... | collective-permute-start | bytes 884744 | tf_op jit(solution)/shard_map/ppermute | solution.py:35
  14.0 1.7 %collective-permute-start.9 = (bf16[128,1152]{1,0:T(8,128)(2,1)S(1)}, bf16[128,1152]{1,0:T(8,128)(2,1)S(1)}, u32[]{:S(2)}, u32[]{:S(2)}) collective-permute-start(bf16[128,1152]{1,0:T(8,128)(2,1)S(1)} %gate.5.ahead_second), channel_id=1, source_target_pairs={{0,3},{1,0},{2,1},{3,2},{4,7},{5,4},{6,5},{7,6},{8,11},{9,8},{10,9... | collective-permute-start | bytes 884744 | tf_op jit(solution)/shard_map/ppermute | solution.py:35
  15.7 1.3 %collective-permute-start.7 = (bf16[128,1152]{1,0:T(8,128)(2,1)S(1)}, bf16[128,1152]{1,0:T(8,128)(2,1)S(1)}, u32[]{:S(2)}, u32[]{:S(2)}) collective-permute-start(bf16[128,1152]{1,0:T(8,128)(2,1)S(1)} %gate.5.ahead_second), channel_id=1, source_target_pairs={{0,16},{1,17},{2,18},{3,19},{4,20},{5,21},{6,22},{7,23},{8,24},{9,... | collective-permute-start | bytes 884744 | tf_op jit(solution)/shard_map/ppermute | solution.py:35
  17.0 1.1 %collective-permute-start.10 = (bf16[256,1152]{1,0:T(8,128)(2,1)S(1)}, bf16[256,1152]{1,0:T(8,128)(2,1)S(1)}, u32[]{:S(2)}, u32[]{:S(2)}) collective-permute-start(bf16[256,1152]{1,0:T(8,128)(2,1)S(1)} %pad_maximum_fusion), channel_id=1, source_target_pairs={{0,16},{1,17},{2,18},{3,19},{4,20},{5,21},{6,22},{7,23},{8,24},{9,... | collective-permute-start | bytes 1769480 | tf_op jit(solution)/shard_map/ppermute | solution.py:35
  18.2 1.7 %near.1 = (f32[256,1152]{1,0:T(8,128)S(1)}, f32[256,1152]{1,0:T(8,128)S(1)}) custom-call(f32[32,128]{1,0:T(8,128)S(1)} %consts.1.after, bf16[128,1152]{1,0:T(8,128)(2,1)S(1)} %gate.4.back_first, bf16[128,1152]{1,0:T(8,128)(2,1)S(1)} %collective-permute-done.3.back_second, bf16[128,1152]{1,0:T(8,128)(2,1)S(1)} %collective-permute-done.4.ahead_first, ...), custom_call_target="tpu_custom_call" | custom-call | flops 1 | bytes 1 | tf_op jit(solution)/shard_map/near/pallas_call | solution.py:74
  19.9 1.8 %collective-permute-start.11 = (bf16[128,1152]{1,0:T(8,128)(2,1)S(1)}, bf16[128,1152]{1,0:T(8,128)(2,1)S(1)}, u32[]{:S(2)}, u32[]{:S(2)}) collective-permute-start(bf16[128,1152]{1,0:T(8,128)(2,1)S(1)} %gate.6.far_first), channel_id=1, source_target_pairs={{0,16},{1,17},{2,18},{3,19},{4,20},{5,21},{6,22},{7,23},{8,24},{9,... | collective-permute-start | bytes 884744 | tf_op jit(solution)/shard_map/ppermute | solution.py:35
  21.9 1.5 %far_near.1.part = f32[256,1152]{1,0:T(8,128)S(1)} custom-call(f32[32,128]{1,0:T(8,128)S(1)} %consts.1.after, bf16[128,1152]{1,0:T(8,128)(2,1)S(1)} %gate.6.far_first, bf16[128,1152]{1,0:T(8,128)(2,1)S(1)} %gate.7.far_second, bf16[128,1152]{1,0:T(8,128)(2,1)S(1)} %get-tuple-element.20.other, ...), custom_call_target="tpu_custom_call" | custom-call | flops 1 | bytes 1 | tf_op jit(solution)/shard_map/far_near/pallas_call | solution.py:74
  23.5 0.8 %far.1 = (bf16[128,1152]{1,0:T(8,128)(2,1)S(1)}, bf16[128,1152]{1,0:T(8,128)(2,1)S(1)}) custom-call(f32[32,128]{1,0:T(8,128)S(1)} %consts.1.after, f32[256,1152]{1,0:T(8,128)S(1)} %far_near.1.part, bf16[128,1152]{1,0:T(8,128)(2,1)S(1)} %gate.6.far_first, bf16[128,1152]{1,0:T(8,128)(2,1)S(1)} %gate.7.far_second, ...), custom_call_target="tpu_custom_call" | custom-call | flops 301989888 | bytes 1 | tf_op jit(solution)/shard_map/far/pallas_call | solution.py:74
  24.3 0.3 collective-permute-start.17
  24.6 2.7 %collective-permute-start.13 = (bf16[128,1152]{1,0:T(8,128)(2,1)S(1)}, bf16[128,1152]{1,0:T(8,128)(2,1)S(1)}, u32[]{:S(2)}, u32[]{:S(2)}) collective-permute-start(bf16[128,1152]{1,0:T(8,128)(2,1)S(1)} %get-tuple-element.27.after), channel_id=1, source_target_pairs={{0,3},{1,0},{2,1},{3,2},{4,7},{5,4},{6,5},{7,6},{8,11},{9,8},{10,9... | collective-permute-start | bytes 884744 | tf_op jit(solution)/shard_map/ppermute | solution.py:35
  27.3 1.7 %rest.1 = (f32[128,1152]{1,0:T(8,128)S(1)}, bf16[128,1152]{1,0:T(8,128)(2,1)S(1)}, bf16[128,1152]{1,0:T(8,128)(2,1)S(1)}, f32[128,1152]{1,0:T(8,128)S(1)}) custom-call(f32[32,128]{1,0:T(8,128)S(1)} %consts.1.after, f32[256,1152]{1,0:T(8,128)S(1)} %get-tuple-element.23.after.part_back, f32[256,1152]{1,0:T(8,128)S(1)} %get-tuple-element.26.part_ahead, ...), custom_call_target="tpu_custom_call" | custom-call | flops 1 | bytes 1 | tf_op jit(solution)/shard_map/rest/pallas_call | solution.py:74
  29.1 2.0 %collective-permute-start.16 = (bf16[128,1152]{1,0:T(8,128)(2,1)S(1)}, bf16[128,1152]{1,0:T(8,128)(2,1)S(1)}, u32[]{:S(2)}, u32[]{:S(2)}) collective-permute-start(bf16[128,1152]{1,0:T(8,128)(2,1)S(1)} %get-tuple-element.35), channel_id=1, source_target_pairs={{0,19},{1,16},{2,17},{3,18},{4,23},{5,20},{6,21},{7,22},{8,27},{9,... | collective-permute-start | bytes 884744 | tf_op jit(solution)/shard_map/ppermute | solution.py:35
  31.1 0.6 %collective-permute-done.17.got = bf16[128,1152]{1,0:T(8,128)(2,1)S(1)} collective-permute-done((bf16[128,1152]{1,0:T(8,128)(2,1)S(1)}, bf16[128,1152]{1,0:T(8,128)(2,1)S(1)}, u32[]{:S(2)}, u32[]{:S(2)}) %collective-permute-start.17) | collective-permute-done | bytes 294944 | tf_op jit(solution)/shard_map/ppermute | solution.py:35
  31.7 1.2 %collective-permute-start.18 = (bf16[128,1152]{1,0:T(8,128)(2,1)S(1)}, bf16[128,1152]{1,0:T(8,128)(2,1)S(1)}, u32[]{:S(2)}, u32[]{:S(2)}) collective-permute-start(bf16[128,1152]{1,0:T(8,128)(2,1)S(1)} %relay.3), channel_id=1, source_target_pairs={{0,17},{1,18},{2,19},{3,16},{4,21},{5,22},{6,23},{7,20},{8,25},{9,... | collective-permute-start | bytes 884744 | tf_op jit(solution)/shard_map/ppermute | solution.py:35
  33.0 2.8 %collective-permute-start.15 = (bf16[128,1152]{1,0:T(8,128)(2,1)S(1)}, bf16[128,1152]{1,0:T(8,128)(2,1)S(1)}, u32[]{:S(2)}, u32[]{:S(2)}) collective-permute-start(bf16[128,1152]{1,0:T(8,128)(2,1)S(1)} %relay.2.after), channel_id=1, source_target_pairs={{0,3},{1,0},{2,1},{3,2},{4,7},{5,4},{6,5},{7,6},{8,11},{9,8},{10,9... | collective-permute-start | bytes 884744 | tf_op jit(solution)/shard_map/ppermute | solution.py:35
  35.8 3.6 %own.1 = (f32[128,1152]{1,0:T(8,128)S(1)}, f32[128,1152]{1,0:T(8,128)S(1)}, f32[128,1152]{1,0:T(8,128)S(1)}, f32[128,1]{1,0:T(8,128)S(1)}) custom-call(f32[32,128]{1,0:T(8,128)S(1)} %consts.1.after, bf16[128,1152]{1,0:T(8,128)(2,1)S(1)} %get-tuple-element.21.first, bf16[128,1152]{1,0:T(8,128)(2,1)S(1)} %collective-permute-done.after.second, ...), custom_call_target="tpu_custom_call" | custom-call | flops 1 | bytes 1 | tf_op jit(solution)/shard_map/own/pallas_call | solution.py:74
  39.5 1.0 %collective-permute-done.18.their_two = bf16[128,1152]{1,0:T(8,128)(2,1)S(1)} collective-permute-done((bf16[128,1152]{1,0:T(8,128)(2,1)S(1)}, bf16[128,1152]{1,0:T(8,128)(2,1)S(1)}, u32[]{:S(2)}, u32[]{:S(2)}) %collective-permute-start.18) | collective-permute-done | bytes 294944 | tf_op jit(solution)/shard_map/ppermute | solution.py:35
  40.5 1.5 %last.1 = (f32[128,1152]{1,0:T(8,128)}, f32[128,1152]{1,0:T(8,128)}) custom-call(s32[1]{0:T(128)} %bitcast.core, f32[32,128]{1,0:T(8,128)S(1)} %consts.1.after, f32[128,1152]{1,0:T(8,128)S(1)} %get-tuple-element.24.after.unit_own, f32[128,1]{1,0:T(8,128)S(1)} %get-tuple-element.25.length_own, f32[128,1152]{1,0:T(8,128)S(1)} %get-tuple-element.30.unit_their, ...), custom_call_target="tpu_custom_call" | custom-call | flops 1 | bytes 1 | tf_op jit(solution)/shard_map/last/pallas_call | solution.py:74
  (35 shorter events, 0.9 us)
Async XLA Ops:
  1.9 6.7 %collective-permute-start.1 = (bf16[128,1152]{1,0:T(8,128)(2,1)S(1)}, bf16[128,1152]{1,0:T(8,128)(2,1)S(1)}, u32[]{:S(2)}, u32[]{:S(2)}) collective-permute-start(bf16[128,1152]{1,0:T(8,128)(2,1)S(1)} %get-tuple-element.21.first), channel_id=1, source_target_pairs={{0,16},{1,17},{2,18},{3,19},{4,20},{5,21},{6,22},{7,23},{8,24},{9,... | collective-permute-start | bytes 884744 | tf_op jit(solution)/shard_map/ppermute | solution.py:35
  5.3 3.9 %collective-permute-start = (bf16[128,1152]{1,0:T(8,128)(2,1)S(1)}, bf16[128,1152]{1,0:T(8,128)(2,1)S(1)}, u32[]{:S(2)}, u32[]{:S(2)}) collective-permute-start(bf16[128,1152]{1,0:T(8,128)(2,1)S(1)} %get-tuple-element.20.other), channel_id=1, source_target_pairs={{0,16},{1,17},{2,18},{3,19},{4,20},{5,21},{6,22},{7,23},{8,24},{9,... | collective-permute-start | bytes 884744 | tf_op jit(solution)/shard_map/ppermute | solution.py:35
  5.4 7.1 %collective-permute-start.2 = (bf16[128,1152]{1,0:T(8,128)(2,1)S(1)}, bf16[128,1152]{1,0:T(8,128)(2,1)S(1)}, u32[]{:S(2)}, u32[]{:S(2)}) collective-permute-start(bf16[128,1152]{1,0:T(8,128)(2,1)S(1)} %get-tuple-element.21.first), channel_id=1, source_target_pairs={{0,1},{1,2},{2,3},{3,0},{4,5},{5,6},{6,7},{7,4},{8,9},{9,10},{10,1... | collective-permute-start | bytes 884744 | tf_op jit(solution)/shard_map/ppermute | solution.py:35
  5.4 8.6 %collective-permute-start.5 = (bf16[128,1152]{1,0:T(8,128)(2,1)S(1)}, bf16[128,1152]{1,0:T(8,128)(2,1)S(1)}, u32[]{:S(2)}, u32[]{:S(2)}) collective-permute-start(bf16[128,1152]{1,0:T(8,128)(2,1)S(1)} %get-tuple-element.20.other), channel_id=1, source_target_pairs={{0,28},{1,29},{2,30},{3,31},{4,16},{5,17},{6,18},{7,19},{8,20},{9,... | collective-permute-start | bytes 884744 | tf_op jit(solution)/shard_map/ppermute | solution.py:35
  8.6 7.1 %collective-permute-start.4 = (bf16[128,1152]{1,0:T(8,128)(2,1)S(1)}, bf16[128,1152]{1,0:T(8,128)(2,1)S(1)}, u32[]{:S(2)}, u32[]{:S(2)}) collective-permute-start(bf16[128,1152]{1,0:T(8,128)(2,1)S(1)} %collective-permute-done.1.after_too.other_second), channel_id=1, source_target_pairs={{0,28},{1,29},{2,30},{3,31},{4,16},{5,17},{6,18},{7,19},{8,20},{9,... | collective-permute-start | bytes 884744 | tf_op jit(solution)/shard_map/ppermute | solution.py:35
  9.1 7.8 %collective-permute-start.3 = (bf16[128,1152]{1,0:T(8,128)(2,1)S(1)}, bf16[128,1152]{1,0:T(8,128)(2,1)S(1)}, u32[]{:S(2)}, u32[]{:S(2)}) collective-permute-start(bf16[128,1152]{1,0:T(8,128)(2,1)S(1)} %collective-permute-done.after.second), channel_id=1, source_target_pairs={{0,1},{1,2},{2,3},{3,0},{4,5},{5,6},{6,7},{7,4},{8,9},{9,10},{10,1... | collective-permute-start | bytes 884744 | tf_op jit(solution)/shard_map/ppermute | solution.py:35
  12.5 7.4 %collective-permute-start.8 = (bf16[128,1152]{1,0:T(8,128)(2,1)S(1)}, bf16[128,1152]{1,0:T(8,128)(2,1)S(1)}, u32[]{:S(2)}, u32[]{:S(2)}) collective-permute-start(bf16[128,1152]{1,0:T(8,128)(2,1)S(1)} %gate.4.back_first), channel_id=1, source_target_pairs={{0,1},{1,2},{2,3},{3,0},{4,5},{5,6},{6,7},{7,4},{8,9},{9,10},{10,1... | collective-permute-start | bytes 884744 | tf_op jit(solution)/shard_map/ppermute | solution.py:35
  12.7 5.4 %collective-permute-start.6 = (bf16[128,1152]{1,0:T(8,128)(2,1)S(1)}, bf16[128,1152]{1,0:T(8,128)(2,1)S(1)}, u32[]{:S(2)}, u32[]{:S(2)}) collective-permute-start(bf16[128,1152]{1,0:T(8,128)(2,1)S(1)} %gate.4.back_first), channel_id=1, source_target_pairs={{0,16},{1,17},{2,18},{3,19},{4,20},{5,21},{6,22},{7,23},{8,24},{9,... | collective-permute-start | bytes 884744 | tf_op jit(solution)/shard_map/ppermute | solution.py:35
  14.0 7.8 %collective-permute-start.9 = (bf16[128,1152]{1,0:T(8,128)(2,1)S(1)}, bf16[128,1152]{1,0:T(8,128)(2,1)S(1)}, u32[]{:S(2)}, u32[]{:S(2)}) collective-permute-start(bf16[128,1152]{1,0:T(8,128)(2,1)S(1)} %gate.5.ahead_second), channel_id=1, source_target_pairs={{0,3},{1,0},{2,1},{3,2},{4,7},{5,4},{6,5},{7,6},{8,11},{9,8},{10,9... | collective-permute-start | bytes 884744 | tf_op jit(solution)/shard_map/ppermute | solution.py:35
  15.7 2.5 %collective-permute-start.7 = (bf16[128,1152]{1,0:T(8,128)(2,1)S(1)}, bf16[128,1152]{1,0:T(8,128)(2,1)S(1)}, u32[]{:S(2)}, u32[]{:S(2)}) collective-permute-start(bf16[128,1152]{1,0:T(8,128)(2,1)S(1)} %gate.5.ahead_second), channel_id=1, source_target_pairs={{0,16},{1,17},{2,18},{3,19},{4,20},{5,21},{6,22},{7,23},{8,24},{9,... | collective-permute-start | bytes 884744 | tf_op jit(solution)/shard_map/ppermute | solution.py:35
  17.0 4.9 %collective-permute-start.10 = (bf16[256,1152]{1,0:T(8,128)(2,1)S(1)}, bf16[256,1152]{1,0:T(8,128)(2,1)S(1)}, u32[]{:S(2)}, u32[]{:S(2)}) collective-permute-start(bf16[256,1152]{1,0:T(8,128)(2,1)S(1)} %pad_maximum_fusion), channel_id=1, source_target_pairs={{0,16},{1,17},{2,18},{3,19},{4,20},{5,21},{6,22},{7,23},{8,24},{9,... | collective-permute-start | bytes 1769480 | tf_op jit(solution)/shard_map/ppermute | solution.py:35
  19.9 3.6 %collective-permute-start.11 = (bf16[128,1152]{1,0:T(8,128)(2,1)S(1)}, bf16[128,1152]{1,0:T(8,128)(2,1)S(1)}, u32[]{:S(2)}, u32[]{:S(2)}) collective-permute-start(bf16[128,1152]{1,0:T(8,128)(2,1)S(1)} %gate.6.far_first), channel_id=1, source_target_pairs={{0,16},{1,17},{2,18},{3,19},{4,20},{5,21},{6,22},{7,23},{8,24},{9,... | collective-permute-start | bytes 884744 | tf_op jit(solution)/shard_map/ppermute | solution.py:35
  21.8 1.7 %collective-permute-start.12 = (bf16[128,1152]{1,0:T(8,128)(2,1)S(1)}, bf16[128,1152]{1,0:T(8,128)(2,1)S(1)}, u32[]{:S(2)}, u32[]{:S(2)}) collective-permute-start(bf16[128,1152]{1,0:T(8,128)(2,1)S(1)} %gate.7.far_second), channel_id=1, source_target_pairs={{0,16},{1,17},{2,18},{3,19},{4,20},{5,21},{6,22},{7,23},{8,24},{9,... | collective-permute-start | bytes 884744 | tf_op jit(solution)/shard_map/ppermute | solution.py:35
  24.3 7.3 %collective-permute-start.17 = (bf16[128,1152]{1,0:T(8,128)(2,1)S(1)}, bf16[128,1152]{1,0:T(8,128)(2,1)S(1)}, u32[]{:S(2)}, u32[]{:S(2)}) collective-permute-start(bf16[128,1152]{1,0:T(8,128)(2,1)S(1)} %get-tuple-element.37), channel_id=1, source_target_pairs={{0,1},{1,2},{2,3},{3,0},{4,5},{5,6},{6,7},{7,4},{8,9},{9,10},{10,1... | collective-permute-start | bytes 884744 | tf_op jit(solution)/shard_map/ppermute | solution.py:35
  24.6 8.3 %collective-permute-start.13 = (bf16[128,1152]{1,0:T(8,128)(2,1)S(1)}, bf16[128,1152]{1,0:T(8,128)(2,1)S(1)}, u32[]{:S(2)}, u32[]{:S(2)}) collective-permute-start(bf16[128,1152]{1,0:T(8,128)(2,1)S(1)} %get-tuple-element.27.after), channel_id=1, source_target_pairs={{0,3},{1,0},{2,1},{3,2},{4,7},{5,4},{6,5},{7,6},{8,11},{9,8},{10,9... | collective-permute-start | bytes 884744 | tf_op jit(solution)/shard_map/ppermute | solution.py:35
  29.0 10.5 %collective-permute-start.14 = (bf16[128,1152]{1,0:T(8,128)(2,1)S(1)}, bf16[128,1152]{1,0:T(8,128)(2,1)S(1)}, u32[]{:S(2)}, u32[]{:S(2)}) collective-permute-start(bf16[128,1152]{1,0:T(8,128)(2,1)S(1)} %get-tuple-element.33), channel_id=1, source_target_pairs={{0,1},{1,2},{2,3},{3,0},{4,5},{5,6},{6,7},{7,4},{8,9},{9,10},{10,1... | collective-permute-start | bytes 884744 | tf_op jit(solution)/shard_map/ppermute | solution.py:35
  29.1 10.4 %collective-permute-start.16 = (bf16[128,1152]{1,0:T(8,128)(2,1)S(1)}, bf16[128,1152]{1,0:T(8,128)(2,1)S(1)}, u32[]{:S(2)}, u32[]{:S(2)}) collective-permute-start(bf16[128,1152]{1,0:T(8,128)(2,1)S(1)} %get-tuple-element.35), channel_id=1, source_target_pairs={{0,19},{1,16},{2,17},{3,18},{4,23},{5,20},{6,21},{7,22},{8,27},{9,... | collective-permute-start | bytes 884744 | tf_op jit(solution)/shard_map/ppermute | solution.py:35
  31.7 8.8 %collective-permute-start.18 = (bf16[128,1152]{1,0:T(8,128)(2,1)S(1)}, bf16[128,1152]{1,0:T(8,128)(2,1)S(1)}, u32[]{:S(2)}, u32[]{:S(2)}) collective-permute-start(bf16[128,1152]{1,0:T(8,128)(2,1)S(1)} %relay.3), channel_id=1, source_target_pairs={{0,17},{1,18},{2,19},{3,16},{4,21},{5,22},{6,23},{7,20},{8,25},{9,... | collective-permute-start | bytes 884744 | tf_op jit(solution)/shard_map/ppermute | solution.py:35
  33.0 7.5 %collective-permute-start.15 = (bf16[128,1152]{1,0:T(8,128)(2,1)S(1)}, bf16[128,1152]{1,0:T(8,128)(2,1)S(1)}, u32[]{:S(2)}, u32[]{:S(2)}) collective-permute-start(bf16[128,1152]{1,0:T(8,128)(2,1)S(1)} %relay.2.after), channel_id=1, source_target_pairs={{0,3},{1,0},{2,1},{3,2},{4,7},{5,4},{6,5},{7,6},{8,11},{9,8},{10,9... | collective-permute-start | bytes 884744 | tf_op jit(solution)/shard_map/ppermute | solution.py:35

commit v6 on v5

--- a/solution.py
+++ b/solution.py
@@ -85,7 +85,7 @@
     return (values / length, length)
 
 
-def rows_kernel(core, image, text, first, other, raw_first, raw_other, sems):
+def rows_kernel(core, image, text, first, other, both, raw_first, raw_other, sems):
 
     @pl.when(core[0] == 0)
     def _():
@@ -99,8 +99,16 @@
 
     pltpu.make_async_copy(image, raw_first, sems.at[0]).wait()
     first[...] = unit_rows(raw_first[...])[0].astype(jnp.bfloat16)
+    both[: first.shape[0]] = first[...]
     pltpu.make_async_copy(text, raw_other, sems.at[1]).wait()
     other[...] = unit_rows(raw_other[...])[0].astype(jnp.bfloat16)
+    both[first.shape[0] :] = other[...]
+
+
+def halves_kernel(both, up, down):
+    rows = up.shape[0]
+    up[...] = both[:rows]
+    down[...] = both[rows:]
 
 
 def consts_kernel(numbers, after, after_too, consts):
@@ -235,15 +243,16 @@
     half = jax.ShapeDtypeStruct((rows, width), jnp.bfloat16)
     full = jax.ShapeDtypeStruct((rows, width), jnp.float32)
     double = jax.ShapeDtypeStruct((2 * rows, width), jnp.float32)
+    pair = jax.ShapeDtypeStruct((2 * rows, width), jnp.bfloat16)
     core = (lax.axis_index("grp") % 2).astype(jnp.int32).reshape(1)
     numbers = jnp.concatenate(
         [jnp.broadcast_to(value, (8, 128)) for value in (scale_logarithm, logit_bias, loss_grad)], 0
     )
     unit = 2 * rows * rows * width
 
-    first, other, raw_first, raw_other = call(
+    first, other, both, raw_first, raw_other = call(
         rows_kernel,
-        [half, half, half, half],
+        [half, half, pair, half, half],
         [SMEM, HBM, HBM],
         10**8,
         "rows",
@@ -252,8 +261,7 @@
 
     back_first = hop(first, 1)
     ahead_second = cross(other, -1)
-    other_second = swap(first)
-    second = swap(other)
+    other_second, second = call(halves_kernel, [half, half], [VMEM], 1, "halves")(swap(both))
     (consts,) = call(consts_kernel, [jax.ShapeDtypeStruct((32, 128), jnp.float32)], [VMEM] * 3, 1, "consts")(
         numbers, second, other_second
     )

time: 42.3 us -> 42.3 us (level)
  starting transfers between devices: 23.7 us -> 23 us
  waiting for transfers between devices: 2.92 us -> 3.35 us
    ppermute x19 -> x18, starting transfers between devices: 23.7 us -> 23 us  [moved(): return lax.ppermute(value, AXES, pairs)]
    ppermute x19 -> x18, waiting for transfers between devices: 2.92 us -> 3.35 us  [moved(): return lax.ppermute(value, AXES, pairs)]
    pallas_call x11 -> x12, Pallas kernels: 12.5 us -> 12.6 us  [call(): run(*[pltpu.with_memory_space_constraint(a, pltpu.VMEM if s is VMEM else...]
  transfers between devices with their start and end apart: 19 -> 18, of which waited for: 4 -> 4; matrix products, arithmetic and copies ran while one was open for 0% -> 0% of each run, Pallas kernels for 21% -> 21%
where the time goes in v6:
time: 42.3 us; the launch traced here: 42.1 us
  starting transfers between devices  23 us (54%)
  Pallas kernels  12.6 us (30%)
  waiting for transfers between devices  3.35 us (8%)
  between operations  2.95 us (7%)
    ppermute x18, starting transfers between devices, moved(): return lax.ppermute(value, AXES, pairs)  23 us
    pallas_call x12, Pallas kernels, call(): run(*[pltpu.with_memory_space_constraint(a, pltpu.VMEM if s is VMEM else...  12.6 us
    ppermute x18, waiting for transfers between devices, moved(): return lax.ppermute(value, AXES, pairs)  3.35 us
  transfers between devices with their start and end apart: 18, of which 4 were waited for; matrix products, arithmetic and copies ran while one was open for 0% of the time, Pallas kernels for 21%

profile of v6, /device:TPU:1, one launch (start us, length us, event | category | flops | bytes accessed | tf_op | source)
XLA Modules:
  0.0 42.1 jit_solution(15997530935183026173)
XLA Ops:
  0.6 1.4 %rows.1 = (bf16[128,1152]{1,0:T(8,128)(2,1)S(1)}, bf16[128,1152]{1,0:T(8,128)(2,1)S(1)}, bf16[256,1152]{1,0:T(8,128)(2,1)S(1)}, bf16[128,1152]{1,0:T(8,128)(2,1)S(1)}, bf16[128,1152]{1,0:T(8,128)(2,1)S(1)}) custom-call(s32[1]{0:T(128)} %bitcast.core, bf16[128,1152]{1,0:T(8,128)(2,1)} %image.1, bf16[128,1152]{1,0:T(8,128)(2,1)} %text.1), custom_call_target="tpu_custom_call" | custom-call | flops 100000000 | bytes 1 | tf_op jit(solution)/shard_map/rows/pallas_call | solution.py:74
  2.0 3.3 %collective-permute-start = (bf16[256,1152]{1,0:T(8,128)(2,1)S(1)}, bf16[256,1152]{1,0:T(8,128)(2,1)S(1)}, u32[]{:S(2)}, u32[]{:S(2)}) collective-permute-start(bf16[256,1152]{1,0:T(8,128)(2,1)S(1)} %get-tuple-element.23), channel_id=1, source_target_pairs={{0,16},{1,17},{2,18},{3,19},{4,20},{5,21},{6,22},{7,23},{8,24},{9,... | collective-permute-start | bytes 1769480 | tf_op jit(solution)/shard_map/ppermute | solution.py:35
  5.3 2.9 %collective-permute-start.4 = (bf16[128,1152]{1,0:T(8,128)(2,1)S(1)}, bf16[128,1152]{1,0:T(8,128)(2,1)S(1)}, u32[]{:S(2)}, u32[]{:S(2)}) collective-permute-start(bf16[128,1152]{1,0:T(8,128)(2,1)S(1)} %get-tuple-element.28.other), channel_id=1, source_target_pairs={{0,28},{1,29},{2,30},{3,31},{4,16},{5,17},{6,18},{7,19},{8,20},{9,... | collective-permute-start | bytes 884744 | tf_op jit(solution)/shard_map/ppermute | solution.py:35
  8.4 3.0 %collective-permute-start.3 = (bf16[128,1152]{1,0:T(8,128)(2,1)S(1)}, bf16[128,1152]{1,0:T(8,128)(2,1)S(1)}, u32[]{:S(2)}, u32[]{:S(2)}) collective-permute-start(bf16[128,1152]{1,0:T(8,128)(2,1)S(1)} %get-tuple-element.25.after_too.other_second), channel_id=1, source_target_pairs={{0,28},{1,29},{2,30},{3,31},{4,16},{5,17},{6,18},{7,19},{8,20},{9,... | collective-permute-start | bytes 884744 | tf_op jit(solution)/shard_map/ppermute | solution.py:35
  13.6 0.2 collective-permute-start.5
  13.8 2.5 %collective-permute-start.8 = (bf16[128,1152]{1,0:T(8,128)(2,1)S(1)}, bf16[128,1152]{1,0:T(8,128)(2,1)S(1)}, u32[]{:S(2)}, u32[]{:S(2)}) collective-permute-start(bf16[128,1152]{1,0:T(8,128)(2,1)S(1)} %gate.5.ahead_second), channel_id=1, source_target_pairs={{0,3},{1,0},{2,1},{3,2},{4,7},{5,4},{6,5},{7,6},{8,11},{9,8},{10,9... | collective-permute-start | bytes 884744 | tf_op jit(solution)/shard_map/ppermute | solution.py:35
  16.3 0.7 %collective-permute-start.6 = (bf16[128,1152]{1,0:T(8,128)(2,1)S(1)}, bf16[128,1152]{1,0:T(8,128)(2,1)S(1)}, u32[]{:S(2)}, u32[]{:S(2)}) collective-permute-start(bf16[128,1152]{1,0:T(8,128)(2,1)S(1)} %gate.5.ahead_second), channel_id=1, source_target_pairs={{0,16},{1,17},{2,18},{3,19},{4,20},{5,21},{6,22},{7,23},{8,24},{9,... | collective-permute-start | bytes 884744 | tf_op jit(solution)/shard_map/ppermute | solution.py:35
  17.1 1.0 %collective-permute-done.6.near_second = bf16[128,1152]{1,0:T(8,128)(2,1)S(1)} collective-permute-done((bf16[128,1152]{1,0:T(8,128)(2,1)S(1)}, bf16[128,1152]{1,0:T(8,128)(2,1)S(1)}, u32[]{:S(2)}, u32[]{:S(2)}) %collective-permute-start.6) | collective-permute-done | bytes 294944 | tf_op jit(solution)/shard_map/ppermute | solution.py:35
  18.1 1.7 %near.1 = (f32[256,1152]{1,0:T(8,128)S(1)}, f32[256,1152]{1,0:T(8,128)S(1)}) custom-call(f32[32,128]{1,0:T(8,128)S(1)} %consts.1.after, bf16[128,1152]{1,0:T(8,128)(2,1)S(1)} %gate.4.back_first, bf16[128,1152]{1,0:T(8,128)(2,1)S(1)} %collective-permute-done.2.back_second, bf16[128,1152]{1,0:T(8,128)(2,1)S(1)} %collective-permute-done.3.ahead_first, ...), custom_call_target="tpu_custom_call" | custom-call | flops 1 | bytes 1 | tf_op jit(solution)/shard_map/near/pallas_call | solution.py:74
  19.8 0.8 %collective-permute-done.7.value = bf16[128,1152]{1,0:T(8,128)(2,1)S(1)} collective-permute-done((bf16[128,1152]{1,0:T(8,128)(2,1)S(1)}, bf16[128,1152]{1,0:T(8,128)(2,1)S(1)}, u32[]{:S(2)}, u32[]{:S(2)}) %collective-permute-start.7) | collective-permute-done | bytes 294944 | tf_op jit(solution)/shard_map/ppermute | solution.py:35
  20.7 0.9 %collective-permute-start.10 = (bf16[128,1152]{1,0:T(8,128)(2,1)S(1)}, bf16[128,1152]{1,0:T(8,128)(2,1)S(1)}, u32[]{:S(2)}, u32[]{:S(2)}) collective-permute-start(bf16[128,1152]{1,0:T(8,128)(2,1)S(1)} %gate.6.far_first), channel_id=1, source_target_pairs={{0,16},{1,17},{2,18},{3,19},{4,20},{5,21},{6,22},{7,23},{8,24},{9,... | collective-permute-start | bytes 884744 | tf_op jit(solution)/shard_map/ppermute | solution.py:35
  21.6 0.2 units.1
  21.9 1.5 %far_near.1.part = f32[256,1152]{1,0:T(8,128)S(1)} custom-call(f32[32,128]{1,0:T(8,128)S(1)} %consts.1.after, bf16[128,1152]{1,0:T(8,128)(2,1)S(1)} %gate.6.far_first, bf16[128,1152]{1,0:T(8,128)(2,1)S(1)} %gate.7.far_second, bf16[128,1152]{1,0:T(8,128)(2,1)S(1)} %get-tuple-element.28.other, bf16[128,1152]{1,0:T(8,128)(2,1)S(1)} %get-tuple-element.25.after_too.other_second, ...), custom_call_target="tpu_custom_call" | custom-call | flops 1 | bytes 1 | tf_op jit(solution)/shard_map/far_near/pallas_call | solution.py:74
  23.5 0.8 %far.1 = (bf16[128,1152]{1,0:T(8,128)(2,1)S(1)}, bf16[128,1152]{1,0:T(8,128)(2,1)S(1)}) custom-call(f32[32,128]{1,0:T(8,128)S(1)} %consts.1.after, f32[256,1152]{1,0:T(8,128)S(1)} %far_near.1.part, bf16[128,1152]{1,0:T(8,128)(2,1)S(1)} %gate.6.far_first, bf16[128,1152]{1,0:T(8,128)(2,1)S(1)} %gate.7.far_second, ...), custom_call_target="tpu_custom_call" | custom-call | flops 301989888 | bytes 1 | tf_op jit(solution)/shard_map/far/pallas_call | solution.py:74
  24.3 0.3 collective-permute-start.16
  24.6 2.7 %collective-permute-start.12 = (bf16[128,1152]{1,0:T(8,128)(2,1)S(1)}, bf16[128,1152]{1,0:T(8,128)(2,1)S(1)}, u32[]{:S(2)}, u32[]{:S(2)}) collective-permute-start(bf16[128,1152]{1,0:T(8,128)(2,1)S(1)} %get-tuple-element.33.after), channel_id=1, source_target_pairs={{0,3},{1,0},{2,1},{3,2},{4,7},{5,4},{6,5},{7,6},{8,11},{9,8},{10,9... | collective-permute-start | bytes 884744 | tf_op jit(solution)/shard_map/ppermute | solution.py:35
  27.2 1.7 %rest.1 = (f32[128,1152]{1,0:T(8,128)S(1)}, bf16[128,1152]{1,0:T(8,128)(2,1)S(1)}, bf16[128,1152]{1,0:T(8,128)(2,1)S(1)}, f32[128,1152]{1,0:T(8,128)S(1)}) custom-call(f32[32,128]{1,0:T(8,128)S(1)} %consts.1.after, f32[256,1152]{1,0:T(8,128)S(1)} %get-tuple-element.29.after.part_back, f32[256,1152]{1,0:T(8,128)S(1)} %get-tuple-element.32.part_ahead, ...), custom_call_target="tpu_custom_call" | custom-call | flops 1 | bytes 1 | tf_op jit(solution)/shard_map/rest/pallas_call | solution.py:74
  29.1 2.2 %collective-permute-start.15 = (bf16[128,1152]{1,0:T(8,128)(2,1)S(1)}, bf16[128,1152]{1,0:T(8,128)(2,1)S(1)}, u32[]{:S(2)}, u32[]{:S(2)}) collective-permute-start(bf16[128,1152]{1,0:T(8,128)(2,1)S(1)} %get-tuple-element.41), channel_id=1, source_target_pairs={{0,19},{1,16},{2,17},{3,18},{4,23},{5,20},{6,21},{7,22},{8,27},{9,... | collective-permute-start | bytes 884744 | tf_op jit(solution)/shard_map/ppermute | solution.py:35
  31.2 0.4 %collective-permute-done.16.got = bf16[128,1152]{1,0:T(8,128)(2,1)S(1)} collective-permute-done((bf16[128,1152]{1,0:T(8,128)(2,1)S(1)}, bf16[128,1152]{1,0:T(8,128)(2,1)S(1)}, u32[]{:S(2)}, u32[]{:S(2)}) %collective-permute-start.16) | collective-permute-done | bytes 294944 | tf_op jit(solution)/shard_map/ppermute | solution.py:35
  31.7 0.5 %collective-permute-start.17 = (bf16[128,1152]{1,0:T(8,128)(2,1)S(1)}, bf16[128,1152]{1,0:T(8,128)(2,1)S(1)}, u32[]{:S(2)}, u32[]{:S(2)}) collective-permute-start(bf16[128,1152]{1,0:T(8,128)(2,1)S(1)} %relay.3), channel_id=1, source_target_pairs={{0,17},{1,18},{2,19},{3,16},{4,21},{5,22},{6,23},{7,20},{8,25},{9,... | collective-permute-start | bytes 884744 | tf_op jit(solution)/shard_map/ppermute | solution.py:35
  32.3 3.5 %collective-permute-start.14 = (bf16[128,1152]{1,0:T(8,128)(2,1)S(1)}, bf16[128,1152]{1,0:T(8,128)(2,1)S(1)}, u32[]{:S(2)}, u32[]{:S(2)}) collective-permute-start(bf16[128,1152]{1,0:T(8,128)(2,1)S(1)} %relay.2.after), channel_id=1, source_target_pairs={{0,3},{1,0},{2,1},{3,2},{4,7},{5,4},{6,5},{7,6},{8,11},{9,8},{10,9... | collective-permute-start | bytes 884744 | tf_op jit(solution)/shard_map/ppermute | solution.py:35
  35.8 3.6 %own.1 = (f32[128,1152]{1,0:T(8,128)S(1)}, f32[128,1152]{1,0:T(8,128)S(1)}, f32[128,1152]{1,0:T(8,128)S(1)}, f32[128,1]{1,0:T(8,128)S(1)}) custom-call(f32[32,128]{1,0:T(8,128)S(1)} %consts.1.after, bf16[128,1152]{1,0:T(8,128)(2,1)S(1)} %get-tuple-element.27.first, bf16[128,1152]{1,0:T(8,128)(2,1)S(1)} %get-tuple-element.24.after.second, ...), custom_call_target="tpu_custom_call" | custom-call | flops 1 | bytes 1 | tf_op jit(solution)/shard_map/own/pallas_call | solution.py:74
  39.5 1.0 %collective-permute-done.17.their_two = bf16[128,1152]{1,0:T(8,128)(2,1)S(1)} collective-permute-done((bf16[128,1152]{1,0:T(8,128)(2,1)S(1)}, bf16[128,1152]{1,0:T(8,128)(2,1)S(1)}, u32[]{:S(2)}, u32[]{:S(2)}) %collective-permute-start.17) | collective-permute-done | bytes 294944 | tf_op jit(solution)/shard_map/ppermute | solution.py:35
  40.5 1.5 %last.1 = (f32[128,1152]{1,0:T(8,128)}, f32[128,1152]{1,0:T(8,128)}) custom-call(s32[1]{0:T(128)} %bitcast.core, f32[32,128]{1,0:T(8,128)S(1)} %consts.1.after, f32[128,1152]{1,0:T(8,128)S(1)} %get-tuple-element.30.after.unit_own, f32[128,1]{1,0:T(8,128)S(1)} %get-tuple-element.31.length_own, f32[128,1152]{1,0:T(8,128)S(1)} %get-tuple-element.36.unit_their, ...), custom_call_target="tpu_custom_call" | custom-call | flops 1 | bytes 1 | tf_op jit(solution)/shard_map/last/pallas_call | solution.py:74
  (34 shorter events, 0.9 us)
Async XLA Ops:
  2.0 6.3 %collective-permute-start = (bf16[256,1152]{1,0:T(8,128)(2,1)S(1)}, bf16[256,1152]{1,0:T(8,128)(2,1)S(1)}, u32[]{:S(2)}, u32[]{:S(2)}) collective-permute-start(bf16[256,1152]{1,0:T(8,128)(2,1)S(1)} %get-tuple-element.23), channel_id=1, source_target_pairs={{0,16},{1,17},{2,18},{3,19},{4,20},{5,21},{6,22},{7,23},{8,24},{9,... | collective-permute-start | bytes 1769480 | tf_op jit(solution)/shard_map/ppermute | solution.py:35
  5.3 8.2 %collective-permute-start.1 = (bf16[128,1152]{1,0:T(8,128)(2,1)S(1)}, bf16[128,1152]{1,0:T(8,128)(2,1)S(1)}, u32[]{:S(2)}, u32[]{:S(2)}) collective-permute-start(bf16[128,1152]{1,0:T(8,128)(2,1)S(1)} %get-tuple-element.27.first), channel_id=1, source_target_pairs={{0,1},{1,2},{2,3},{3,0},{4,5},{5,6},{6,7},{7,4},{8,9},{9,10},{10,1... | collective-permute-start | bytes 884744 | tf_op jit(solution)/shard_map/ppermute | solution.py:35
  5.3 8.5 %collective-permute-start.4 = (bf16[128,1152]{1,0:T(8,128)(2,1)S(1)}, bf16[128,1152]{1,0:T(8,128)(2,1)S(1)}, u32[]{:S(2)}, u32[]{:S(2)}) collective-permute-start(bf16[128,1152]{1,0:T(8,128)(2,1)S(1)} %get-tuple-element.28.other), channel_id=1, source_target_pairs={{0,28},{1,29},{2,30},{3,31},{4,16},{5,17},{6,18},{7,19},{8,20},{9,... | collective-permute-start | bytes 884744 | tf_op jit(solution)/shard_map/ppermute | solution.py:35
  8.3 8.0 %collective-permute-start.2 = (bf16[128,1152]{1,0:T(8,128)(2,1)S(1)}, bf16[128,1152]{1,0:T(8,128)(2,1)S(1)}, u32[]{:S(2)}, u32[]{:S(2)}) collective-permute-start(bf16[128,1152]{1,0:T(8,128)(2,1)S(1)} %get-tuple-element.24.after.second), channel_id=1, source_target_pairs={{0,1},{1,2},{2,3},{3,0},{4,5},{5,6},{6,7},{7,4},{8,9},{9,10},{10,1... | collective-permute-start | bytes 884744 | tf_op jit(solution)/shard_map/ppermute | solution.py:35
  8.4 8.5 %collective-permute-start.3 = (bf16[128,1152]{1,0:T(8,128)(2,1)S(1)}, bf16[128,1152]{1,0:T(8,128)(2,1)S(1)}, u32[]{:S(2)}, u32[]{:S(2)}) collective-permute-start(bf16[128,1152]{1,0:T(8,128)(2,1)S(1)} %get-tuple-element.25.after_too.other_second), channel_id=1, source_target_pairs={{0,28},{1,29},{2,30},{3,31},{4,16},{5,17},{6,18},{7,19},{8,20},{9,... | collective-permute-start | bytes 884744 | tf_op jit(solution)/shard_map/ppermute | solution.py:35
  13.5 7.2 %collective-permute-start.7 = (bf16[128,1152]{1,0:T(8,128)(2,1)S(1)}, bf16[128,1152]{1,0:T(8,128)(2,1)S(1)}, u32[]{:S(2)}, u32[]{:S(2)}) collective-permute-start(bf16[128,1152]{1,0:T(8,128)(2,1)S(1)} %gate.4.back_first), channel_id=1, source_target_pairs={{0,1},{1,2},{2,3},{3,0},{4,5},{5,6},{6,7},{7,4},{8,9},{9,10},{10,1... | collective-permute-start | bytes 884744 | tf_op jit(solution)/shard_map/ppermute | solution.py:35
  13.6 3.5 %collective-permute-start.5 = (bf16[128,1152]{1,0:T(8,128)(2,1)S(1)}, bf16[128,1152]{1,0:T(8,128)(2,1)S(1)}, u32[]{:S(2)}, u32[]{:S(2)}) collective-permute-start(bf16[128,1152]{1,0:T(8,128)(2,1)S(1)} %gate.4.back_first), channel_id=1, source_target_pairs={{0,16},{1,17},{2,18},{3,19},{4,20},{5,21},{6,22},{7,23},{8,24},{9,... | collective-permute-start | bytes 884744 | tf_op jit(solution)/shard_map/ppermute | solution.py:35
  13.8 8.0 %collective-permute-start.8 = (bf16[128,1152]{1,0:T(8,128)(2,1)S(1)}, bf16[128,1152]{1,0:T(8,128)(2,1)S(1)}, u32[]{:S(2)}, u32[]{:S(2)}) collective-permute-start(bf16[128,1152]{1,0:T(8,128)(2,1)S(1)} %gate.5.ahead_second), channel_id=1, source_target_pairs={{0,3},{1,0},{2,1},{3,2},{4,7},{5,4},{6,5},{7,6},{8,11},{9,8},{10,9... | collective-permute-start | bytes 884744 | tf_op jit(solution)/shard_map/ppermute | solution.py:35
  16.3 1.9 %collective-permute-start.6 = (bf16[128,1152]{1,0:T(8,128)(2,1)S(1)}, bf16[128,1152]{1,0:T(8,128)(2,1)S(1)}, u32[]{:S(2)}, u32[]{:S(2)}) collective-permute-start(bf16[128,1152]{1,0:T(8,128)(2,1)S(1)} %gate.5.ahead_second), channel_id=1, source_target_pairs={{0,16},{1,17},{2,18},{3,19},{4,20},{5,21},{6,22},{7,23},{8,24},{9,... | collective-permute-start | bytes 884744 | tf_op jit(solution)/shard_map/ppermute | solution.py:35
  17.0 4.9 %collective-permute-start.9 = (bf16[256,1152]{1,0:T(8,128)(2,1)S(1)}, bf16[256,1152]{1,0:T(8,128)(2,1)S(1)}, u32[]{:S(2)}, u32[]{:S(2)}) collective-permute-start(bf16[256,1152]{1,0:T(8,128)(2,1)S(1)} %pad_maximum_fusion), channel_id=1, source_target_pairs={{0,16},{1,17},{2,18},{3,19},{4,20},{5,21},{6,22},{7,23},{8,24},{9,... | collective-permute-start | bytes 1769480 | tf_op jit(solution)/shard_map/ppermute | solution.py:35
  20.7 2.7 %collective-permute-start.10 = (bf16[128,1152]{1,0:T(8,128)(2,1)S(1)}, bf16[128,1152]{1,0:T(8,128)(2,1)S(1)}, u32[]{:S(2)}, u32[]{:S(2)}) collective-permute-start(bf16[128,1152]{1,0:T(8,128)(2,1)S(1)} %gate.6.far_first), channel_id=1, source_target_pairs={{0,16},{1,17},{2,18},{3,19},{4,20},{5,21},{6,22},{7,23},{8,24},{9,... | collective-permute-start | bytes 884744 | tf_op jit(solution)/shard_map/ppermute | solution.py:35
  21.8 1.7 %collective-permute-start.11 = (bf16[128,1152]{1,0:T(8,128)(2,1)S(1)}, bf16[128,1152]{1,0:T(8,128)(2,1)S(1)}, u32[]{:S(2)}, u32[]{:S(2)}) collective-permute-start(bf16[128,1152]{1,0:T(8,128)(2,1)S(1)} %gate.7.far_second), channel_id=1, source_target_pairs={{0,16},{1,17},{2,18},{3,19},{4,20},{5,21},{6,22},{7,23},{8,24},{9,... | collective-permute-start | bytes 884744 | tf_op jit(solution)/shard_map/ppermute | solution.py:35
  24.3 7.3 %collective-permute-start.16 = (bf16[128,1152]{1,0:T(8,128)(2,1)S(1)}, bf16[128,1152]{1,0:T(8,128)(2,1)S(1)}, u32[]{:S(2)}, u32[]{:S(2)}) collective-permute-start(bf16[128,1152]{1,0:T(8,128)(2,1)S(1)} %get-tuple-element.43), channel_id=1, source_target_pairs={{0,1},{1,2},{2,3},{3,0},{4,5},{5,6},{6,7},{7,4},{8,9},{9,10},{10,1... | collective-permute-start | bytes 884744 | tf_op jit(solution)/shard_map/ppermute | solution.py:35
  24.6 7.6 %collective-permute-start.12 = (bf16[128,1152]{1,0:T(8,128)(2,1)S(1)}, bf16[128,1152]{1,0:T(8,128)(2,1)S(1)}, u32[]{:S(2)}, u32[]{:S(2)}) collective-permute-start(bf16[128,1152]{1,0:T(8,128)(2,1)S(1)} %get-tuple-element.33.after), channel_id=1, source_target_pairs={{0,3},{1,0},{2,1},{3,2},{4,7},{5,4},{6,5},{7,6},{8,11},{9,8},{10,9... | collective-permute-start | bytes 884744 | tf_op jit(solution)/shard_map/ppermute | solution.py:35
  29.0 10.5 %collective-permute-start.13 = (bf16[128,1152]{1,0:T(8,128)(2,1)S(1)}, bf16[128,1152]{1,0:T(8,128)(2,1)S(1)}, u32[]{:S(2)}, u32[]{:S(2)}) collective-permute-start(bf16[128,1152]{1,0:T(8,128)(2,1)S(1)} %get-tuple-element.39), channel_id=1, source_target_pairs={{0,1},{1,2},{2,3},{3,0},{4,5},{5,6},{6,7},{7,4},{8,9},{9,10},{10,1... | collective-permute-start | bytes 884744 | tf_op jit(solution)/shard_map/ppermute | solution.py:35
  29.1 10.4 %collective-permute-start.15 = (bf16[128,1152]{1,0:T(8,128)(2,1)S(1)}, bf16[128,1152]{1,0:T(8,128)(2,1)S(1)}, u32[]{:S(2)}, u32[]{:S(2)}) collective-permute-start(bf16[128,1152]{1,0:T(8,128)(2,1)S(1)} %get-tuple-element.41), channel_id=1, source_target_pairs={{0,19},{1,16},{2,17},{3,18},{4,23},{5,20},{6,21},{7,22},{8,27},{9,... | collective-permute-start | bytes 884744 | tf_op jit(solution)/shard_map/ppermute | solution.py:35
  31.7 8.7 %collective-permute-start.17 = (bf16[128,1152]{1,0:T(8,128)(2,1)S(1)}, bf16[128,1152]{1,0:T(8,128)(2,1)S(1)}, u32[]{:S(2)}, u32[]{:S(2)}) collective-permute-start(bf16[128,1152]{1,0:T(8,128)(2,1)S(1)} %relay.3), channel_id=1, source_target_pairs={{0,17},{1,18},{2,19},{3,16},{4,21},{5,22},{6,23},{7,20},{8,25},{9,... | collective-permute-start | bytes 884744 | tf_op jit(solution)/shard_map/ppermute | solution.py:35
  32.3 8.2 %collective-permute-start.14 = (bf16[128,1152]{1,0:T(8,128)(2,1)S(1)}, bf16[128,1152]{1,0:T(8,128)(2,1)S(1)}, u32[]{:S(2)}, u32[]{:S(2)}) collective-permute-start(bf16[128,1152]{1,0:T(8,128)(2,1)S(1)} %relay.2.after), channel_id=1, source_target_pairs={{0,3},{1,0},{2,1},{3,2},{4,7},{5,4},{6,5},{7,6},{8,11},{9,8},{10,9... | collective-permute-start | bytes 884744 | tf_op jit(solution)/shard_map/ppermute | solution.py:35

commit v7 on v6

--- a/solution.py
+++ b/solution.py
@@ -207,16 +207,17 @@
 def last_kernel(core, consts, unit_own, length_own, unit_their, length_their, own, own_one, own_two, their, their_one,
                 their_two, image_out, text_out, grads, sems):
     scale = consts[0:1, 0:1]
-    for place, unit, length, mine, one, two in (
-        (core[0], unit_own, length_own, own, own_one, own_two),
-        (1 - core[0], unit_their, length_their, their, their_one, their_two),
-    ):
+    copies = [pltpu.make_async_copy(grads.at[i], out, sems.at[i]) for i, out in enumerate((image_out, text_out))]
+    for kind, (unit, length, mine, one, two) in enumerate((
+        (unit_their, length_their, their, their_one, their_two),
+        (unit_own, length_own, own, own_one, own_two),
+    )):
+        place = 1 - core[0] if kind == 0 else core[0]
         direction = scale * (mine[...] + one[...].astype(jnp.float32) + two[...].astype(jnp.float32))
         along = jnp.sum(unit[...] * direction, axis=1, keepdims=True)
         grads[place] = (direction - unit[...] * along) * (1.0 / length[...])
-    copies = [pltpu.make_async_copy(grads.at[i], out, sems.at[i]) for i, out in enumerate((image_out, text_out))]
-    for copy in copies:
-        copy.start()
+        for i, copy in enumerate(copies):
+            pl.when(place == i)(copy.start)
     for copy in copies:
         copy.wait()
 

time: 42.3 us -> 42.2 us (level)
  no operation moved by 1% of the time
where the time goes in v7:
time: 42.2 us; the launch traced here: 42.1 us
  starting transfers between devices  23 us (55%)
  Pallas kernels  12.6 us (30%)
  waiting for transfers between devices  3.35 us (8%)
  between operations  2.95 us (7%)
    ppermute x18, starting transfers between devices, moved(): return lax.ppermute(value, AXES, pairs)  23 us
    pallas_call x12, Pallas kernels, call(): run(*[pltpu.with_memory_space_constraint(a, pltpu.VMEM if s is VMEM else...  12.6 us
    ppermute x18, waiting for transfers between devices, moved(): return lax.ppermute(value, AXES, pairs)  3.35 us
  transfers between devices with their start and end apart: 18, of which 4 were waited for; matrix products, arithmetic and copies ran while one was open for 0% of the time, Pallas kernels for 21%

profile of v7, /device:TPU:1, one launch (start us, length us, event | category | flops | bytes accessed | tf_op | source)
XLA Modules:
  0.0 42.1 jit_solution(15773377118877223836)
XLA Ops:
  0.6 1.4 %rows.1 = (bf16[128,1152]{1,0:T(8,128)(2,1)S(1)}, bf16[128,1152]{1,0:T(8,128)(2,1)S(1)}, bf16[256,1152]{1,0:T(8,128)(2,1)S(1)}, bf16[128,1152]{1,0:T(8,128)(2,1)S(1)}, bf16[128,1152]{1,0:T(8,128)(2,1)S(1)}) custom-call(s32[1]{0:T(128)} %bitcast.core, bf16[128,1152]{1,0:T(8,128)(2,1)} %image.1, bf16[128,1152]{1,0:T(8,128)(2,1)} %text.1), custom_call_target="tpu_custom_call" | custom-call | flops 100000000 | bytes 1 | tf_op jit(solution)/shard_map/rows/pallas_call | solution.py:74
  2.0 3.3 %collective-permute-start = (bf16[256,1152]{1,0:T(8,128)(2,1)S(1)}, bf16[256,1152]{1,0:T(8,128)(2,1)S(1)}, u32[]{:S(2)}, u32[]{:S(2)}) collective-permute-start(bf16[256,1152]{1,0:T(8,128)(2,1)S(1)} %get-tuple-element.23), channel_id=1, source_target_pairs={{0,16},{1,17},{2,18},{3,19},{4,20},{5,21},{6,22},{7,23},{8,24},{9,... | collective-permute-start | bytes 1769480 | tf_op jit(solution)/shard_map/ppermute | solution.py:35
  5.3 2.9 %collective-permute-start.4 = (bf16[128,1152]{1,0:T(8,128)(2,1)S(1)}, bf16[128,1152]{1,0:T(8,128)(2,1)S(1)}, u32[]{:S(2)}, u32[]{:S(2)}) collective-permute-start(bf16[128,1152]{1,0:T(8,128)(2,1)S(1)} %get-tuple-element.28.other), channel_id=1, source_target_pairs={{0,28},{1,29},{2,30},{3,31},{4,16},{5,17},{6,18},{7,19},{8,20},{9,... | collective-permute-start | bytes 884744 | tf_op jit(solution)/shard_map/ppermute | solution.py:35
  8.4 3.0 %collective-permute-start.3 = (bf16[128,1152]{1,0:T(8,128)(2,1)S(1)}, bf16[128,1152]{1,0:T(8,128)(2,1)S(1)}, u32[]{:S(2)}, u32[]{:S(2)}) collective-permute-start(bf16[128,1152]{1,0:T(8,128)(2,1)S(1)} %get-tuple-element.25.after_too.other_second), channel_id=1, source_target_pairs={{0,28},{1,29},{2,30},{3,31},{4,16},{5,17},{6,18},{7,19},{8,20},{9,... | collective-permute-start | bytes 884744 | tf_op jit(solution)/shard_map/ppermute | solution.py:35
  13.6 0.2 collective-permute-start.5
  13.8 2.5 %collective-permute-start.8 = (bf16[128,1152]{1,0:T(8,128)(2,1)S(1)}, bf16[128,1152]{1,0:T(8,128)(2,1)S(1)}, u32[]{:S(2)}, u32[]{:S(2)}) collective-permute-start(bf16[128,1152]{1,0:T(8,128)(2,1)S(1)} %gate.5.ahead_second), channel_id=1, source_target_pairs={{0,3},{1,0},{2,1},{3,2},{4,7},{5,4},{6,5},{7,6},{8,11},{9,8},{10,9... | collective-permute-start | bytes 884744 | tf_op jit(solution)/shard_map/ppermute | solution.py:35
  16.3 0.7 %collective-permute-start.6 = (bf16[128,1152]{1,0:T(8,128)(2,1)S(1)}, bf16[128,1152]{1,0:T(8,128)(2,1)S(1)}, u32[]{:S(2)}, u32[]{:S(2)}) collective-permute-start(bf16[128,1152]{1,0:T(8,128)(2,1)S(1)} %gate.5.ahead_second), channel_id=1, source_target_pairs={{0,16},{1,17},{2,18},{3,19},{4,20},{5,21},{6,22},{7,23},{8,24},{9,... | collective-permute-start | bytes 884744 | tf_op jit(solution)/shard_map/ppermute | solution.py:35
  17.1 1.0 %collective-permute-done.6.near_second = bf16[128,1152]{1,0:T(8,128)(2,1)S(1)} collective-permute-done((bf16[128,1152]{1,0:T(8,128)(2,1)S(1)}, bf16[128,1152]{1,0:T(8,128)(2,1)S(1)}, u32[]{:S(2)}, u32[]{:S(2)}) %collective-permute-start.6) | collective-permute-done | bytes 294944 | tf_op jit(solution)/shard_map/ppermute | solution.py:35
  18.1 1.7 %near.1 = (f32[256,1152]{1,0:T(8,128)S(1)}, f32[256,1152]{1,0:T(8,128)S(1)}) custom-call(f32[32,128]{1,0:T(8,128)S(1)} %consts.1.after, bf16[128,1152]{1,0:T(8,128)(2,1)S(1)} %gate.4.back_first, bf16[128,1152]{1,0:T(8,128)(2,1)S(1)} %collective-permute-done.2.back_second, bf16[128,1152]{1,0:T(8,128)(2,1)S(1)} %collective-permute-done.3.ahead_first, ...), custom_call_target="tpu_custom_call" | custom-call | flops 1 | bytes 1 | tf_op jit(solution)/shard_map/near/pallas_call | solution.py:74
  19.8 0.8 %collective-permute-done.7.value = bf16[128,1152]{1,0:T(8,128)(2,1)S(1)} collective-permute-done((bf16[128,1152]{1,0:T(8,128)(2,1)S(1)}, bf16[128,1152]{1,0:T(8,128)(2,1)S(1)}, u32[]{:S(2)}, u32[]{:S(2)}) %collective-permute-start.7) | collective-permute-done | bytes 294944 | tf_op jit(solution)/shard_map/ppermute | solution.py:35
  20.7 0.9 %collective-permute-start.10 = (bf16[128,1152]{1,0:T(8,128)(2,1)S(1)}, bf16[128,1152]{1,0:T(8,128)(2,1)S(1)}, u32[]{:S(2)}, u32[]{:S(2)}) collective-permute-start(bf16[128,1152]{1,0:T(8,128)(2,1)S(1)} %gate.6.far_first), channel_id=1, source_target_pairs={{0,16},{1,17},{2,18},{3,19},{4,20},{5,21},{6,22},{7,23},{8,24},{9,... | collective-permute-start | bytes 884744 | tf_op jit(solution)/shard_map/ppermute | solution.py:35
  21.6 0.2 units.1
  21.9 1.5 %far_near.1.part = f32[256,1152]{1,0:T(8,128)S(1)} custom-call(f32[32,128]{1,0:T(8,128)S(1)} %consts.1.after, bf16[128,1152]{1,0:T(8,128)(2,1)S(1)} %gate.6.far_first, bf16[128,1152]{1,0:T(8,128)(2,1)S(1)} %gate.7.far_second, bf16[128,1152]{1,0:T(8,128)(2,1)S(1)} %get-tuple-element.28.other, bf16[128,1152]{1,0:T(8,128)(2,1)S(1)} %get-tuple-element.25.after_too.other_second, ...), custom_call_target="tpu_custom_call" | custom-call | flops 1 | bytes 1 | tf_op jit(solution)/shard_map/far_near/pallas_call | solution.py:74
  23.5 0.8 %far.1 = (bf16[128,1152]{1,0:T(8,128)(2,1)S(1)}, bf16[128,1152]{1,0:T(8,128)(2,1)S(1)}) custom-call(f32[32,128]{1,0:T(8,128)S(1)} %consts.1.after, f32[256,1152]{1,0:T(8,128)S(1)} %far_near.1.part, bf16[128,1152]{1,0:T(8,128)(2,1)S(1)} %gate.6.far_first, bf16[128,1152]{1,0:T(8,128)(2,1)S(1)} %gate.7.far_second, ...), custom_call_target="tpu_custom_call" | custom-call | flops 301989888 | bytes 1 | tf_op jit(solution)/shard_map/far/pallas_call | solution.py:74
  24.3 0.3 collective-permute-start.16
  24.6 2.7 %collective-permute-start.12 = (bf16[128,1152]{1,0:T(8,128)(2,1)S(1)}, bf16[128,1152]{1,0:T(8,128)(2,1)S(1)}, u32[]{:S(2)}, u32[]{:S(2)}) collective-permute-start(bf16[128,1152]{1,0:T(8,128)(2,1)S(1)} %get-tuple-element.33.after), channel_id=1, source_target_pairs={{0,3},{1,0},{2,1},{3,2},{4,7},{5,4},{6,5},{7,6},{8,11},{9,8},{10,9... | collective-permute-start | bytes 884744 | tf_op jit(solution)/shard_map/ppermute | solution.py:35
  27.2 1.7 %rest.1 = (f32[128,1152]{1,0:T(8,128)S(1)}, bf16[128,1152]{1,0:T(8,128)(2,1)S(1)}, bf16[128,1152]{1,0:T(8,128)(2,1)S(1)}, f32[128,1152]{1,0:T(8,128)S(1)}) custom-call(f32[32,128]{1,0:T(8,128)S(1)} %consts.1.after, f32[256,1152]{1,0:T(8,128)S(1)} %get-tuple-element.29.after.part_back, f32[256,1152]{1,0:T(8,128)S(1)} %get-tuple-element.32.part_ahead, ...), custom_call_target="tpu_custom_call" | custom-call | flops 1 | bytes 1 | tf_op jit(solution)/shard_map/rest/pallas_call | solution.py:74
  29.1 2.2 %collective-permute-start.15 = (bf16[128,1152]{1,0:T(8,128)(2,1)S(1)}, bf16[128,1152]{1,0:T(8,128)(2,1)S(1)}, u32[]{:S(2)}, u32[]{:S(2)}) collective-permute-start(bf16[128,1152]{1,0:T(8,128)(2,1)S(1)} %get-tuple-element.41), channel_id=1, source_target_pairs={{0,19},{1,16},{2,17},{3,18},{4,23},{5,20},{6,21},{7,22},{8,27},{9,... | collective-permute-start | bytes 884744 | tf_op jit(solution)/shard_map/ppermute | solution.py:35
  31.2 0.4 %collective-permute-done.16.got = bf16[128,1152]{1,0:T(8,128)(2,1)S(1)} collective-permute-done((bf16[128,1152]{1,0:T(8,128)(2,1)S(1)}, bf16[128,1152]{1,0:T(8,128)(2,1)S(1)}, u32[]{:S(2)}, u32[]{:S(2)}) %collective-permute-start.16) | collective-permute-done | bytes 294944 | tf_op jit(solution)/shard_map/ppermute | solution.py:35
  31.7 0.5 %collective-permute-start.17 = (bf16[128,1152]{1,0:T(8,128)(2,1)S(1)}, bf16[128,1152]{1,0:T(8,128)(2,1)S(1)}, u32[]{:S(2)}, u32[]{:S(2)}) collective-permute-start(bf16[128,1152]{1,0:T(8,128)(2,1)S(1)} %relay.3), channel_id=1, source_target_pairs={{0,17},{1,18},{2,19},{3,16},{4,21},{5,22},{6,23},{7,20},{8,25},{9,... | collective-permute-start | bytes 884744 | tf_op jit(solution)/shard_map/ppermute | solution.py:35
  32.3 3.5 %collective-permute-start.14 = (bf16[128,1152]{1,0:T(8,128)(2,1)S(1)}, bf16[128,1152]{1,0:T(8,128)(2,1)S(1)}, u32[]{:S(2)}, u32[]{:S(2)}) collective-permute-start(bf16[128,1152]{1,0:T(8,128)(2,1)S(1)} %relay.2.after), channel_id=1, source_target_pairs={{0,3},{1,0},{2,1},{3,2},{4,7},{5,4},{6,5},{7,6},{8,11},{9,8},{10,9... | collective-permute-start | bytes 884744 | tf_op jit(solution)/shard_map/ppermute | solution.py:35
  35.8 3.6 %own.1 = (f32[128,1152]{1,0:T(8,128)S(1)}, f32[128,1152]{1,0:T(8,128)S(1)}, f32[128,1152]{1,0:T(8,128)S(1)}, f32[128,1]{1,0:T(8,128)S(1)}) custom-call(f32[32,128]{1,0:T(8,128)S(1)} %consts.1.after, bf16[128,1152]{1,0:T(8,128)(2,1)S(1)} %get-tuple-element.27.first, bf16[128,1152]{1,0:T(8,128)(2,1)S(1)} %get-tuple-element.24.after.second, ...), custom_call_target="tpu_custom_call" | custom-call | flops 1 | bytes 1 | tf_op jit(solution)/shard_map/own/pallas_call | solution.py:74
  39.5 1.0 %collective-permute-done.17.their_two = bf16[128,1152]{1,0:T(8,128)(2,1)S(1)} collective-permute-done((bf16[128,1152]{1,0:T(8,128)(2,1)S(1)}, bf16[128,1152]{1,0:T(8,128)(2,1)S(1)}, u32[]{:S(2)}, u32[]{:S(2)}) %collective-permute-start.17) | collective-permute-done | bytes 294944 | tf_op jit(solution)/shard_map/ppermute | solution.py:35
  40.5 1.5 %last.1 = (f32[128,1152]{1,0:T(8,128)}, f32[128,1152]{1,0:T(8,128)}) custom-call(s32[1]{0:T(128)} %bitcast.core, f32[32,128]{1,0:T(8,128)S(1)} %consts.1.after, f32[128,1152]{1,0:T(8,128)S(1)} %get-tuple-element.30.after.unit_own, f32[128,1]{1,0:T(8,128)S(1)} %get-tuple-element.31.length_own, f32[128,1152]{1,0:T(8,128)S(1)} %get-tuple-element.36.unit_their, ...), custom_call_target="tpu_custom_call" | custom-call | flops 1 | bytes 1 | tf_op jit(solution)/shard_map/last/pallas_call | solution.py:74
  (34 shorter events, 0.9 us)
Async XLA Ops:
  2.0 6.3 %collective-permute-start = (bf16[256,1152]{1,0:T(8,128)(2,1)S(1)}, bf16[256,1152]{1,0:T(8,128)(2,1)S(1)}, u32[]{:S(2)}, u32[]{:S(2)}) collective-permute-start(bf16[256,1152]{1,0:T(8,128)(2,1)S(1)} %get-tuple-element.23), channel_id=1, source_target_pairs={{0,16},{1,17},{2,18},{3,19},{4,20},{5,21},{6,22},{7,23},{8,24},{9,... | collective-permute-start | bytes 1769480 | tf_op jit(solution)/shard_map/ppermute | solution.py:35
  5.3 8.2 %collective-permute-start.1 = (bf16[128,1152]{1,0:T(8,128)(2,1)S(1)}, bf16[128,1152]{1,0:T(8,128)(2,1)S(1)}, u32[]{:S(2)}, u32[]{:S(2)}) collective-permute-start(bf16[128,1152]{1,0:T(8,128)(2,1)S(1)} %get-tuple-element.27.first), channel_id=1, source_target_pairs={{0,1},{1,2},{2,3},{3,0},{4,5},{5,6},{6,7},{7,4},{8,9},{9,10},{10,1... | collective-permute-start | bytes 884744 | tf_op jit(solution)/shard_map/ppermute | solution.py:35
  5.3 8.5 %collective-permute-start.4 = (bf16[128,1152]{1,0:T(8,128)(2,1)S(1)}, bf16[128,1152]{1,0:T(8,128)(2,1)S(1)}, u32[]{:S(2)}, u32[]{:S(2)}) collective-permute-start(bf16[128,1152]{1,0:T(8,128)(2,1)S(1)} %get-tuple-element.28.other), channel_id=1, source_target_pairs={{0,28},{1,29},{2,30},{3,31},{4,16},{5,17},{6,18},{7,19},{8,20},{9,... | collective-permute-start | bytes 884744 | tf_op jit(solution)/shard_map/ppermute | solution.py:35
  8.3 8.0 %collective-permute-start.2 = (bf16[128,1152]{1,0:T(8,128)(2,1)S(1)}, bf16[128,1152]{1,0:T(8,128)(2,1)S(1)}, u32[]{:S(2)}, u32[]{:S(2)}) collective-permute-start(bf16[128,1152]{1,0:T(8,128)(2,1)S(1)} %get-tuple-element.24.after.second), channel_id=1, source_target_pairs={{0,1},{1,2},{2,3},{3,0},{4,5},{5,6},{6,7},{7,4},{8,9},{9,10},{10,1... | collective-permute-start | bytes 884744 | tf_op jit(solution)/shard_map/ppermute | solution.py:35
  8.4 8.5 %collective-permute-start.3 = (bf16[128,1152]{1,0:T(8,128)(2,1)S(1)}, bf16[128,1152]{1,0:T(8,128)(2,1)S(1)}, u32[]{:S(2)}, u32[]{:S(2)}) collective-permute-start(bf16[128,1152]{1,0:T(8,128)(2,1)S(1)} %get-tuple-element.25.after_too.other_second), channel_id=1, source_target_pairs={{0,28},{1,29},{2,30},{3,31},{4,16},{5,17},{6,18},{7,19},{8,20},{9,... | collective-permute-start | bytes 884744 | tf_op jit(solution)/shard_map/ppermute | solution.py:35
  13.5 7.2 %collective-permute-start.7 = (bf16[128,1152]{1,0:T(8,128)(2,1)S(1)}, bf16[128,1152]{1,0:T(8,128)(2,1)S(1)}, u32[]{:S(2)}, u32[]{:S(2)}) collective-permute-start(bf16[128,1152]{1,0:T(8,128)(2,1)S(1)} %gate.4.back_first), channel_id=1, source_target_pairs={{0,1},{1,2},{2,3},{3,0},{4,5},{5,6},{6,7},{7,4},{8,9},{9,10},{10,1... | collective-permute-start | bytes 884744 | tf_op jit(solution)/shard_map/ppermute | solution.py:35
  13.6 3.5 %collective-permute-start.5 = (bf16[128,1152]{1,0:T(8,128)(2,1)S(1)}, bf16[128,1152]{1,0:T(8,128)(2,1)S(1)}, u32[]{:S(2)}, u32[]{:S(2)}) collective-permute-start(bf16[128,1152]{1,0:T(8,128)(2,1)S(1)} %gate.4.back_first), channel_id=1, source_target_pairs={{0,16},{1,17},{2,18},{3,19},{4,20},{5,21},{6,22},{7,23},{8,24},{9,... | collective-permute-start | bytes 884744 | tf_op jit(solution)/shard_map/ppermute | solution.py:35
  13.8 8.0 %collective-permute-start.8 = (bf16[128,1152]{1,0:T(8,128)(2,1)S(1)}, bf16[128,1152]{1,0:T(8,128)(2,1)S(1)}, u32[]{:S(2)}, u32[]{:S(2)}) collective-permute-start(bf16[128,1152]{1,0:T(8,128)(2,1)S(1)} %gate.5.ahead_second), channel_id=1, source_target_pairs={{0,3},{1,0},{2,1},{3,2},{4,7},{5,4},{6,5},{7,6},{8,11},{9,8},{10,9... | collective-permute-start | bytes 884744 | tf_op jit(solution)/shard_map/ppermute | solution.py:35
  16.3 1.9 %collective-permute-start.6 = (bf16[128,1152]{1,0:T(8,128)(2,1)S(1)}, bf16[128,1152]{1,0:T(8,128)(2,1)S(1)}, u32[]{:S(2)}, u32[]{:S(2)}) collective-permute-start(bf16[128,1152]{1,0:T(8,128)(2,1)S(1)} %gate.5.ahead_second), channel_id=1, source_target_pairs={{0,16},{1,17},{2,18},{3,19},{4,20},{5,21},{6,22},{7,23},{8,24},{9,... | collective-permute-start | bytes 884744 | tf_op jit(solution)/shard_map/ppermute | solution.py:35
  17.0 4.9 %collective-permute-start.9 = (bf16[256,1152]{1,0:T(8,128)(2,1)S(1)}, bf16[256,1152]{1,0:T(8,128)(2,1)S(1)}, u32[]{:S(2)}, u32[]{:S(2)}) collective-permute-start(bf16[256,1152]{1,0:T(8,128)(2,1)S(1)} %pad_maximum_fusion), channel_id=1, source_target_pairs={{0,16},{1,17},{2,18},{3,19},{4,20},{5,21},{6,22},{7,23},{8,24},{9,... | collective-permute-start | bytes 1769480 | tf_op jit(solution)/shard_map/ppermute | solution.py:35
  20.7 2.7 %collective-permute-start.10 = (bf16[128,1152]{1,0:T(8,128)(2,1)S(1)}, bf16[128,1152]{1,0:T(8,128)(2,1)S(1)}, u32[]{:S(2)}, u32[]{:S(2)}) collective-permute-start(bf16[128,1152]{1,0:T(8,128)(2,1)S(1)} %gate.6.far_first), channel_id=1, source_target_pairs={{0,16},{1,17},{2,18},{3,19},{4,20},{5,21},{6,22},{7,23},{8,24},{9,... | collective-permute-start | bytes 884744 | tf_op jit(solution)/shard_map/ppermute | solution.py:35
  21.8 1.7 %collective-permute-start.11 = (bf16[128,1152]{1,0:T(8,128)(2,1)S(1)}, bf16[128,1152]{1,0:T(8,128)(2,1)S(1)}, u32[]{:S(2)}, u32[]{:S(2)}) collective-permute-start(bf16[128,1152]{1,0:T(8,128)(2,1)S(1)} %gate.7.far_second), channel_id=1, source_target_pairs={{0,16},{1,17},{2,18},{3,19},{4,20},{5,21},{6,22},{7,23},{8,24},{9,... | collective-permute-start | bytes 884744 | tf_op jit(solution)/shard_map/ppermute | solution.py:35
  24.3 7.3 %collective-permute-start.16 = (bf16[128,1152]{1,0:T(8,128)(2,1)S(1)}, bf16[128,1152]{1,0:T(8,128)(2,1)S(1)}, u32[]{:S(2)}, u32[]{:S(2)}) collective-permute-start(bf16[128,1152]{1,0:T(8,128)(2,1)S(1)} %get-tuple-element.43), channel_id=1, source_target_pairs={{0,1},{1,2},{2,3},{3,0},{4,5},{5,6},{6,7},{7,4},{8,9},{9,10},{10,1... | collective-permute-start | bytes 884744 | tf_op jit(solution)/shard_map/ppermute | solution.py:35
  24.6 7.6 %collective-permute-start.12 = (bf16[128,1152]{1,0:T(8,128)(2,1)S(1)}, bf16[128,1152]{1,0:T(8,128)(2,1)S(1)}, u32[]{:S(2)}, u32[]{:S(2)}) collective-permute-start(bf16[128,1152]{1,0:T(8,128)(2,1)S(1)} %get-tuple-element.33.after), channel_id=1, source_target_pairs={{0,3},{1,0},{2,1},{3,2},{4,7},{5,4},{6,5},{7,6},{8,11},{9,8},{10,9... | collective-permute-start | bytes 884744 | tf_op jit(solution)/shard_map/ppermute | solution.py:35
  29.0 10.5 %collective-permute-start.13 = (bf16[128,1152]{1,0:T(8,128)(2,1)S(1)}, bf16[128,1152]{1,0:T(8,128)(2,1)S(1)}, u32[]{:S(2)}, u32[]{:S(2)}) collective-permute-start(bf16[128,1152]{1,0:T(8,128)(2,1)S(1)} %get-tuple-element.39), channel_id=1, source_target_pairs={{0,1},{1,2},{2,3},{3,0},{4,5},{5,6},{6,7},{7,4},{8,9},{9,10},{10,1... | collective-permute-start | bytes 884744 | tf_op jit(solution)/shard_map/ppermute | solution.py:35
  29.1 10.4 %collective-permute-start.15 = (bf16[128,1152]{1,0:T(8,128)(2,1)S(1)}, bf16[128,1152]{1,0:T(8,128)(2,1)S(1)}, u32[]{:S(2)}, u32[]{:S(2)}) collective-permute-start(bf16[128,1152]{1,0:T(8,128)(2,1)S(1)} %get-tuple-element.41), channel_id=1, source_target_pairs={{0,19},{1,16},{2,17},{3,18},{4,23},{5,20},{6,21},{7,22},{8,27},{9,... | collective-permute-start | bytes 884744 | tf_op jit(solution)/shard_map/ppermute | solution.py:35
  31.7 8.7 %collective-permute-start.17 = (bf16[128,1152]{1,0:T(8,128)(2,1)S(1)}, bf16[128,1152]{1,0:T(8,128)(2,1)S(1)}, u32[]{:S(2)}, u32[]{:S(2)}) collective-permute-start(bf16[128,1152]{1,0:T(8,128)(2,1)S(1)} %relay.3), channel_id=1, source_target_pairs={{0,17},{1,18},{2,19},{3,16},{4,21},{5,22},{6,23},{7,20},{8,25},{9,... | collective-permute-start | bytes 884744 | tf_op jit(solution)/shard_map/ppermute | solution.py:35
  32.3 8.2 %collective-permute-start.14 = (bf16[128,1152]{1,0:T(8,128)(2,1)S(1)}, bf16[128,1152]{1,0:T(8,128)(2,1)S(1)}, u32[]{:S(2)}, u32[]{:S(2)}) collective-permute-start(bf16[128,1152]{1,0:T(8,128)(2,1)S(1)} %relay.2.after), channel_id=1, source_target_pairs={{0,3},{1,0},{2,1},{3,2},{4,7},{5,4},{6,5},{7,6},{8,11},{9,8},{10,9... | collective-permute-start | bytes 884744 | tf_op jit(solution)/shard_map/ppermute | solution.py:35

commit v8 on v6

--- a/solution.py
+++ b/solution.py
@@ -82,7 +82,7 @@
 def unit_rows(matrix):
     values = matrix.astype(jnp.float32)
     length = jnp.sqrt(jnp.sum(values * values, axis=1, keepdims=True) + epsilon)
-    return (values / length, length)
+    return (values * (1.0 / length), length)
 
 
 def rows_kernel(core, image, text, first, other, both, raw_first, raw_other, sems):
@@ -98,11 +98,13 @@
         pltpu.make_async_copy(image, raw_other, sems.at[1]).start()
 
     pltpu.make_async_copy(image, raw_first, sems.at[0]).wait()
-    first[...] = unit_rows(raw_first[...])[0].astype(jnp.bfloat16)
-    both[: first.shape[0]] = first[...]
+    half = unit_rows(raw_first[...])[0].astype(jnp.bfloat16)
+    first[...] = half
+    both[: first.shape[0]] = half
     pltpu.make_async_copy(text, raw_other, sems.at[1]).wait()
-    other[...] = unit_rows(raw_other[...])[0].astype(jnp.bfloat16)
-    both[first.shape[0] :] = other[...]
+    half = unit_rows(raw_other[...])[0].astype(jnp.bfloat16)
+    other[...] = half
+    both[first.shape[0] :] = half
 
 
 def halves_kernel(both, up, down):

time: 42.3 us -> 42.2 us (level)
  no operation moved by 1% of the time
where the time goes in v8:
time: 42.2 us; the launch traced here: 42.1 us
  starting transfers between devices  23.1 us (55%)
  Pallas kernels  12.6 us (30%)
  waiting for transfers between devices  3.34 us (8%)
  between operations  2.95 us (7%)
    ppermute x18, starting transfers between devices, moved(): return lax.ppermute(value, AXES, pairs)  23.1 us
    pallas_call x12, Pallas kernels, call(): run(*[pltpu.with_memory_space_constraint(a, pltpu.VMEM if s is VMEM else...  12.6 us
    ppermute x18, waiting for transfers between devices, moved(): return lax.ppermute(value, AXES, pairs)  3.34 us
  transfers between devices with their start and end apart: 18, of which 4 were waited for; matrix products, arithmetic and copies ran while one was open for 0% of the time, Pallas kernels for 21%

profile of v8, /device:TPU:1, one launch (start us, length us, event | category | flops | bytes accessed | tf_op | source)
XLA Modules:
  0.0 42.1 jit_solution(16817985509067990359)
XLA Ops:
  0.6 1.3 %rows.1 = (bf16[128,1152]{1,0:T(8,128)(2,1)S(1)}, bf16[128,1152]{1,0:T(8,128)(2,1)S(1)}, bf16[256,1152]{1,0:T(8,128)(2,1)S(1)}, bf16[128,1152]{1,0:T(8,128)(2,1)S(1)}, bf16[128,1152]{1,0:T(8,128)(2,1)S(1)}) custom-call(s32[1]{0:T(128)} %bitcast.core, bf16[128,1152]{1,0:T(8,128)(2,1)} %image.1, bf16[128,1152]{1,0:T(8,128)(2,1)} %text.1), custom_call_target="tpu_custom_call" | custom-call | flops 100000000 | bytes 1 | tf_op jit(solution)/shard_map/rows/pallas_call | solution.py:74
  2.0 3.3 %collective-permute-start = (bf16[256,1152]{1,0:T(8,128)(2,1)S(1)}, bf16[256,1152]{1,0:T(8,128)(2,1)S(1)}, u32[]{:S(2)}, u32[]{:S(2)}) collective-permute-start(bf16[256,1152]{1,0:T(8,128)(2,1)S(1)} %get-tuple-element.23), channel_id=1, source_target_pairs={{0,16},{1,17},{2,18},{3,19},{4,20},{5,21},{6,22},{7,23},{8,24},{9,... | collective-permute-start | bytes 1769480 | tf_op jit(solution)/shard_map/ppermute | solution.py:35
  5.3 2.9 %collective-permute-start.4 = (bf16[128,1152]{1,0:T(8,128)(2,1)S(1)}, bf16[128,1152]{1,0:T(8,128)(2,1)S(1)}, u32[]{:S(2)}, u32[]{:S(2)}) collective-permute-start(bf16[128,1152]{1,0:T(8,128)(2,1)S(1)} %get-tuple-element.28.other), channel_id=1, source_target_pairs={{0,28},{1,29},{2,30},{3,31},{4,16},{5,17},{6,18},{7,19},{8,20},{9,... | collective-permute-start | bytes 884744 | tf_op jit(solution)/shard_map/ppermute | solution.py:35
  8.4 3.0 %collective-permute-start.3 = (bf16[128,1152]{1,0:T(8,128)(2,1)S(1)}, bf16[128,1152]{1,0:T(8,128)(2,1)S(1)}, u32[]{:S(2)}, u32[]{:S(2)}) collective-permute-start(bf16[128,1152]{1,0:T(8,128)(2,1)S(1)} %get-tuple-element.25.after_too.other_second), channel_id=1, source_target_pairs={{0,28},{1,29},{2,30},{3,31},{4,16},{5,17},{6,18},{7,19},{8,20},{9,... | collective-permute-start | bytes 884744 | tf_op jit(solution)/shard_map/ppermute | solution.py:35
  13.6 0.2 collective-permute-start.5
  13.7 2.5 %collective-permute-start.8 = (bf16[128,1152]{1,0:T(8,128)(2,1)S(1)}, bf16[128,1152]{1,0:T(8,128)(2,1)S(1)}, u32[]{:S(2)}, u32[]{:S(2)}) collective-permute-start(bf16[128,1152]{1,0:T(8,128)(2,1)S(1)} %gate.5.ahead_second), channel_id=1, source_target_pairs={{0,3},{1,0},{2,1},{3,2},{4,7},{5,4},{6,5},{7,6},{8,11},{9,8},{10,9... | collective-permute-start | bytes 884744 | tf_op jit(solution)/shard_map/ppermute | solution.py:35
  16.2 0.7 %collective-permute-start.6 = (bf16[128,1152]{1,0:T(8,128)(2,1)S(1)}, bf16[128,1152]{1,0:T(8,128)(2,1)S(1)}, u32[]{:S(2)}, u32[]{:S(2)}) collective-permute-start(bf16[128,1152]{1,0:T(8,128)(2,1)S(1)} %gate.5.ahead_second), channel_id=1, source_target_pairs={{0,16},{1,17},{2,18},{3,19},{4,20},{5,21},{6,22},{7,23},{8,24},{9,... | collective-permute-start | bytes 884744 | tf_op jit(solution)/shard_map/ppermute | solution.py:35
  17.1 1.0 %collective-permute-done.6.near_second = bf16[128,1152]{1,0:T(8,128)(2,1)S(1)} collective-permute-done((bf16[128,1152]{1,0:T(8,128)(2,1)S(1)}, bf16[128,1152]{1,0:T(8,128)(2,1)S(1)}, u32[]{:S(2)}, u32[]{:S(2)}) %collective-permute-start.6) | collective-permute-done | bytes 294944 | tf_op jit(solution)/shard_map/ppermute | solution.py:35
  18.1 1.7 %near.1 = (f32[256,1152]{1,0:T(8,128)S(1)}, f32[256,1152]{1,0:T(8,128)S(1)}) custom-call(f32[32,128]{1,0:T(8,128)S(1)} %consts.1.after, bf16[128,1152]{1,0:T(8,128)(2,1)S(1)} %gate.4.back_first, bf16[128,1152]{1,0:T(8,128)(2,1)S(1)} %collective-permute-done.2.back_second, bf16[128,1152]{1,0:T(8,128)(2,1)S(1)} %collective-permute-done.3.ahead_first, ...), custom_call_target="tpu_custom_call" | custom-call | flops 1 | bytes 1 | tf_op jit(solution)/shard_map/near/pallas_call | solution.py:74
  19.8 0.8 %collective-permute-done.7.value = bf16[128,1152]{1,0:T(8,128)(2,1)S(1)} collective-permute-done((bf16[128,1152]{1,0:T(8,128)(2,1)S(1)}, bf16[128,1152]{1,0:T(8,128)(2,1)S(1)}, u32[]{:S(2)}, u32[]{:S(2)}) %collective-permute-start.7) | collective-permute-done | bytes 294944 | tf_op jit(solution)/shard_map/ppermute | solution.py:35
  20.6 0.9 %collective-permute-start.10 = (bf16[128,1152]{1,0:T(8,128)(2,1)S(1)}, bf16[128,1152]{1,0:T(8,128)(2,1)S(1)}, u32[]{:S(2)}, u32[]{:S(2)}) collective-permute-start(bf16[128,1152]{1,0:T(8,128)(2,1)S(1)} %gate.6.far_first), channel_id=1, source_target_pairs={{0,16},{1,17},{2,18},{3,19},{4,20},{5,21},{6,22},{7,23},{8,24},{9,... | collective-permute-start | bytes 884744 | tf_op jit(solution)/shard_map/ppermute | solution.py:35
  21.6 0.2 units.1
  21.9 1.5 %far_near.1.part = f32[256,1152]{1,0:T(8,128)S(1)} custom-call(f32[32,128]{1,0:T(8,128)S(1)} %consts.1.after, bf16[128,1152]{1,0:T(8,128)(2,1)S(1)} %gate.6.far_first, bf16[128,1152]{1,0:T(8,128)(2,1)S(1)} %gate.7.far_second, bf16[128,1152]{1,0:T(8,128)(2,1)S(1)} %get-tuple-element.28.other, bf16[128,1152]{1,0:T(8,128)(2,1)S(1)} %get-tuple-element.25.after_too.other_second, ...), custom_call_target="tpu_custom_call" | custom-call | flops 1 | bytes 1 | tf_op jit(solution)/shard_map/far_near/pallas_call | solution.py:74
  23.4 0.8 %far.1 = (bf16[128,1152]{1,0:T(8,128)(2,1)S(1)}, bf16[128,1152]{1,0:T(8,128)(2,1)S(1)}) custom-call(f32[32,128]{1,0:T(8,128)S(1)} %consts.1.after, f32[256,1152]{1,0:T(8,128)S(1)} %far_near.1.part, bf16[128,1152]{1,0:T(8,128)(2,1)S(1)} %gate.6.far_first, bf16[128,1152]{1,0:T(8,128)(2,1)S(1)} %gate.7.far_second, ...), custom_call_target="tpu_custom_call" | custom-call | flops 301989888 | bytes 1 | tf_op jit(solution)/shard_map/far/pallas_call | solution.py:74
  24.2 0.3 collective-permute-start.16
  24.5 2.7 %collective-permute-start.12 = (bf16[128,1152]{1,0:T(8,128)(2,1)S(1)}, bf16[128,1152]{1,0:T(8,128)(2,1)S(1)}, u32[]{:S(2)}, u32[]{:S(2)}) collective-permute-start(bf16[128,1152]{1,0:T(8,128)(2,1)S(1)} %get-tuple-element.33.after), channel_id=1, source_target_pairs={{0,3},{1,0},{2,1},{3,2},{4,7},{5,4},{6,5},{7,6},{8,11},{9,8},{10,9... | collective-permute-start | bytes 884744 | tf_op jit(solution)/shard_map/ppermute | solution.py:35
  27.2 1.7 %rest.1 = (f32[128,1152]{1,0:T(8,128)S(1)}, bf16[128,1152]{1,0:T(8,128)(2,1)S(1)}, bf16[128,1152]{1,0:T(8,128)(2,1)S(1)}, f32[128,1152]{1,0:T(8,128)S(1)}) custom-call(f32[32,128]{1,0:T(8,128)S(1)} %consts.1.after, f32[256,1152]{1,0:T(8,128)S(1)} %get-tuple-element.29.after.part_back, f32[256,1152]{1,0:T(8,128)S(1)} %get-tuple-element.32.part_ahead, ...), custom_call_target="tpu_custom_call" | custom-call | flops 1 | bytes 1 | tf_op jit(solution)/shard_map/rest/pallas_call | solution.py:74
  29.0 2.2 %collective-permute-start.15 = (bf16[128,1152]{1,0:T(8,128)(2,1)S(1)}, bf16[128,1152]{1,0:T(8,128)(2,1)S(1)}, u32[]{:S(2)}, u32[]{:S(2)}) collective-permute-start(bf16[128,1152]{1,0:T(8,128)(2,1)S(1)} %get-tuple-element.41), channel_id=1, source_target_pairs={{0,19},{1,16},{2,17},{3,18},{4,23},{5,20},{6,21},{7,22},{8,27},{9,... | collective-permute-start | bytes 884744 | tf_op jit(solution)/shard_map/ppermute | solution.py:35
  31.2 0.4 %collective-permute-done.16.got = bf16[128,1152]{1,0:T(8,128)(2,1)S(1)} collective-permute-done((bf16[128,1152]{1,0:T(8,128)(2,1)S(1)}, bf16[128,1152]{1,0:T(8,128)(2,1)S(1)}, u32[]{:S(2)}, u32[]{:S(2)}) %collective-permute-start.16) | collective-permute-done | bytes 294944 | tf_op jit(solution)/shard_map/ppermute | solution.py:35
  31.7 0.5 %collective-permute-start.17 = (bf16[128,1152]{1,0:T(8,128)(2,1)S(1)}, bf16[128,1152]{1,0:T(8,128)(2,1)S(1)}, u32[]{:S(2)}, u32[]{:S(2)}) collective-permute-start(bf16[128,1152]{1,0:T(8,128)(2,1)S(1)} %relay.3), channel_id=1, source_target_pairs={{0,17},{1,18},{2,19},{3,16},{4,21},{5,22},{6,23},{7,20},{8,25},{9,... | collective-permute-start | bytes 884744 | tf_op jit(solution)/shard_map/ppermute | solution.py:35
  32.2 3.5 %collective-permute-start.14 = (bf16[128,1152]{1,0:T(8,128)(2,1)S(1)}, bf16[128,1152]{1,0:T(8,128)(2,1)S(1)}, u32[]{:S(2)}, u32[]{:S(2)}) collective-permute-start(bf16[128,1152]{1,0:T(8,128)(2,1)S(1)} %relay.2.after), channel_id=1, source_target_pairs={{0,3},{1,0},{2,1},{3,2},{4,7},{5,4},{6,5},{7,6},{8,11},{9,8},{10,9... | collective-permute-start | bytes 884744 | tf_op jit(solution)/shard_map/ppermute | solution.py:35
  35.8 3.6 %own.1 = (f32[128,1152]{1,0:T(8,128)S(1)}, f32[128,1152]{1,0:T(8,128)S(1)}, f32[128,1152]{1,0:T(8,128)S(1)}, f32[128,1]{1,0:T(8,128)S(1)}) custom-call(f32[32,128]{1,0:T(8,128)S(1)} %consts.1.after, bf16[128,1152]{1,0:T(8,128)(2,1)S(1)} %get-tuple-element.27.first, bf16[128,1152]{1,0:T(8,128)(2,1)S(1)} %get-tuple-element.24.after.second, ...), custom_call_target="tpu_custom_call" | custom-call | flops 1 | bytes 1 | tf_op jit(solution)/shard_map/own/pallas_call | solution.py:74
  39.4 1.0 %collective-permute-done.17.their_two = bf16[128,1152]{1,0:T(8,128)(2,1)S(1)} collective-permute-done((bf16[128,1152]{1,0:T(8,128)(2,1)S(1)}, bf16[128,1152]{1,0:T(8,128)(2,1)S(1)}, u32[]{:S(2)}, u32[]{:S(2)}) %collective-permute-start.17) | collective-permute-done | bytes 294944 | tf_op jit(solution)/shard_map/ppermute | solution.py:35
  40.4 1.5 %last.1 = (f32[128,1152]{1,0:T(8,128)}, f32[128,1152]{1,0:T(8,128)}) custom-call(s32[1]{0:T(128)} %bitcast.core, f32[32,128]{1,0:T(8,128)S(1)} %consts.1.after, f32[128,1152]{1,0:T(8,128)S(1)} %get-tuple-element.30.after.unit_own, f32[128,1]{1,0:T(8,128)S(1)} %get-tuple-element.31.length_own, f32[128,1152]{1,0:T(8,128)S(1)} %get-tuple-element.36.unit_their, ...), custom_call_target="tpu_custom_call" | custom-call | flops 1 | bytes 1 | tf_op jit(solution)/shard_map/last/pallas_call | solution.py:74
  (34 shorter events, 0.9 us)
Async XLA Ops:
  2.0 6.3 %collective-permute-start = (bf16[256,1152]{1,0:T(8,128)(2,1)S(1)}, bf16[256,1152]{1,0:T(8,128)(2,1)S(1)}, u32[]{:S(2)}, u32[]{:S(2)}) collective-permute-start(bf16[256,1152]{1,0:T(8,128)(2,1)S(1)} %get-tuple-element.23), channel_id=1, source_target_pairs={{0,16},{1,17},{2,18},{3,19},{4,20},{5,21},{6,22},{7,23},{8,24},{9,... | collective-permute-start | bytes 1769480 | tf_op jit(solution)/shard_map/ppermute | solution.py:35
  5.3 8.2 %collective-permute-start.1 = (bf16[128,1152]{1,0:T(8,128)(2,1)S(1)}, bf16[128,1152]{1,0:T(8,128)(2,1)S(1)}, u32[]{:S(2)}, u32[]{:S(2)}) collective-permute-start(bf16[128,1152]{1,0:T(8,128)(2,1)S(1)} %get-tuple-element.27.first), channel_id=1, source_target_pairs={{0,1},{1,2},{2,3},{3,0},{4,5},{5,6},{6,7},{7,4},{8,9},{9,10},{10,1... | collective-permute-start | bytes 884744 | tf_op jit(solution)/shard_map/ppermute | solution.py:35
  5.3 8.5 %collective-permute-start.4 = (bf16[128,1152]{1,0:T(8,128)(2,1)S(1)}, bf16[128,1152]{1,0:T(8,128)(2,1)S(1)}, u32[]{:S(2)}, u32[]{:S(2)}) collective-permute-start(bf16[128,1152]{1,0:T(8,128)(2,1)S(1)} %get-tuple-element.28.other), channel_id=1, source_target_pairs={{0,28},{1,29},{2,30},{3,31},{4,16},{5,17},{6,18},{7,19},{8,20},{9,... | collective-permute-start | bytes 884744 | tf_op jit(solution)/shard_map/ppermute | solution.py:35
  8.3 8.0 %collective-permute-start.2 = (bf16[128,1152]{1,0:T(8,128)(2,1)S(1)}, bf16[128,1152]{1,0:T(8,128)(2,1)S(1)}, u32[]{:S(2)}, u32[]{:S(2)}) collective-permute-start(bf16[128,1152]{1,0:T(8,128)(2,1)S(1)} %get-tuple-element.24.after.second), channel_id=1, source_target_pairs={{0,1},{1,2},{2,3},{3,0},{4,5},{5,6},{6,7},{7,4},{8,9},{9,10},{10,1... | collective-permute-start | bytes 884744 | tf_op jit(solution)/shard_map/ppermute | solution.py:35
  8.4 8.5 %collective-permute-start.3 = (bf16[128,1152]{1,0:T(8,128)(2,1)S(1)}, bf16[128,1152]{1,0:T(8,128)(2,1)S(1)}, u32[]{:S(2)}, u32[]{:S(2)}) collective-permute-start(bf16[128,1152]{1,0:T(8,128)(2,1)S(1)} %get-tuple-element.25.after_too.other_second), channel_id=1, source_target_pairs={{0,28},{1,29},{2,30},{3,31},{4,16},{5,17},{6,18},{7,19},{8,20},{9,... | collective-permute-start | bytes 884744 | tf_op jit(solution)/shard_map/ppermute | solution.py:35
  13.5 7.2 %collective-permute-start.7 = (bf16[128,1152]{1,0:T(8,128)(2,1)S(1)}, bf16[128,1152]{1,0:T(8,128)(2,1)S(1)}, u32[]{:S(2)}, u32[]{:S(2)}) collective-permute-start(bf16[128,1152]{1,0:T(8,128)(2,1)S(1)} %gate.4.back_first), channel_id=1, source_target_pairs={{0,1},{1,2},{2,3},{3,0},{4,5},{5,6},{6,7},{7,4},{8,9},{9,10},{10,1... | collective-permute-start | bytes 884744 | tf_op jit(solution)/shard_map/ppermute | solution.py:35
  13.6 3.5 %collective-permute-start.5 = (bf16[128,1152]{1,0:T(8,128)(2,1)S(1)}, bf16[128,1152]{1,0:T(8,128)(2,1)S(1)}, u32[]{:S(2)}, u32[]{:S(2)}) collective-permute-start(bf16[128,1152]{1,0:T(8,128)(2,1)S(1)} %gate.4.back_first), channel_id=1, source_target_pairs={{0,16},{1,17},{2,18},{3,19},{4,20},{5,21},{6,22},{7,23},{8,24},{9,... | collective-permute-start | bytes 884744 | tf_op jit(solution)/shard_map/ppermute | solution.py:35
  13.7 8.0 %collective-permute-start.8 = (bf16[128,1152]{1,0:T(8,128)(2,1)S(1)}, bf16[128,1152]{1,0:T(8,128)(2,1)S(1)}, u32[]{:S(2)}, u32[]{:S(2)}) collective-permute-start(bf16[128,1152]{1,0:T(8,128)(2,1)S(1)} %gate.5.ahead_second), channel_id=1, source_target_pairs={{0,3},{1,0},{2,1},{3,2},{4,7},{5,4},{6,5},{7,6},{8,11},{9,8},{10,9... | collective-permute-start | bytes 884744 | tf_op jit(solution)/shard_map/ppermute | solution.py:35
  16.2 1.9 %collective-permute-start.6 = (bf16[128,1152]{1,0:T(8,128)(2,1)S(1)}, bf16[128,1152]{1,0:T(8,128)(2,1)S(1)}, u32[]{:S(2)}, u32[]{:S(2)}) collective-permute-start(bf16[128,1152]{1,0:T(8,128)(2,1)S(1)} %gate.5.ahead_second), channel_id=1, source_target_pairs={{0,16},{1,17},{2,18},{3,19},{4,20},{5,21},{6,22},{7,23},{8,24},{9,... | collective-permute-start | bytes 884744 | tf_op jit(solution)/shard_map/ppermute | solution.py:35
  16.9 4.9 %collective-permute-start.9 = (bf16[256,1152]{1,0:T(8,128)(2,1)S(1)}, bf16[256,1152]{1,0:T(8,128)(2,1)S(1)}, u32[]{:S(2)}, u32[]{:S(2)}) collective-permute-start(bf16[256,1152]{1,0:T(8,128)(2,1)S(1)} %pad_maximum_fusion), channel_id=1, source_target_pairs={{0,16},{1,17},{2,18},{3,19},{4,20},{5,21},{6,22},{7,23},{8,24},{9,... | collective-permute-start | bytes 1769480 | tf_op jit(solution)/shard_map/ppermute | solution.py:35
  20.6 2.8 %collective-permute-start.10 = (bf16[128,1152]{1,0:T(8,128)(2,1)S(1)}, bf16[128,1152]{1,0:T(8,128)(2,1)S(1)}, u32[]{:S(2)}, u32[]{:S(2)}) collective-permute-start(bf16[128,1152]{1,0:T(8,128)(2,1)S(1)} %gate.6.far_first), channel_id=1, source_target_pairs={{0,16},{1,17},{2,18},{3,19},{4,20},{5,21},{6,22},{7,23},{8,24},{9,... | collective-permute-start | bytes 884744 | tf_op jit(solution)/shard_map/ppermute | solution.py:35
  21.8 1.7 %collective-permute-start.11 = (bf16[128,1152]{1,0:T(8,128)(2,1)S(1)}, bf16[128,1152]{1,0:T(8,128)(2,1)S(1)}, u32[]{:S(2)}, u32[]{:S(2)}) collective-permute-start(bf16[128,1152]{1,0:T(8,128)(2,1)S(1)} %gate.7.far_second), channel_id=1, source_target_pairs={{0,16},{1,17},{2,18},{3,19},{4,20},{5,21},{6,22},{7,23},{8,24},{9,... | collective-permute-start | bytes 884744 | tf_op jit(solution)/shard_map/ppermute | solution.py:35
  24.2 7.3 %collective-permute-start.16 = (bf16[128,1152]{1,0:T(8,128)(2,1)S(1)}, bf16[128,1152]{1,0:T(8,128)(2,1)S(1)}, u32[]{:S(2)}, u32[]{:S(2)}) collective-permute-start(bf16[128,1152]{1,0:T(8,128)(2,1)S(1)} %get-tuple-element.43), channel_id=1, source_target_pairs={{0,1},{1,2},{2,3},{3,0},{4,5},{5,6},{6,7},{7,4},{8,9},{9,10},{10,1... | collective-permute-start | bytes 884744 | tf_op jit(solution)/shard_map/ppermute | solution.py:35
  24.5 7.7 %collective-permute-start.12 = (bf16[128,1152]{1,0:T(8,128)(2,1)S(1)}, bf16[128,1152]{1,0:T(8,128)(2,1)S(1)}, u32[]{:S(2)}, u32[]{:S(2)}) collective-permute-start(bf16[128,1152]{1,0:T(8,128)(2,1)S(1)} %get-tuple-element.33.after), channel_id=1, source_target_pairs={{0,3},{1,0},{2,1},{3,2},{4,7},{5,4},{6,5},{7,6},{8,11},{9,8},{10,9... | collective-permute-start | bytes 884744 | tf_op jit(solution)/shard_map/ppermute | solution.py:35
  28.9 10.5 %collective-permute-start.13 = (bf16[128,1152]{1,0:T(8,128)(2,1)S(1)}, bf16[128,1152]{1,0:T(8,128)(2,1)S(1)}, u32[]{:S(2)}, u32[]{:S(2)}) collective-permute-start(bf16[128,1152]{1,0:T(8,128)(2,1)S(1)} %get-tuple-element.39), channel_id=1, source_target_pairs={{0,1},{1,2},{2,3},{3,0},{4,5},{5,6},{6,7},{7,4},{8,9},{9,10},{10,1... | collective-permute-start | bytes 884744 | tf_op jit(solution)/shard_map/ppermute | solution.py:35
  29.0 10.4 %collective-permute-start.15 = (bf16[128,1152]{1,0:T(8,128)(2,1)S(1)}, bf16[128,1152]{1,0:T(8,128)(2,1)S(1)}, u32[]{:S(2)}, u32[]{:S(2)}) collective-permute-start(bf16[128,1152]{1,0:T(8,128)(2,1)S(1)} %get-tuple-element.41), channel_id=1, source_target_pairs={{0,19},{1,16},{2,17},{3,18},{4,23},{5,20},{6,21},{7,22},{8,27},{9,... | collective-permute-start | bytes 884744 | tf_op jit(solution)/shard_map/ppermute | solution.py:35
  31.7 8.7 %collective-permute-start.17 = (bf16[128,1152]{1,0:T(8,128)(2,1)S(1)}, bf16[128,1152]{1,0:T(8,128)(2,1)S(1)}, u32[]{:S(2)}, u32[]{:S(2)}) collective-permute-start(bf16[128,1152]{1,0:T(8,128)(2,1)S(1)} %relay.3), channel_id=1, source_target_pairs={{0,17},{1,18},{2,19},{3,16},{4,21},{5,22},{6,23},{7,20},{8,25},{9,... | collective-permute-start | bytes 884744 | tf_op jit(solution)/shard_map/ppermute | solution.py:35
  32.2 8.2 %collective-permute-start.14 = (bf16[128,1152]{1,0:T(8,128)(2,1)S(1)}, bf16[128,1152]{1,0:T(8,128)(2,1)S(1)}, u32[]{:S(2)}, u32[]{:S(2)}) collective-permute-start(bf16[128,1152]{1,0:T(8,128)(2,1)S(1)} %relay.2.after), channel_id=1, source_target_pairs={{0,3},{1,0},{2,1},{3,2},{4,7},{5,4},{6,5},{7,6},{8,11},{9,8},{10,9... | collective-permute-start | bytes 884744 | tf_op jit(solution)/shard_map/ppermute | solution.py:35
